TPU v7x, 32 devices: a whole 2x2x4 slice. The times are simulated.
32 devices in a mesh: groups: 2 (over x), owner: 16 (over z, y, core).
Axes of the slice: x: 2, y: 2, z: 4, core: 2. Of those that a mesh axis runs over, the one named last changes fastest.
Arguments:
- embeds: bfloat16 [16384, 768], P(('groups', 'owner')), parts along dimension 0, may hold values from -6 to 6
- clusters: int32 [16384], P(('groups', 'owner')), parts along dimension 0, may hold values from 0 to 17, as said below
- ranks: int32 [16384], P(('groups', 'owner')), parts along dimension 0, may hold values from 0 to 4095
Outputs:
- maxima: float32 [16384], P(('groups', 'owner')), parts along dimension 0
There are 2 independent parts, one for each index of `groups`. A program takes and returns all parts, laid end to end along the dimension named above; each array names one. Nothing has to cross between parts.
Inputs may be any that keep to these rules, and one draw needn't show every extreme that they name: A cluster c below 16 is small and all its rows go to device c of owner; a cluster c of 16 or more is large and its row with rank r goes to device 8 * (c - 16) + r % 8. Of the rows of one device at most 64 go to one device. In every draw one device receives exactly 64 rows from every device, exactly half of them in large clusters.
All inputs are finite; a program needn't handle non-finite values.
Results may differ from a plain program's by a relative error of at most 0.0014.
Values may be sent and summed in bfloat16 or wider, within the bound.
No kernel may reach another device: no remote copies, remote signals or barrier semaphores. Data moves between devices by JAX's collectives and lax.ppermute only.
A program may use at most 64 MiB of HBM per device.

v0:
```python
import jax
import jax.numpy as jnp
from jax import lax
from jax.sharding import PartitionSpec as P


def as_sent(array):
    return jax.tree.map(lambda a: a.astype(jnp.bfloat16) if a.dtype == jnp.float32 else a, array)


def from_partner(block, axis, apart):
    count = lax.axis_size(axis)
    route = []
    for low in range(count):
        high = low | 1 << apart
        if high != low and high < count:
            route += [(low, high), (high, low)]
    return lax.ppermute(block, axis, route)


def best_against(best, mine, other):
    mine_unit, mine_cluster, mine_rank = mine
    other_unit, other_cluster, other_rank = other
    query_total = mine_unit.shape[0]
    key_total = other_unit.shape[0]
    query_size = min(512, query_total)
    key_size = min(512, key_total)

    def query_block(query_index, current_best):
        query_start = query_index * query_size
        query_unit = lax.dynamic_slice_in_dim(mine_unit, query_start, query_size, 0)
        query_cluster = lax.dynamic_slice_in_dim(mine_cluster, query_start, query_size, 0)
        query_rank = lax.dynamic_slice_in_dim(mine_rank, query_start, query_size, 0)
        running = lax.dynamic_slice_in_dim(current_best, query_start, query_size, 0)

        def key_block(key_index, running_best):
            key_start = key_index * key_size
            key_unit = lax.dynamic_slice_in_dim(other_unit, key_start, key_size, 0)
            key_cluster = lax.dynamic_slice_in_dim(other_cluster, key_start, key_size, 0)
            key_rank = lax.dynamic_slice_in_dim(other_rank, key_start, key_size, 0)
            allowed = (key_cluster[None, :] == query_cluster[:, None]) & (key_cluster[None, :] >= 0)
            allowed = allowed & (key_rank[None, :] < query_rank[:, None])
            scores = jnp.einsum(
                "qd,kd->qk", query_unit, key_unit, preferred_element_type=jnp.float32
            )
            return jnp.maximum(
                running_best, jnp.max(jnp.where(allowed, scores, jnp.float32(-1.0)), axis=1)
            )

        running = lax.fori_loop(0, key_total // key_size, key_block, running)
        return lax.dynamic_update_slice_in_dim(current_best, running, query_start, 0)

    return lax.fori_loop(0, query_total // query_size, query_block, best)


def local(embeds, clusters, ranks):
    count = lax.axis_size("owner")
    rows, width = embeds.shape
    slots = max(2, 2 * rows // count)
    total = count * slots
    large_cap = total // 2
    values = embeds.astype(jnp.float32)
    unit = (values * lax.rsqrt(jnp.sum(values * values, axis=1, keepdims=True) + 1e-06)).astype(
        jnp.bfloat16
    )
    is_large = clusters >= count
    target = jnp.where(is_large, 8 * (clusters - count) + ranks % 8, clusters)
    positions = jnp.arange(rows, dtype=jnp.int32)
    later = positions[:, None] > positions[None, :]
    earlier = (target[:, None] == target[None, :]) & later
    place = target * slots + jnp.sum(earlier.astype(jnp.int32), axis=1)
    send_unit = jnp.zeros((total, width), jnp.bfloat16).at[place].set(unit)
    send_cluster = jnp.full((total,), -1, jnp.int32).at[place].set(clusters)
    send_rank = jnp.zeros((total,), jnp.int32).at[place].set(ranks)
    got_unit, got_cluster, got_rank = (
        lax.all_to_all(
            send_unit.reshape(count, slots, width), "owner", split_axis=0, concat_axis=0, tiled=True
        ),
        lax.all_to_all(
            send_cluster.reshape(count, slots), "owner", split_axis=0, concat_axis=0, tiled=True
        ),
        lax.all_to_all(
            send_rank.reshape(count, slots), "owner", split_axis=0, concat_axis=0, tiled=True
        ),
    )
    mine = (got_unit.reshape(total, width), got_cluster.reshape(total), got_rank.reshape(total))
    best = jnp.full((total,), -1.0, jnp.float32)
    best = best_against(best, mine, mine)
    large_slot = mine[1] >= count
    large_position = jnp.cumsum(large_slot.astype(jnp.int32)) - 1
    large_place = jnp.where(large_slot, large_position, large_cap)
    large = (
        jnp.zeros((large_cap, width), jnp.bfloat16).at[large_place].set(mine[0], mode="drop"),
        jnp.full((large_cap,), -1, jnp.int32).at[large_place].set(mine[1], mode="drop"),
        jnp.zeros((large_cap,), jnp.int32).at[large_place].set(mine[2], mode="drop"),
    )
    large_best = jnp.full((large_cap,), -1.0, jnp.float32)
    gathered = large
    for level in range(3):
        partner = jax.tree.map(
            lambda part, own: part.astype(own.dtype),
            from_partner(as_sent(gathered), "owner", level),
            gathered,
        )
        large_best = best_against(large_best, large, partner)
        if level < 2:
            gathered = jax.tree.map(
                lambda left, right: jnp.concatenate([left, right], axis=0), gathered, partner
            )
    picked = large_best[jnp.clip(large_position, 0, large_cap - 1)]
    best = jnp.where(large_slot, jnp.maximum(best, picked), best)
    returned = lax.all_to_all(
        best.reshape(count, slots), "owner", split_axis=0, concat_axis=0, tiled=True
    )
    return returned.reshape(total)[place]


def solution(mesh):
    return jax.shard_map(
        local,
        mesh=mesh,
        in_specs=(P(("groups", "owner"), None), P(("groups", "owner")), P(("groups", "owner"))),
        out_specs=P(("groups", "owner")),
        check_vma=False,
    )
```

profile of v0, /device:TPU:0, one launch (start us, length us, event | category | flops | bytes accessed | tf_op | source)
XLA Modules:
  0.0 224.0 jit_solution(16567223176435365162)
XLA Ops:
  0.0 0.7 compare_select_fusion.3
  0.7 0.3 convert_reduce_fusion
  1.0 2.6 %scatter_custom_fusion = s32[1024]{0:T(1024)S(1)} fusion(s32[512]{0:T(512)S(1)} %compare_select_fusion.2, s32[512]{0:T(512)} %param.12, s32[]{:T(128)} %constant.227.clone.1), kind=kCustom, calls=%fused_computation.66 | custom fusion | bytes 4608 | tf_op jit(solution)/shard_map/scatter | solution.py:73
  3.6 0.7 all_to_all.21
  4.3 7.4 %all-to-all-start = ((s32[16,1,64]{2,1,0:T(1,128)}), s32[16,1,64]{2,1,0:T(1,128)S(1)}, u32[]{:S(2)}, u32[]{:S(2)}) async-start(s32[16,1,64]{2,1,0:T(1,128)} %all_to_all.21), calls=%async_computation | async-start | bytes 16384 | tf_op jit(solution)/shard_map/all_to_all | solution.py:79
  11.6 1.4 fusion.12
  13.0 4.5 %scatter_custom_fusion.2 = bf16[1024,768]{1,0:T(8,128)(2,1)} fusion(s32[512]{0:T(512)S(1)} %compare_select_fusion.2, bf16[512,768]{1,0:T(8,128)(2,1)} %param.11, f32[512]{0:T(512)S(1)} %add_rsqrt_fusion, bf16[]{:T(256)} %constant.236.clone.1), kind=kCustom, calls=%fused_computation.37 | custom fusion | flops 1179648 | bytes 2361346 | tf_op jit(solution)/shard_map/scatter | solution.py:72
  17.5 0.5 all-to-all-done
  18.0 5.5 %all-to-all-start.2 = ((bf16[16,64,768]{2,1,0:T(8,128)(2,1)}), bf16[16,64,768]{2,1,0:T(8,128)(2,1)S(1)}, u32[]{:S(2)}, u32[]{:S(2)}) async-start(bf16[16,64,768]{2,1,0:T(8,128)(2,1)} %bitcast.42), calls=%async_computation.2 | async-start | bytes 3145728 | tf_op jit(solution)/shard_map/all_to_all | solution.py:76
  23.5 0.6 broadcast.206
  24.1 0.7 fusion.21
  24.9 0.3 reduce-window.9
  25.3 0.1 ge.60
  25.4 0.1 slice_reduce_fusion
  25.6 29.9 %all-to-all-done.2 = bf16[16,64,768]{2,1,0:T(8,128)(2,1)S(1)} async-done(((bf16[16,64,768]{2,1,0:T(8,128)(2,1)}), bf16[16,64,768]{2,1,0:T(8,128)(2,1)S(1)}, u32[]{:S(2)}, u32[]{:S(2)}) %all-to-all-start.2) | async-done | bytes 1572896 | tf_op jit(solution)/shard_map/all_to_all | solution.py:76
  55.5 5.3 %scatter_custom_fusion.5 = bf16[512,768]{1,0:T(8,128)(2,1)S(1)} fusion(s32[1024]{0:T(1024)S(1)} %bitcast.45, bf16[1024,768]{1,0:T(8,128)(2,1)S(1)} %bitcast.40, bf16[]{:T(256)} %constant.236.clone.1), kind=kCustom, calls=%fused_computation.40 | custom fusion | bytes 786434 | tf_op jit(solution)/shard_map/scatter | solution.py:93
  60.8 0.8 collective-permute-start.2
  61.7 1.9 collective-permute-done.2
  63.6 1.4 pad_maximum_fusion.1
  64.9 2.7 %collective-permute-start.5 = (bf16[1024,768]{1,0:T(8,128)(2,1)}, bf16[1024,768]{1,0:T(8,128)(2,1)}, u32[]{:S(2)}, u32[]{:S(2)}) collective-permute-start(bf16[1024,768]{1,0:T(8,128)(2,1)} %pad_maximum_fusion.1), channel_id=1, source_target_pairs={{0,2},{2,0},{1,3},{3,1},{4,6},{6,4},{5,7},{7,5},{8,10},{10,8},{9,1... | collective-permute-start | bytes 4718600 | tf_op jit(solution)/shard_map/ppermute | solution.py:18
  67.6 2.6 %scatter_custom_fusion.1 = s32[1024]{0:T(1024)S(1)} fusion(s32[512]{0:T(512)S(1)} %compare_select_fusion.2, s32[512]{0:T(512)} %param.13, s32[]{:T(128)} %constant.231.clone.1), kind=kCustom, calls=%fused_computation.64 | custom fusion | bytes 4608 | tf_op jit(solution)/shard_map/scatter | solution.py:74
  70.2 0.7 all_to_all.23
  70.9 7.0 %all-to-all-start.1 = ((s32[16,1,64]{2,1,0:T(1,128)}), s32[16,1,64]{2,1,0:T(1,128)S(1)}, u32[]{:S(2)}, u32[]{:S(2)}) async-start(s32[16,1,64]{2,1,0:T(1,128)} %all_to_all.23), calls=%async_computation.1 | async-start | bytes 16384 | tf_op jit(solution)/shard_map/all_to_all | solution.py:82
  78.0 24.9 %all-to-all-done.1 = s32[16,1,64]{2,1,0:T(1,128)S(1)} async-done(((s32[16,1,64]{2,1,0:T(1,128)}), s32[16,1,64]{2,1,0:T(1,128)S(1)}, u32[]{:S(2)}, u32[]{:S(2)}) %all-to-all-start.1) | async-done | bytes 4128 | tf_op jit(solution)/shard_map/all_to_all | solution.py:82
  102.9 0.7 reduce.18
  103.7 4.3 %scatter_custom_fusion.4 = s32[512]{0:T(512)S(1)} fusion(s32[1024]{0:T(1024)S(1)} %bitcast.46, s32[1024]{0:T(1024)S(1)} %reshape.207, s32[]{:T(128)} %constant.231.clone.1), kind=kCustom, calls=%fused_computation.71 | custom fusion | bytes 2052 | tf_op jit(solution)/shard_map/scatter | solution.py:95
  108.0 4.5 %scatter_custom_fusion.3 = s32[512]{0:T(512)S(1)} fusion(s32[1024]{0:T(1024)S(1)} %bitcast.47, s32[1024]{0:T(1024)S(1)} %reshape.199, s32[]{:T(128)} %constant.227.clone.1), kind=kCustom, calls=%fused_computation.68 | custom fusion | bytes 2052 | tf_op jit(solution)/shard_map/scatter | solution.py:94
  112.5 0.2 collective-permute-start.1
  112.6 0.4 collective-permute-start
  113.1 0.8 collective-permute-done
  113.9 1.7 collective-permute-start.3
  115.6 0.3 collective-permute-start.4
  116.0 3.3 %pad_maximum_fusion = bf16[2048,768]{1,0:T(8,128)(2,1)} fusion(bf16[1024,768]{1,0:T(8,128)(2,1)} %collective-permute-done.5, bf16[512,768]{1,0:T(8,128)(2,1)S(1)} %collective-permute-done.2, bf16[512,768]{1,0:T(8,128)(2,1)S(1)} %scatter_custom_fusion.5), kind=kLoop, calls=%fused_computation.27 | loop fusion | flops 9437184 | bytes 6291456 | tf_op jit(solution)/shard_map/concatenate | solution.py:108
  119.3 4.3 %collective-permute-start.8 = (bf16[2048,768]{1,0:T(8,128)(2,1)}, bf16[2048,768]{1,0:T(8,128)(2,1)}, u32[]{:S(2)}, u32[]{:S(2)}) collective-permute-start(bf16[2048,768]{1,0:T(8,128)(2,1)} %pad_maximum_fusion), channel_id=1, source_target_pairs={{0,4},{4,0},{1,5},{5,1},{2,6},{6,2},{3,7},{7,3},{8,12},{12,8},{9,1... | collective-permute-start | bytes 9437192 | tf_op jit(solution)/shard_map/ppermute | solution.py:18
  123.6 0.1 collective-permute-start.6
  123.7 2.1 collective-permute-start.7
  125.8 4.5 %while.93 = (s32[]{:T(128)}, f32[1024]{0:T(1024)S(1)}, s32[1024]{0:T(1024)S(1)}, s32[1024]{0:T(1024)S(1)}, bf16[1024,768]{1,0:T(8,128)(2,1)S(1)}, /*index=5*/s32...) while((s32[]{:T(128)}, f32[1024]{0:T(1024)S(1)}, ...), condition=%wide.region_9.10_spmd, body=%wide.region_5.9_spmd.sunk | while | flops 404226560 | bytes 3188198 | solution.py:53
  126.1 1.7 while.96
  126.2 0.7 fusion.54
  127.1 0.7 fusion.54
  127.8 0.2 dynamic_update_slice.14
  128.3 1.7 while.96
  128.5 0.7 fusion.54
  129.4 0.7 fusion.54
  130.1 0.2 dynamic_update_slice.14
  130.3 1.8 select_reduce_fusion
  132.2 4.0 %while.94 = (s32[]{:T(128)}, f32[512]{0:T(512)S(1)}, s32[1024]{0:T(1024)S(1)}, s32[512]{0:T(512)S(1)}, s32[1024]{0:T(1024)S(1)}, /*index=5*/s32[512]{0:T(512)S(1...) while((s32[]{:T(128)}, f32[512]{0:T(512)S(1)}, ...), condition=%wide.region_18.19_spmd, body=%wide.region_16.18_spmd.sunk | while | flops 404226560 | bytes 1598647 | solution.py:50
  132.3 1.8 fusion.48
  134.3 1.8 fusion.48
  136.2 56.0 %collective-permute-done.6 = s32[2048]{0:T(1024)S(1)} collective-permute-done((s32[2048]{0:T(1024)S(1)}, s32[2048]{0:T(1024)S(1)}, u32[]{:S(2)}, u32[]{:S(2)}) %collective-permute-start.6) | collective-permute-done | bytes 8224 | tf_op jit(solution)/shard_map/ppermute | solution.py:18
  192.2 8.0 %while.95 = (s32[]{:T(128)}, f32[512]{0:T(512)S(1)}, s32[2048]{0:T(1024)S(1)}, s32[512]{0:T(512)S(1)}, s32[2048]{0:T(1024)S(1)}, /*index=5*/s32[512]{0:T(512)S(1...) while((s32[]{:T(128)}, f32[512]{0:T(512)S(1)}, ...), condition=%wide.region_21.22_spmd, body=%wide.region_19.21_spmd.sunk | while | flops 404226560 | bytes 1598647 | solution.py:50
  192.4 1.8 fusion.51
  194.2 0.1 dynamic_slice.160
  194.4 1.8 fusion.51
  196.2 0.1 dynamic_slice.160
  196.4 1.8 fusion.51
  198.4 1.8 fusion.51
  200.2 6.9 %gather_fusion = f32[1024]{0:T(1024)S(1)} fusion(f32[512]{0:T(512)S(1)} %get-tuple-element.675, s32[1024]{0:T(1024)S(1)} %broadcast_clamp_fusion), kind=kCustom, calls=%fused_computation | custom fusion | bytes 12288 | tf_op jit(solution)/shard_map/gather | solution.py:110
  207.1 0.7 all_to_all.26
  207.8 5.1 %all-to-all-start.3 = ((f32[16,1,64]{2,1,0:T(1,128)}), f32[16,1,64]{2,1,0:T(1,128)S(1)}, u32[]{:S(2)}, u32[]{:S(2)}) async-start(f32[16,1,64]{2,1,0:T(1,128)} %all_to_all.26), calls=%async_computation.3 | async-start | bytes 16384 | tf_op jit(solution)/shard_map/all_to_all | solution.py:112
  212.9 6.4 %all-to-all-done.3 = f32[16,1,64]{2,1,0:T(1,128)S(1)} async-done(((f32[16,1,64]{2,1,0:T(1,128)}), f32[16,1,64]{2,1,0:T(1,128)S(1)}, u32[]{:S(2)}, u32[]{:S(2)}) %all-to-all-start.3) | async-done | bytes 4128 | tf_op jit(solution)/shard_map/all_to_all | solution.py:112
  219.3 0.5 broadcast.208
  219.8 0.7 reduce.19
  220.6 3.4 %gather_fusion.1 = f32[512]{0:T(512)} fusion(f32[1024]{0:T(1024)S(1)} %reshape.153, s32[1024]{0:T(1024)S(1)} %pad_clamp_fusion), kind=kCustom, calls=%fused_computation.1 | custom fusion | bytes 6144 | tf_op jit(solution)/shard_map/gather | solution.py:115
  (65 shorter events, 2.7 us)
Async XLA Ops:
  4.3 13.8 %all-to-all-start = ((s32[16,1,64]{2,1,0:T(1,128)}), s32[16,1,64]{2,1,0:T(1,128)S(1)}, u32[]{:S(2)}, u32[]{:S(2)}) async-start(s32[16,1,64]{2,1,0:T(1,128)} %all_to_all.21), calls=%async_computation | async-start | bytes 16384 | tf_op jit(solution)/shard_map/all_to_all | solution.py:79
  18.0 37.5 %all-to-all-start.2 = ((bf16[16,64,768]{2,1,0:T(8,128)(2,1)}), bf16[16,64,768]{2,1,0:T(8,128)(2,1)S(1)}, u32[]{:S(2)}, u32[]{:S(2)}) async-start(bf16[16,64,768]{2,1,0:T(8,128)(2,1)} %bitcast.42), calls=%async_computation.2 | async-start | bytes 3145728 | tf_op jit(solution)/shard_map/all_to_all | solution.py:76
  60.8 2.7 %collective-permute-start.2 = (bf16[512,768]{1,0:T(8,128)(2,1)S(1)}, bf16[512,768]{1,0:T(8,128)(2,1)S(1)}, u32[]{:S(2)}, u32[]{:S(2)}) collective-permute-start(bf16[512,768]{1,0:T(8,128)(2,1)S(1)} %scatter_custom_fusion.5), channel_id=1, source_target_pairs={{0,1},{1,0},{2,3},{3,2},{4,5},{5,4},{6,7},{7,6},{8,9},{9,8},{10,11... | collective-permute-start | bytes 2359304 | tf_op jit(solution)/shard_map/ppermute | solution.py:18
  63.6 52.4 %copy-start = (bf16[512,768]{1,0:T(8,128)(2,1)}, bf16[512,768]{1,0:T(8,128)(2,1)S(1)}, u32[]{:S(2)}) copy-start(bf16[512,768]{1,0:T(8,128)(2,1)S(1)} %collective-permute-done.2) | copy-start | bytes 2359300
  64.9 51.0 %collective-permute-start.5 = (bf16[1024,768]{1,0:T(8,128)(2,1)}, bf16[1024,768]{1,0:T(8,128)(2,1)}, u32[]{:S(2)}, u32[]{:S(2)}) collective-permute-start(bf16[1024,768]{1,0:T(8,128)(2,1)} %pad_maximum_fusion.1), channel_id=1, source_target_pairs={{0,2},{2,0},{1,3},{3,1},{4,6},{6,4},{5,7},{7,5},{8,10},{10,8},{9,1... | collective-permute-start | bytes 4718600 | tf_op jit(solution)/shard_map/ppermute | solution.py:18
  70.9 32.0 %all-to-all-start.1 = ((s32[16,1,64]{2,1,0:T(1,128)}), s32[16,1,64]{2,1,0:T(1,128)S(1)}, u32[]{:S(2)}, u32[]{:S(2)}) async-start(s32[16,1,64]{2,1,0:T(1,128)} %all_to_all.23), calls=%async_computation.1 | async-start | bytes 16384 | tf_op jit(solution)/shard_map/all_to_all | solution.py:82
  112.5 3.2 %collective-permute-start.1 = (s32[512]{0:T(512)S(1)}, s32[512]{0:T(512)S(1)}, u32[]{:S(2)}, u32[]{:S(2)}) collective-permute-start(s32[512]{0:T(512)S(1)} %scatter_custom_fusion.4), channel_id=1, source_target_pairs={{0,1},{1,0},{2,3},{3,2},{4,5},{5,4},{6,7},{7,6},{8,9},{9,8},{10,11... | collective-permute-start | bytes 6152 | tf_op jit(solution)/shard_map/ppermute | solution.py:18
  112.6 1.2 collective-permute-start
  113.9 9.7 %collective-permute-start.3 = (s32[1024]{0:T(1024)S(1)}, s32[1024]{0:T(1024)S(1)}, u32[]{:S(2)}, u32[]{:S(2)}) collective-permute-start(s32[1024]{0:T(1024)S(1)} %pad_add_fusion.2), channel_id=1, source_target_pairs={{0,2},{2,0},{1,3},{3,1},{4,6},{6,4},{5,7},{7,5},{8,10},{10,8},{9,1... | collective-permute-start | bytes 12296 | tf_op jit(solution)/shard_map/ppermute | solution.py:18
  115.6 8.1 %collective-permute-start.4 = (s32[1024]{0:T(1024)S(1)}, s32[1024]{0:T(1024)S(1)}, u32[]{:S(2)}, u32[]{:S(2)}) collective-permute-start(s32[1024]{0:T(1024)S(1)} %pad_add_fusion.3), channel_id=1, source_target_pairs={{0,2},{2,0},{1,3},{3,1},{4,6},{6,4},{5,7},{7,5},{8,10},{10,8},{9,1... | collective-permute-start | bytes 12296 | tf_op jit(solution)/shard_map/ppermute | solution.py:18
  119.3 72.9 %collective-permute-start.8 = (bf16[2048,768]{1,0:T(8,128)(2,1)}, bf16[2048,768]{1,0:T(8,128)(2,1)}, u32[]{:S(2)}, u32[]{:S(2)}) collective-permute-start(bf16[2048,768]{1,0:T(8,128)(2,1)} %pad_maximum_fusion), channel_id=1, source_target_pairs={{0,4},{4,0},{1,5},{5,1},{2,6},{6,2},{3,7},{7,3},{8,12},{12,8},{9,1... | collective-permute-start | bytes 9437192 | tf_op jit(solution)/shard_map/ppermute | solution.py:18
  123.6 68.5 %collective-permute-start.6 = (s32[2048]{0:T(1024)S(1)}, s32[2048]{0:T(1024)S(1)}, u32[]{:S(2)}, u32[]{:S(2)}) collective-permute-start(s32[2048]{0:T(1024)S(1)} %pad_add_fusion), channel_id=1, source_target_pairs={{0,4},{4,0},{1,5},{5,1},{2,6},{6,2},{3,7},{7,3},{8,12},{12,8},{9,1... | collective-permute-start | bytes 24584 | tf_op jit(solution)/shard_map/ppermute | solution.py:18
  123.7 68.5 %collective-permute-start.7 = (s32[2048]{0:T(1024)S(1)}, s32[2048]{0:T(1024)S(1)}, u32[]{:S(2)}, u32[]{:S(2)}) collective-permute-start(s32[2048]{0:T(1024)S(1)} %pad_add_fusion.1), channel_id=1, source_target_pairs={{0,4},{4,0},{1,5},{5,1},{2,6},{6,2},{3,7},{7,3},{8,12},{12,8},{9,1... | collective-permute-start | bytes 24584 | tf_op jit(solution)/shard_map/ppermute | solution.py:18
  207.8 11.5 %all-to-all-start.3 = ((f32[16,1,64]{2,1,0:T(1,128)}), f32[16,1,64]{2,1,0:T(1,128)S(1)}, u32[]{:S(2)}, u32[]{:S(2)}) async-start(f32[16,1,64]{2,1,0:T(1,128)} %all_to_all.26), calls=%async_computation.3 | async-start | bytes 16384 | tf_op jit(solution)/shard_map/all_to_all | solution.py:112
where the time goes:
time: 225 us; the launch traced here: 224 us
  waiting for transfers between devices  121 us (54%)
  starting transfers between devices  37.7 us (17%)
  local copies, waits for them, and re-layouts  35.1 us (16%)
  matrix products  15.4 us (7%)
  other arithmetic  14.9 us (7%)
    ppermute x9, waiting for transfers between devices, from_partner(): return lax.ppermute(block, axis, route)  58.8 us
    all_to_all x1, waiting for transfers between devices, local(): lax.all_to_all(send_unit.reshape(count, slots, width), 'owner', split_axi...  29.9 us
    all_to_all x1, waiting for transfers between devices, local(): lax.all_to_all(send_rank.reshape(count, slots), 'owner', split_axis=0, co...  24.9 us
    dot_general x11, matrix products, key_block(): jnp.einsum('qd,kd->qk', query_unit, key_unit, preferred_element_type=jnp....  15.4 us
    ppermute x9, starting transfers between devices, from_partner(): return lax.ppermute(block, axis, route)  12.6 us
    all_to_all x1, starting transfers between devices, local(): lax.all_to_all(send_cluster.reshape(count, slots), 'owner', split_axis=0,...  7.39 us
    all_to_all x1, starting transfers between devices, local(): lax.all_to_all(send_rank.reshape(count, slots), 'owner', split_axis=0, co...  7.02 us
    gather x1, local copies, waits for them, and re-layouts, local(): picked = large_best[jnp.clip(large_position, 0, large_cap - 1)]  6.87 us
  transfers between devices with their start and end apart: 13, of which 8 were waited for; matrix products, arithmetic and copies ran while one was open for 15% of the time, Pallas kernels for 0%

commit v1 on v0

--- a/solution.py
+++ b/solution.py
@@ -1,7 +1,219 @@
+import functools
+
 import jax
 import jax.numpy as jnp
 from jax import lax
+from jax.experimental import pallas as pl
+from jax.experimental.pallas import tpu as pltpu
 from jax.sharding import PartitionSpec as P
+
+OWNERS = 16
+CHIPS = 8
+HOMES = (2, 3, 4, 5)
+BLOCK = 160
+CAP = 156
+META = 16
+VMEM_LIMIT = 48 * 1024 * 1024
+NT = (((1,), (1,)), ((), ()))
+
+
+def is_home(chip):
+    return (chip >= HOMES[0]) & (chip <= HOMES[-1])
+
+
+def pack_kernel(x_ref, cluster_ref, rank_ref, *outs):
+    slot_ref = outs[CHIPS]
+    chip = lax.axis_index("owner") // 2
+    values = x_ref[...].astype(jnp.float32)
+    unit = (values * lax.rsqrt(jnp.sum(values * values, axis=1, keepdims=True) + 1e-06)).astype(
+        jnp.bfloat16
+    )
+    rows, width = unit.shape
+    cluster = cluster_ref[...]
+    rank = rank_ref[...]
+    home = jnp.where(
+        cluster < OWNERS // 2,
+        3,
+        jnp.where(cluster < OWNERS, 4, jnp.where(cluster == OWNERS, 2, 5)),
+    )
+    number = lax.broadcasted_iota(jnp.int32, (CHIPS, rows), 0)
+    member = number == (home ^ chip)
+    upper = (
+        lax.broadcasted_iota(jnp.int32, (rows, rows), 0)
+        < lax.broadcasted_iota(jnp.int32, (rows, rows), 1)
+    ).astype(jnp.float32).astype(jnp.bfloat16)
+    before = jnp.dot(
+        member.astype(jnp.float32).astype(jnp.bfloat16), upper, preferred_element_type=jnp.float32
+    )
+    slot = jnp.where(member, before.astype(jnp.int32), -1)
+    slot_ref[...] = slot
+    over = (jnp.max(slot) >= CAP).astype(jnp.float32)
+    line = lax.broadcasted_iota(jnp.int32, (META, rows), 0)
+    first = META - (BLOCK - CAP)
+    meta = jnp.where(
+        line == first,
+        cluster + 1,
+        jnp.where(line == first + 1, rank >> 6, jnp.where(line == first + 2, rank & 63, 0)),
+    )
+    meta = meta.astype(jnp.float32).astype(jnp.bfloat16)
+    for k in range(CHIPS):
+
+        @pl.when(is_home(chip ^ k))
+        def _():
+            place = lax.broadcasted_iota(jnp.int32, (256, rows), 0)
+            hot = ((place == slot[k : k + 1]) & (place < CAP)).astype(jnp.float32)
+            hot = hot.astype(jnp.bfloat16)
+            block = jnp.dot(hot[:BLOCK], unit, preferred_element_type=jnp.float32)
+            outs[k][...] = block.astype(jnp.bfloat16)
+            tail = lax.dot_general(meta, hot, NT, preferred_element_type=jnp.float32)
+            row = lax.broadcasted_iota(jnp.int32, (META, 256), 0)
+            tail = jnp.where(row == META - 1, over, tail)
+            tail = jnp.where(row >= first, tail, block[BLOCK - META :, :256])
+            outs[k][BLOCK - META :, :256] = tail.astype(jnp.bfloat16)
+
+
+def compare_kernel(*refs):
+    blocks = refs[: 2 * CHIPS]
+    out_ref, keys, codes, sems = refs[2 * CHIPS :]
+    me = lax.axis_index("owner")
+    chip = me // 2
+    core = me % 2
+
+    @pl.when(is_home(chip))
+    def _():
+        copies = [
+            pltpu.make_async_copy(ref, keys.at[pl.ds(n * BLOCK, BLOCK)], sems.at[n])
+            for n, ref in enumerate(blocks)
+        ]
+        for copy in copies:
+            copy.start()
+        for copy in copies:
+            copy.wait()
+        eye = (
+            lax.broadcasted_iota(jnp.int32, (BLOCK, 256), 0)
+            == lax.broadcasted_iota(jnp.int32, (BLOCK, 256), 1)
+        ).astype(jnp.float32).astype(jnp.bfloat16)
+        lane = lax.broadcasted_iota(jnp.int32, (1, META), 1)
+        first = META - (BLOCK - CAP)
+        scale = jnp.where(
+            lane == first, 4096.0, jnp.where(lane == first + 1, 64.0, jnp.where(lane == first + 2, 1.0, 0.0))
+        )
+        over = jnp.zeros((1, 128), jnp.float32)
+        for n in range(2 * CHIPS):
+            meta = keys[(n + 1) * BLOCK - META : (n + 1) * BLOCK, :256]
+            over = jnp.maximum(over, meta[META - 1 :, :128].astype(jnp.float32))
+            columns = lax.dot_general(eye, meta, NT, preferred_element_type=jnp.float32)
+            code = jnp.sum(columns * scale, axis=1, keepdims=True)
+            codes[n * BLOCK : (n + 1) * BLOCK] = jnp.broadcast_to(code, (BLOCK, 128))
+        over = jnp.max(over)
+        queries = CHIPS * BLOCK
+        step = 2 * queries // 4
+        found = []
+        for t in range(queries // 256):
+            query = keys[t * 256 : (t + 1) * 256]
+            top = jnp.transpose(codes[t * 256 : (t + 1) * 256])[:1]
+            base = jnp.floor(top * (1.0 / 4096.0)) * 4096.0
+            best = jnp.full((8, 256), -1.0, jnp.float32)
+            for j in range(4):
+                score = lax.dot_general(
+                    keys[j * step : (j + 1) * step], query, NT, preferred_element_type=jnp.float32
+                )
+                code = codes[j * step : (j + 1) * step]
+                code = jnp.concatenate([code, code], axis=1)
+                score = jnp.where((code >= base) & (code < top), score, -1.0)
+                best = jnp.maximum(best, jnp.max(score.reshape(step // 8, 8, 256), axis=0))
+            found.append(jnp.max(best, axis=0, keepdims=True))
+        found = jnp.concatenate(found, axis=1)
+        place = lax.broadcasted_iota(jnp.int32, (1, queries), 1) % BLOCK
+        found = jnp.where(place >= CAP, over, found)
+        found = jnp.broadcast_to(found, (8, queries))
+        for k in range(CHIPS):
+            line = found if k == 0 else pltpu.roll(found, queries - k * BLOCK, 1)
+            row = 8 * (2 * (chip ^ k) + core)
+            out_ref[pl.ds(row, 1), :] = line[:1, :128]
+            out_ref[pl.ds(row + 1, 1), :] = line[:1, 128:256]
+
+
+def unpack_kernel(back_ref, slot_ref, best_ref, over_ref):
+    me = lax.axis_index("owner")
+    chip = me // 2
+    core = me % 2
+    rows = slot_ref.shape[1]
+    best_ref[...] = jnp.zeros_like(best_ref)
+    place = lax.broadcasted_iota(jnp.int32, (128, rows), 0)
+    row = lax.broadcasted_iota(jnp.int32, (8, 128), 0)
+    over_ref[0, 0] = 0
+    for k in range(CHIPS):
+        home = chip ^ k
+
+        @pl.when(is_home(home))
+        def _():
+            slot = slot_ref[k : k + 1]
+            part = back_ref[pl.ds(pl.multiple_of(8 * (2 * home + core), 8), 8), :]
+            total = jnp.zeros((8, rows), jnp.float32)
+            for n in range(2):
+                value = part[n : n + 1]
+                high = value.astype(jnp.bfloat16).astype(jnp.float32)
+                middle = (value - high).astype(jnp.bfloat16).astype(jnp.float32)
+                low = value - high - middle
+                split = jnp.where(row == 0, high, jnp.where(row == 1, middle, jnp.where(row == 2, low, 0.0)))
+                hot = (place + 128 * n == slot).astype(jnp.float32).astype(jnp.bfloat16)
+                total = total + jnp.dot(
+                    split.astype(jnp.bfloat16), hot, preferred_element_type=jnp.float32
+                )
+            best_ref[...] += jnp.sum(total, axis=0, keepdims=True)
+            over_ref[0, 0] = over_ref[0, 0] | (part[1, BLOCK - 1 - 128] > 0.0).astype(jnp.int32)
+
+
+def meet(embeds, clusters, ranks):
+    rows, width = embeds.shape
+    vmem = pl.BlockSpec(memory_space=pltpu.VMEM)
+    params = pltpu.CompilerParams(vmem_limit_bytes=VMEM_LIMIT)
+    packed = pl.pallas_call(
+        pack_kernel,
+        out_shape=[jax.ShapeDtypeStruct((BLOCK, width), jnp.bfloat16)] * CHIPS
+        + [jax.ShapeDtypeStruct((CHIPS, rows), jnp.int32)],
+        in_specs=[vmem] * 3,
+        out_specs=[vmem] * (CHIPS + 1),
+        compiler_params=params,
+        name="pack",
+    )(embeds, clusters.reshape(1, rows), ranks.reshape(1, rows))
+    blocks, slot = list(packed[:CHIPS]), packed[CHIPS]
+    for k in (4, 5, 6, 7, 3, 2, 1):
+        route = [
+            (2 * s + c, 2 * (s ^ k) + c) for s in range(CHIPS) if s ^ k in HOMES for c in range(2)
+        ]
+        blocks[k] = lax.ppermute(blocks[k], "owner", route)
+    swap = [(2 * h + c, 2 * h + 1 - c) for h in HOMES for c in range(2)]
+    other = [lax.ppermute(block, "owner", swap) for block in blocks]
+    found = pl.pallas_call(
+        compare_kernel,
+        out_shape=jax.ShapeDtypeStruct((8 * OWNERS, 128), jnp.float32),
+        in_specs=[pl.BlockSpec(memory_space=pl.ANY)] * (2 * CHIPS),
+        out_specs=vmem,
+        scratch_shapes=[
+            pltpu.VMEM((2 * CHIPS * BLOCK, width), jnp.bfloat16),
+            pltpu.VMEM((2 * CHIPS * BLOCK, 128), jnp.float32),
+            pltpu.SemaphoreType.DMA((2 * CHIPS,)),
+        ],
+        compiler_params=params,
+        name="compare",
+    )(*blocks, *other)
+    back = lax.all_to_all(
+        found.reshape(OWNERS, 8, 128), "owner", split_axis=0, concat_axis=0, tiled=True
+    )
+    best, over = pl.pallas_call(
+        unpack_kernel,
+        out_shape=[
+            jax.ShapeDtypeStruct((1, rows), jnp.float32),
+            jax.ShapeDtypeStruct((1, 1), jnp.int32),
+        ],
+        in_specs=[vmem] * 2,
+        out_specs=[vmem, pl.BlockSpec(memory_space=pltpu.SMEM)],
+        compiler_params=params,
+        name="unpack",
+    )(back.reshape(8 * OWNERS, 128), slot)
+    return best.reshape(rows), over[0, 0] > 0
 
 
 def as_sent(array):
@@ -53,12 +265,12 @@
     return lax.fori_loop(0, query_total // query_size, query_block, best)
 
 
-def local(embeds, clusters, ranks):
+def route_rows(embeds, clusters, ranks):
     count = lax.axis_size("owner")
     rows, width = embeds.shape
     slots = max(2, 2 * rows // count)
     total = count * slots
-    large_cap = total // 2
+    large_cap = total
     values = embeds.astype(jnp.float32)
     unit = (values * lax.rsqrt(jnp.sum(values * values, axis=1, keepdims=True) + 1e-06)).astype(
         jnp.bfloat16
@@ -115,6 +327,14 @@
     return returned.reshape(total)[place]
 
 
+def local(embeds, clusters, ranks):
+    if lax.axis_size("owner") != OWNERS:
+        return route_rows(embeds, clusters, ranks)
+    best, over = meet(embeds, clusters, ranks)
+    return lax.cond(over, lambda *args: route_rows(*args[:3]), lambda *args: args[3],
+                    embeds, clusters, ranks, best)
+
+
 def solution(mesh):
     return jax.shard_map(
         local,

time: 225 us -> 75.3 us (0.33)
  waiting for transfers between devices: 121 us -> 19.9 us
  local copies, waits for them, and re-layouts: 35.1 us -> 0.58 us
  matrix products: 15.4 us -> 0 us
  other arithmetic: 14.9 us -> 0 us
  starting transfers between devices: 37.7 us -> 48.3 us
  Pallas kernels: 0 us -> 4.82 us
    all_to_all x4 -> x1, waiting for transfers between devices: 61.8 us -> 6.9 us  [meet(): lax.all_to_all(found.reshape(OWNERS, 8, 128), 'owner', split_axis=0, conc...]
    ppermute x9 -> x15, waiting for transfers between devices: 58.8 us -> 13 us  [the longest x7 13 us: meet(): blocks[k] = lax.ppermute(blocks[k], 'owner', route)]
    scatter x5 -> x0, local copies, waits for them, and re-layouts: 19.3 us -> none  [the longest x1 5.31 us: local(): jnp.zeros((large_cap, width), jnp.bfloat16).at[large_place]]
    dot_general x11 -> x0, matrix products: 15.4 us -> none  [key_block(): jnp.einsum('qd,kd->qk', query_unit, key_unit, preferred_element_type=jnp....]
    gather x2 -> x0, local copies, waits for them, and re-layouts: 10.3 us -> none  [the longest x1 6.87 us: local(): picked = large_best[jnp.clip(large_position, 0, large_cap - 1)]]
    ppermute x9 -> x15, starting transfers between devices: 12.6 us -> 20.1 us  [the longest x7 14.6 us: meet(): blocks[k] = lax.ppermute(blocks[k], 'owner', route)]
    pallas_call x0 -> x3, Pallas kernels: none -> 4.82 us  [the longest x1 2.86 us: meet(): pl.pallas_call(pack_kernel, out_shape=[jax.ShapeDtypeStruct((BLOCK, width...]
    concatenate x6 -> x0, other arithmetic: 4.69 us -> none  [local(): jnp.concatenate([left, right], axis=0)]
  transfers between devices with their start and end apart: 13 -> 16, of which waited for: 8 -> 5; matrix products, arithmetic and copies ran while one was open for 15% -> 0% of each run, Pallas kernels for 0% -> 0%
where the time goes in v1:
time: 75.3 us; the launch traced here: 74.8 us
  starting transfers between devices  48.3 us (64%)
  waiting for transfers between devices  19.9 us (26%)
  Pallas kernels  4.82 us (6%)
  between operations  0.93 us (1%)
    all_to_all x1, starting transfers between devices, meet(): lax.all_to_all(found.reshape(OWNERS, 8, 128), 'owner', split_axis=0, conc...  28.2 us
    ppermute x7, starting transfers between devices, meet(): blocks[k] = lax.ppermute(blocks[k], 'owner', route)  14.6 us
    ppermute x7, waiting for transfers between devices, meet(): blocks[k] = lax.ppermute(blocks[k], 'owner', route)  13 us
    all_to_all x1, waiting for transfers between devices, meet(): lax.all_to_all(found.reshape(OWNERS, 8, 128), 'owner', split_axis=0, conc...  6.9 us
    ppermute x8, starting transfers between devices, meet(): other = [lax.ppermute(block, 'owner', swap) for block in blocks]  5.51 us
    pallas_call x1, Pallas kernels, meet(): pl.pallas_call(pack_kernel, out_shape=[jax.ShapeDtypeStruct((BLOCK, width...  2.86 us
  transfers between devices with their start and end apart: 16, of which 5 were waited for; matrix products, arithmetic and copies ran while one was open for 0% of the time, Pallas kernels for 0%

profile of v1, /device:TPU:0, one launch (start us, length us, event | category | flops | bytes accessed | tf_op | source)
XLA Modules:
  0.0 74.8 jit_solution(16479555858622213514)
XLA Ops:
  0.0 2.9 %pack.1 = (bf16[160,768]{1,0:T(8,128)(2,1)S(1)}, bf16[160,768]{1,0:T(8,128)(2,1)S(1)}, bf16[160,768]{1,0:T(8,128)(2,1)S(1)}, bf16[160,768]{1,0:T(8,128)(2,1)S(1)...) custom-call(bf16[512,768]{1,0:T(8,128)(2,1)} %x_ref.1, ...), custom_call_target="tpu_custom_call" | custom-call | tf_op jit(solution)/shard_map/pack/pallas_call | solution.py:172
  2.9 0.7 collective-permute-start.9
  3.6 7.7 %collective-permute-start.10 = (bf16[160,768]{1,0:T(8,128)(2,1)S(1)}, bf16[160,768]{1,0:T(8,128)(2,1)S(1)}, u32[]{:S(2)}, u32[]{:S(2)}) collective-permute-start(bf16[160,768]{1,0:T(8,128)(2,1)S(1)} %get-tuple-element.1180), channel_id=1, source_target_pairs={{0,4},{1,5},{2,6},{3,7},{12,8},{13,9},{14,10},{15,11},{16,20},{17,... | collective-permute-start | bytes 737288 | tf_op jit(solution)/shard_map/ppermute | solution.py:186
  11.2 1.3 %collective-permute-start.11 = (bf16[160,768]{1,0:T(8,128)(2,1)S(1)}, bf16[160,768]{1,0:T(8,128)(2,1)S(1)}, u32[]{:S(2)}, u32[]{:S(2)}) collective-permute-start(bf16[160,768]{1,0:T(8,128)(2,1)S(1)} %get-tuple-element.1181), channel_id=1, source_target_pairs={{0,6},{1,7},{2,4},{3,5},{12,10},{13,11},{14,8},{15,9},{16,22},{17,... | collective-permute-start | bytes 737288 | tf_op jit(solution)/shard_map/ppermute | solution.py:186
  12.6 2.3 %collective-permute-start.12 = (bf16[160,768]{1,0:T(8,128)(2,1)S(1)}, bf16[160,768]{1,0:T(8,128)(2,1)S(1)}, u32[]{:S(2)}, u32[]{:S(2)}) collective-permute-start(bf16[160,768]{1,0:T(8,128)(2,1)S(1)} %get-tuple-element.1182), channel_id=1, source_target_pairs={{0,8},{1,9},{2,10},{3,11},{12,4},{13,5},{14,6},{15,7},{16,24},{17,... | collective-permute-start | bytes 737288 | tf_op jit(solution)/shard_map/ppermute | solution.py:186
  14.9 1.3 %collective-permute-start.13 = (bf16[160,768]{1,0:T(8,128)(2,1)S(1)}, bf16[160,768]{1,0:T(8,128)(2,1)S(1)}, u32[]{:S(2)}, u32[]{:S(2)}) collective-permute-start(bf16[160,768]{1,0:T(8,128)(2,1)S(1)} %get-tuple-element.1183), channel_id=1, source_target_pairs={{0,10},{1,11},{2,8},{3,9},{12,6},{13,7},{14,4},{15,5},{16,26},{17,... | collective-permute-start | bytes 737288 | tf_op jit(solution)/shard_map/ppermute | solution.py:186
  16.2 0.0 collective-permute-done.9.refs_1_
  16.2 0.7 collective-permute-start.14
  16.9 0.7 collective-permute-done.10.refs_2_
  17.6 0.7 collective-permute-start.15
  18.3 4.6 %collective-permute-done.11.refs_3_ = bf16[160,768]{1,0:T(8,128)(2,1)S(1)} collective-permute-done((bf16[160,768]{1,0:T(8,128)(2,1)S(1)}, bf16[160,768]{1,0:T(8,128)(2,1)S(1)}, u32[]{:S(2)}, u32[]{:S(2)}) %collective-permute-start.11) | collective-permute-done | bytes 245792 | tf_op jit(solution)/shard_map/ppermute | solution.py:186
  22.9 0.0 copy-start
  22.9 0.0 copy-start.2
  22.9 0.0 copy-start.3
  22.9 0.8 %collective-permute-start.16 = (bf16[160,768]{1,0:T(8,128)(2,1)S(1)}, bf16[160,768]{1,0:T(8,128)(2,1)S(1)}, u32[]{:S(2)}, u32[]{:S(2)}) collective-permute-start(bf16[160,768]{1,0:T(8,128)(2,1)S(1)} %get-tuple-element.1178.refs_0_), channel_id=1, source_target_pairs={{4,5},{5,4},{6,7},{7,6},{8,9},{9,8},{10,11},{11,10},{20,21},{21,20... | collective-permute-start | bytes 737288 | tf_op jit(solution)/shard_map/ppermute | solution.py:188
  23.7 4.5 %collective-permute-done.12.refs_4_ = bf16[160,768]{1,0:T(8,128)(2,1)S(1)} collective-permute-done((bf16[160,768]{1,0:T(8,128)(2,1)S(1)}, bf16[160,768]{1,0:T(8,128)(2,1)S(1)}, u32[]{:S(2)}, u32[]{:S(2)}) %collective-permute-start.12) | collective-permute-done | bytes 245792 | tf_op jit(solution)/shard_map/ppermute | solution.py:186
  28.2 0.7 collective-permute-start.17
  28.9 3.1 %collective-permute-done.13.refs_5_ = bf16[160,768]{1,0:T(8,128)(2,1)S(1)} collective-permute-done((bf16[160,768]{1,0:T(8,128)(2,1)S(1)}, bf16[160,768]{1,0:T(8,128)(2,1)S(1)}, u32[]{:S(2)}, u32[]{:S(2)}) %collective-permute-start.13) | collective-permute-done | bytes 245792 | tf_op jit(solution)/shard_map/ppermute | solution.py:186
  32.0 0.7 collective-permute-start.18
  32.7 0.0 collective-permute-done.14.refs_6_
  32.7 0.7 collective-permute-start.19
  33.4 0.0 collective-permute-done.15.refs_7_
  33.4 0.7 collective-permute-start.20
  34.1 0.0 collective-permute-done.16.refs_8_
  34.1 0.7 collective-permute-start.21
  34.8 0.0 collective-permute-done.17.refs_9_
  34.8 0.7 collective-permute-start.22
  35.4 0.0 collective-permute-done.18.refs_10_
  35.5 0.7 collective-permute-start.23
  36.1 0.0 collective-permute-done.19.refs_11_
  36.2 0.0 collective-permute-done.20.refs_12_
  36.2 0.0 collective-permute-done.21.refs_13_
  36.2 0.0 collective-permute-done.22.refs_14_
  36.2 0.0 collective-permute-done.23.refs_15_
  36.2 0.8 %compare.2 = f32[128,128]{1,0:T(8,128)} custom-call(bf16[160,768]{1,0:T(8,128)(2,1)S(1)} %get-tuple-element.1178.refs_0_, bf16[160,768]{1,0:T(8,128)(2,1)S(1)} %collective-permute-done.9.refs_1_, bf16[160,768]{1,0:T(8,128)(2,1)S(1)} %collective-permute-done.10.refs_2_, bf16[160,768]{1,0:T(8,128)(2,1)S(1)} %collective-permute-done.11.refs_3_, ...), custom_call_target="tpu_custom_call" | custom-call | tf_op jit(solution)/shard_map/compare/pallas_call | solution.py:189
  37.0 28.2 %all-to-all-start.4 = ((f32[16,8,128]{2,1,0:T(8,128)}), f32[16,8,128]{2,1,0:T(8,128)S(1)}, u32[]{:S(2)}, u32[]{:S(2)}) async-start(f32[16,8,128]{2,1,0:T(8,128)} %bitcast.12), calls=%async_computation.4 | async-start | bytes 131072 | tf_op jit(solution)/shard_map/all_to_all | solution.py:202
  65.2 6.9 %all-to-all-done.4 = f32[16,8,128]{2,1,0:T(8,128)S(1)} async-done(((f32[16,8,128]{2,1,0:T(8,128)}), f32[16,8,128]{2,1,0:T(8,128)S(1)}, u32[]{:S(2)}, u32[]{:S(2)}) %all-to-all-start.4) | async-done | bytes 65568 | tf_op jit(solution)/shard_map/all_to_all | solution.py:202
  72.1 1.2 %unpack.1 = (f32[1,512]{1,0:T(1,128)S(1)}, s32[1,1]{1,0:T(1,128)}) custom-call(f32[128,128]{1,0:T(8,128)S(1)} %bitcast.55, s32[8,512]{1,0:T(8,128)S(1)} %get-tuple-element.1186.slot_ref), custom_call_target="tpu_custom_call" | custom-call | tf_op jit(solution)/shard_map/unpack/pallas_call | solution.py:205
  74.0 0.0 copy-done
  74.0 0.0 copy-done.2
  74.0 0.0 copy-done.3
  74.0 0.2 conditional.1
  74.2 0.0 copy-start.4
  74.2 0.6 copy-done.4
Async XLA Ops:
  2.9 13.3 %collective-permute-start.9 = (bf16[160,768]{1,0:T(8,128)(2,1)S(1)}, bf16[160,768]{1,0:T(8,128)(2,1)S(1)}, u32[]{:S(2)}, u32[]{:S(2)}) collective-permute-start(bf16[160,768]{1,0:T(8,128)(2,1)S(1)} %get-tuple-element.1179), channel_id=1, source_target_pairs={{4,6},{5,7},{6,4},{7,5},{8,10},{9,11},{10,8},{11,9},{20,22},{21,23... | collective-permute-start | bytes 737288 | tf_op jit(solution)/shard_map/ppermute | solution.py:186
  3.6 14.1 %collective-permute-start.10 = (bf16[160,768]{1,0:T(8,128)(2,1)S(1)}, bf16[160,768]{1,0:T(8,128)(2,1)S(1)}, u32[]{:S(2)}, u32[]{:S(2)}) collective-permute-start(bf16[160,768]{1,0:T(8,128)(2,1)S(1)} %get-tuple-element.1180), channel_id=1, source_target_pairs={{0,4},{1,5},{2,6},{3,7},{12,8},{13,9},{14,10},{15,11},{16,20},{17,... | collective-permute-start | bytes 737288 | tf_op jit(solution)/shard_map/ppermute | solution.py:186
  11.2 11.6 %collective-permute-start.11 = (bf16[160,768]{1,0:T(8,128)(2,1)S(1)}, bf16[160,768]{1,0:T(8,128)(2,1)S(1)}, u32[]{:S(2)}, u32[]{:S(2)}) collective-permute-start(bf16[160,768]{1,0:T(8,128)(2,1)S(1)} %get-tuple-element.1181), channel_id=1, source_target_pairs={{0,6},{1,7},{2,4},{3,5},{12,10},{13,11},{14,8},{15,9},{16,22},{17,... | collective-permute-start | bytes 737288 | tf_op jit(solution)/shard_map/ppermute | solution.py:186
  12.6 15.6 %collective-permute-start.12 = (bf16[160,768]{1,0:T(8,128)(2,1)S(1)}, bf16[160,768]{1,0:T(8,128)(2,1)S(1)}, u32[]{:S(2)}, u32[]{:S(2)}) collective-permute-start(bf16[160,768]{1,0:T(8,128)(2,1)S(1)} %get-tuple-element.1182), channel_id=1, source_target_pairs={{0,8},{1,9},{2,10},{3,11},{12,4},{13,5},{14,6},{15,7},{16,24},{17,... | collective-permute-start | bytes 737288 | tf_op jit(solution)/shard_map/ppermute | solution.py:186
  14.9 17.1 %collective-permute-start.13 = (bf16[160,768]{1,0:T(8,128)(2,1)S(1)}, bf16[160,768]{1,0:T(8,128)(2,1)S(1)}, u32[]{:S(2)}, u32[]{:S(2)}) collective-permute-start(bf16[160,768]{1,0:T(8,128)(2,1)S(1)} %get-tuple-element.1183), channel_id=1, source_target_pairs={{0,10},{1,11},{2,8},{3,9},{12,6},{13,7},{14,4},{15,5},{16,26},{17,... | collective-permute-start | bytes 737288 | tf_op jit(solution)/shard_map/ppermute | solution.py:186
  16.2 16.5 %collective-permute-start.14 = (bf16[160,768]{1,0:T(8,128)(2,1)S(1)}, bf16[160,768]{1,0:T(8,128)(2,1)S(1)}, u32[]{:S(2)}, u32[]{:S(2)}) collective-permute-start(bf16[160,768]{1,0:T(8,128)(2,1)S(1)} %get-tuple-element.1184), channel_id=1, source_target_pairs={{4,8},{5,9},{6,10},{7,11},{8,4},{9,5},{10,6},{11,7},{20,24},{21,25... | collective-permute-start | bytes 737288 | tf_op jit(solution)/shard_map/ppermute | solution.py:186
  17.6 15.8 %collective-permute-start.15 = (bf16[160,768]{1,0:T(8,128)(2,1)S(1)}, bf16[160,768]{1,0:T(8,128)(2,1)S(1)}, u32[]{:S(2)}, u32[]{:S(2)}) collective-permute-start(bf16[160,768]{1,0:T(8,128)(2,1)S(1)} %get-tuple-element.1185), channel_id=1, source_target_pairs={{4,10},{5,11},{6,8},{7,9},{8,6},{9,7},{10,4},{11,5},{20,26},{21,27... | collective-permute-start | bytes 737288 | tf_op jit(solution)/shard_map/ppermute | solution.py:186
  22.9 51.1 %copy-start = (bf16[512,768]{1,0:T(8,128)(2,1)S(1)}, bf16[512,768]{1,0:T(8,128)(2,1)}, u32[]{:S(2)}) copy-start(bf16[512,768]{1,0:T(8,128)(2,1)} %x_ref.1) | copy-start | bytes 2359300
  22.9 51.1 %copy-start.2 = (s32[512]{0:T(512)S(1)}, s32[512]{0:T(512)}, u32[]{:S(2)}) copy-start(s32[512]{0:T(512)} %param.22) | copy-start | bytes 6148
  22.9 51.1 %copy-start.3 = (s32[512]{0:T(512)S(1)}, s32[512]{0:T(512)}, u32[]{:S(2)}) copy-start(s32[512]{0:T(512)} %param.23) | copy-start | bytes 6148
  22.9 11.2 %collective-permute-start.16 = (bf16[160,768]{1,0:T(8,128)(2,1)S(1)}, bf16[160,768]{1,0:T(8,128)(2,1)S(1)}, u32[]{:S(2)}, u32[]{:S(2)}) collective-permute-start(bf16[160,768]{1,0:T(8,128)(2,1)S(1)} %get-tuple-element.1178.refs_0_), channel_id=1, source_target_pairs={{4,5},{5,4},{6,7},{7,6},{8,9},{9,8},{10,11},{11,10},{20,21},{21,20... | collective-permute-start | bytes 737288 | tf_op jit(solution)/shard_map/ppermute | solution.py:188
  28.2 6.6 %collective-permute-start.17 = (bf16[160,768]{1,0:T(8,128)(2,1)S(1)}, bf16[160,768]{1,0:T(8,128)(2,1)S(1)}, u32[]{:S(2)}, u32[]{:S(2)}) collective-permute-start(bf16[160,768]{1,0:T(8,128)(2,1)S(1)} %collective-permute-done.9.refs_1_), channel_id=1, source_target_pairs={{4,5},{5,4},{6,7},{7,6},{8,9},{9,8},{10,11},{11,10},{20,21},{21,20... | collective-permute-start | bytes 737288 | tf_op jit(solution)/shard_map/ppermute | solution.py:188
  32.0 3.5 %collective-permute-start.18 = (bf16[160,768]{1,0:T(8,128)(2,1)S(1)}, bf16[160,768]{1,0:T(8,128)(2,1)S(1)}, u32[]{:S(2)}, u32[]{:S(2)}) collective-permute-start(bf16[160,768]{1,0:T(8,128)(2,1)S(1)} %collective-permute-done.10.refs_2_), channel_id=1, source_target_pairs={{4,5},{5,4},{6,7},{7,6},{8,9},{9,8},{10,11},{11,10},{20,21},{21,20... | collective-permute-start | bytes 737288 | tf_op jit(solution)/shard_map/ppermute | solution.py:188
  32.7 3.5 %collective-permute-start.19 = (bf16[160,768]{1,0:T(8,128)(2,1)S(1)}, bf16[160,768]{1,0:T(8,128)(2,1)S(1)}, u32[]{:S(2)}, u32[]{:S(2)}) collective-permute-start(bf16[160,768]{1,0:T(8,128)(2,1)S(1)} %collective-permute-done.11.refs_3_), channel_id=1, source_target_pairs={{4,5},{5,4},{6,7},{7,6},{8,9},{9,8},{10,11},{11,10},{20,21},{21,20... | collective-permute-start | bytes 737288 | tf_op jit(solution)/shard_map/ppermute | solution.py:188
  33.4 2.8 %collective-permute-start.20 = (bf16[160,768]{1,0:T(8,128)(2,1)S(1)}, bf16[160,768]{1,0:T(8,128)(2,1)S(1)}, u32[]{:S(2)}, u32[]{:S(2)}) collective-permute-start(bf16[160,768]{1,0:T(8,128)(2,1)S(1)} %collective-permute-done.12.refs_4_), channel_id=1, source_target_pairs={{4,5},{5,4},{6,7},{7,6},{8,9},{9,8},{10,11},{11,10},{20,21},{21,20... | collective-permute-start | bytes 737288 | tf_op jit(solution)/shard_map/ppermute | solution.py:188
  34.1 2.1 %collective-permute-start.21 = (bf16[160,768]{1,0:T(8,128)(2,1)S(1)}, bf16[160,768]{1,0:T(8,128)(2,1)S(1)}, u32[]{:S(2)}, u32[]{:S(2)}) collective-permute-start(bf16[160,768]{1,0:T(8,128)(2,1)S(1)} %collective-permute-done.13.refs_5_), channel_id=1, source_target_pairs={{4,5},{5,4},{6,7},{7,6},{8,9},{9,8},{10,11},{11,10},{20,21},{21,20... | collective-permute-start | bytes 737288 | tf_op jit(solution)/shard_map/ppermute | solution.py:188
  34.8 1.4 %collective-permute-start.22 = (bf16[160,768]{1,0:T(8,128)(2,1)S(1)}, bf16[160,768]{1,0:T(8,128)(2,1)S(1)}, u32[]{:S(2)}, u32[]{:S(2)}) collective-permute-start(bf16[160,768]{1,0:T(8,128)(2,1)S(1)} %collective-permute-done.14.refs_6_), channel_id=1, source_target_pairs={{4,5},{5,4},{6,7},{7,6},{8,9},{9,8},{10,11},{11,10},{20,21},{21,20... | collective-permute-start | bytes 737288 | tf_op jit(solution)/shard_map/ppermute | solution.py:188
  35.5 0.7 collective-permute-start.23
  37.0 35.1 %all-to-all-start.4 = ((f32[16,8,128]{2,1,0:T(8,128)}), f32[16,8,128]{2,1,0:T(8,128)S(1)}, u32[]{:S(2)}, u32[]{:S(2)}) async-start(f32[16,8,128]{2,1,0:T(8,128)} %bitcast.12), calls=%async_computation.4 | async-start | bytes 131072 | tf_op jit(solution)/shard_map/all_to_all | solution.py:202
  74.2 0.6 copy-start.4

commit v2 on v1

--- a/solution.py
+++ b/solution.py
@@ -72,66 +72,151 @@
             outs[k][BLOCK - META :, :256] = tail.astype(jnp.bfloat16)
 
 
-def compare_kernel(*refs):
-    blocks = refs[: 2 * CHIPS]
-    out_ref, keys, codes, sems = refs[2 * CHIPS :]
+def fill_codes(keys, codes, first_block, blocks):
+    eye = (
+        lax.broadcasted_iota(jnp.int32, (BLOCK, 256), 0)
+        == lax.broadcasted_iota(jnp.int32, (BLOCK, 256), 1)
+    ).astype(jnp.float32).astype(jnp.bfloat16)
+    lane = lax.broadcasted_iota(jnp.int32, (1, META), 1)
+    first = META - (BLOCK - CAP)
+    scale = jnp.where(
+        lane == first, 4096.0, jnp.where(lane == first + 1, 64.0, jnp.where(lane == first + 2, 1.0, 0.0))
+    )
+    over = jnp.zeros((1, 128), jnp.float32)
+    for n in range(first_block, first_block + blocks):
+        meta = keys[(n + 1) * BLOCK - META : (n + 1) * BLOCK, :256]
+        over = jnp.maximum(over, meta[META - 1 :, :128].astype(jnp.float32))
+        columns = lax.dot_general(eye, meta, NT, preferred_element_type=jnp.float32)
+        code = jnp.sum(columns * scale, axis=1, keepdims=True)
+        codes[n * BLOCK : (n + 1) * BLOCK] = jnp.broadcast_to(code, (BLOCK, 128))
+    return over
+
+
+def best_of(keys, codes, key_start, key_count, key_step, query_start, size):
+    query = keys[query_start : query_start + size]
+    top = jnp.transpose(codes[query_start : query_start + size])[:1]
+    base = jnp.floor(top * (1.0 / 4096.0)) * 4096.0
+    best = jnp.full((8, size), -1.0, jnp.float32)
+    for start in range(key_start, key_start + key_count, key_step):
+        score = lax.dot_general(
+            keys[start : start + key_step], query, NT, preferred_element_type=jnp.float32
+        )
+        code = jnp.concatenate([codes[start : start + key_step]] * (size // 128), axis=1)
+        score = jnp.where((code >= base) & (code < top), score, -1.0)
+        best = jnp.maximum(best, jnp.max(score.reshape(key_step // 8, 8, size), axis=0))
+    return best
+
+
+def fetch(pairs, sems):
+    copies = [
+        pltpu.make_async_copy(source, target, sems.at[n]) for n, (source, target) in enumerate(pairs)
+    ]
+    for copy in copies:
+        copy.start()
+    for copy in copies:
+        copy.wait()
+
+
+def join_kernel(*refs):
+    blocks, out_ref, sems = refs[:-2], refs[-2], refs[-1]
+    fetch([(ref, out_ref.at[pl.ds(n * BLOCK, BLOCK)]) for n, ref in enumerate(blocks)], sems)
+
+
+EARLY = (0, 1, 2, 3, 6, 7)
+LATE = (4, 5)
+EARLY_ROWS = len(EARLY) * BLOCK
+LATE_ROWS = len(LATE) * BLOCK
+EARLY_QUERIES = 1024
+BOTH_QUERIES = 2048
+LATE_QUERIES = 384
+LATE_START = 2 * EARLY_ROWS
+
+
+def early_kernel(mine_ref, other_ref, best_ref, over_ref, keys, codes, sems):
+    @pl.when(is_home(lax.axis_index("owner") // 2))
+    def _():
+        fetch(
+            [
+                (mine_ref, keys.at[pl.ds(0, EARLY_ROWS)]),
+                (other_ref, keys.at[pl.ds(EARLY_ROWS, EARLY_ROWS)]),
+            ],
+            sems,
+        )
+        over = fill_codes(keys, codes, 0, 2 * len(EARLY))
+        over_ref[...] = jnp.broadcast_to(over, over_ref.shape)
+        for start in range(0, EARLY_QUERIES, 256):
+            best_ref[:, start : start + 256] = best_of(
+                keys, codes, 0, 2 * EARLY_ROWS, 640, start, 256
+            )
+
+
+def late_kernel(mine_ref, other_ref, first_ref, second_ref, early_ref, best_ref, late_ref, keys, codes, sems):
+    @pl.when(is_home(lax.axis_index("owner") // 2))
+    def _():
+        fetch(
+            [
+                (mine_ref, keys.at[pl.ds(0, EARLY_ROWS)]),
+                (other_ref, keys.at[pl.ds(EARLY_ROWS, EARLY_ROWS)]),
+                (first_ref, keys.at[pl.ds(LATE_START, BLOCK)]),
+                (second_ref, keys.at[pl.ds(LATE_START + BLOCK, BLOCK)]),
+            ],
+            sems,
+        )
+        fill_codes(keys, codes, 0, 2 * len(EARLY) + len(LATE))
+        for start in range(0, BOTH_QUERIES, 256):
+            found = best_of(keys, codes, LATE_START, LATE_ROWS, LATE_ROWS, start, 256)
+            if start + 256 <= EARLY_ROWS:
+                found = jnp.maximum(found, early_ref[:, start : start + 256])
+            elif start < EARLY_ROWS:
+                lane = lax.broadcasted_iota(jnp.int32, (8, 256), 1)
+                known = jnp.where(lane < EARLY_ROWS - start, early_ref[:, start : start + 256], -1.0)
+                found = jnp.maximum(found, known)
+            best_ref[:, start : start + 256] = found
+        late_ref[...] = best_of(
+            keys, codes, 0, LATE_START + LATE_ROWS, 448, LATE_START, LATE_QUERIES
+        )
+
+
+def last_kernel(*refs):
+    mine, other = refs[: len(LATE)], refs[len(LATE) : 2 * len(LATE)]
+    early_ref, late_ref, over_ref, out_ref, keys, codes, sems = refs[2 * len(LATE) :]
     me = lax.axis_index("owner")
     chip = me // 2
     core = me % 2
 
     @pl.when(is_home(chip))
     def _():
-        copies = [
-            pltpu.make_async_copy(ref, keys.at[pl.ds(n * BLOCK, BLOCK)], sems.at[n])
-            for n, ref in enumerate(blocks)
-        ]
-        for copy in copies:
-            copy.start()
-        for copy in copies:
-            copy.wait()
-        eye = (
-            lax.broadcasted_iota(jnp.int32, (BLOCK, 256), 0)
-            == lax.broadcasted_iota(jnp.int32, (BLOCK, 256), 1)
-        ).astype(jnp.float32).astype(jnp.bfloat16)
-        lane = lax.broadcasted_iota(jnp.int32, (1, META), 1)
-        first = META - (BLOCK - CAP)
-        scale = jnp.where(
-            lane == first, 4096.0, jnp.where(lane == first + 1, 64.0, jnp.where(lane == first + 2, 1.0, 0.0))
-        )
-        over = jnp.zeros((1, 128), jnp.float32)
-        for n in range(2 * CHIPS):
-            meta = keys[(n + 1) * BLOCK - META : (n + 1) * BLOCK, :256]
-            over = jnp.maximum(over, meta[META - 1 :, :128].astype(jnp.float32))
-            columns = lax.dot_general(eye, meta, NT, preferred_element_type=jnp.float32)
-            code = jnp.sum(columns * scale, axis=1, keepdims=True)
-            codes[n * BLOCK : (n + 1) * BLOCK] = jnp.broadcast_to(code, (BLOCK, 128))
-        over = jnp.max(over)
-        queries = CHIPS * BLOCK
-        step = 2 * queries // 4
-        found = []
-        for t in range(queries // 256):
-            query = keys[t * 256 : (t + 1) * 256]
-            top = jnp.transpose(codes[t * 256 : (t + 1) * 256])[:1]
-            base = jnp.floor(top * (1.0 / 4096.0)) * 4096.0
-            best = jnp.full((8, 256), -1.0, jnp.float32)
-            for j in range(4):
-                score = lax.dot_general(
-                    keys[j * step : (j + 1) * step], query, NT, preferred_element_type=jnp.float32
-                )
-                code = codes[j * step : (j + 1) * step]
-                code = jnp.concatenate([code, code], axis=1)
-                score = jnp.where((code >= base) & (code < top), score, -1.0)
-                best = jnp.maximum(best, jnp.max(score.reshape(step // 8, 8, 256), axis=0))
-            found.append(jnp.max(best, axis=0, keepdims=True))
-        found = jnp.concatenate(found, axis=1)
-        place = lax.broadcasted_iota(jnp.int32, (1, queries), 1) % BLOCK
-        found = jnp.where(place >= CAP, over, found)
-        found = jnp.broadcast_to(found, (8, queries))
-        for k in range(CHIPS):
-            line = found if k == 0 else pltpu.roll(found, queries - k * BLOCK, 1)
-            row = 8 * (2 * (chip ^ k) + core)
+        fetch(
+            [
+                (ref, keys.at[pl.ds(n * BLOCK, BLOCK)])
+                for n, ref in enumerate(mine + other)
+            ],
+            sems,
+        )
+        over = fill_codes(keys, codes, 0, 2 * len(LATE))
+        over = jnp.max(jnp.maximum(over, over_ref[:1]))
+        late = jnp.maximum(
+            late_ref[...], best_of(keys, codes, LATE_ROWS, LATE_ROWS, LATE_ROWS, 0, LATE_QUERIES)
+        )
+        early = early_ref[...]
+
+        def send(found, start, to_chip, to_core):
+            line = jnp.max(found, axis=0, keepdims=True)
+            line = jnp.broadcast_to(line, (8, line.shape[1]))
+            if start:
+                line = pltpu.roll(line, line.shape[1] - start, 1)
+            row = 8 * (2 * to_chip + to_core)
             out_ref[pl.ds(row, 1), :] = line[:1, :128]
-            out_ref[pl.ds(row + 1, 1), :] = line[:1, 128:256]
+            lane = lax.broadcasted_iota(jnp.int32, (1, 128), 1)
+            out_ref[pl.ds(row + 1, 1), :] = jnp.where(lane >= CAP - 128, over, line[:1, 128:256])
+
+        early = jnp.max(early, axis=0, keepdims=True)
+        late = jnp.max(late, axis=0, keepdims=True)
+        for n, k in enumerate(EARLY):
+            send(early, n * BLOCK, chip ^ k, core)
+            send(early, EARLY_ROWS + n * BLOCK, chip ^ k, 1 - core)
+        for n, k in enumerate(LATE):
+            send(late, n * BLOCK, chip ^ k, core)
 
 
 def unpack_kernel(back_ref, slot_ref, best_ref, over_ref):
@@ -150,6 +235,9 @@
         def _():
             slot = slot_ref[k : k + 1]
             part = back_ref[pl.ds(pl.multiple_of(8 * (2 * home + core), 8), 8), :]
+            if k in EARLY:
+                second = back_ref[pl.ds(pl.multiple_of(8 * (2 * home + 1 - core), 8), 8), :]
+                part = jnp.maximum(part, second)
             total = jnp.zeros((8, rows), jnp.float32)
             for n in range(2):
                 value = part[n : n + 1]
@@ -179,26 +267,72 @@
         name="pack",
     )(embeds, clusters.reshape(1, rows), ranks.reshape(1, rows))
     blocks, slot = list(packed[:CHIPS]), packed[CHIPS]
-    for k in (4, 5, 6, 7, 3, 2, 1):
+    for k in (2, 3, 6, 7, 1, 4, 5):
         route = [
             (2 * s + c, 2 * (s ^ k) + c) for s in range(CHIPS) if s ^ k in HOMES for c in range(2)
         ]
         blocks[k] = lax.ppermute(blocks[k], "owner", route)
     swap = [(2 * h + c, 2 * h + 1 - c) for h in HOMES for c in range(2)]
-    other = [lax.ppermute(block, "owner", swap) for block in blocks]
+    anywhere = pl.BlockSpec(memory_space=pl.ANY)
+
+    def keys_scratch(total, copies):
+        return [
+            pltpu.VMEM((total, width), jnp.bfloat16),
+            pltpu.VMEM((total, 128), jnp.float32),
+            pltpu.SemaphoreType.DMA((copies,)),
+        ]
+
+    def cost(pairs):
+        return pl.CostEstimate(
+            flops=8 * pairs * width, bytes_accessed=2 * 2 * EARLY_ROWS * width, transcendentals=0
+        )
+
+    mine = pl.pallas_call(
+        join_kernel,
+        out_shape=jax.ShapeDtypeStruct((EARLY_ROWS, width), jnp.bfloat16),
+        in_specs=[anywhere] * len(EARLY),
+        out_specs=anywhere,
+        scratch_shapes=[pltpu.SemaphoreType.DMA((len(EARLY),))],
+        name="join",
+    )(*[blocks[k] for k in EARLY])
+    other = lax.ppermute(mine, "owner", swap)
+    late_mine = [blocks[k] for k in LATE]
+    late_other = [lax.ppermute(block, "owner", swap) for block in late_mine]
+    early, over = pl.pallas_call(
+        early_kernel,
+        out_shape=[
+            jax.ShapeDtypeStruct((8, EARLY_QUERIES), jnp.float32),
+            jax.ShapeDtypeStruct((8, 128), jnp.float32),
+        ],
+        in_specs=[anywhere] * 2,
+        out_specs=[vmem] * 2,
+        scratch_shapes=keys_scratch(2 * EARLY_ROWS, 2),
+        compiler_params=params,
+        cost_estimate=cost(EARLY_QUERIES * 2 * EARLY_ROWS),
+        name="early",
+    )(mine, other)
+    early, late = pl.pallas_call(
+        late_kernel,
+        out_shape=[
+            jax.ShapeDtypeStruct((8, BOTH_QUERIES), jnp.float32),
+            jax.ShapeDtypeStruct((8, LATE_QUERIES), jnp.float32),
+        ],
+        in_specs=[anywhere] * 4 + [vmem],
+        out_specs=[vmem] * 2,
+        scratch_shapes=keys_scratch(max(BOTH_QUERIES, LATE_START + LATE_QUERIES), 4),
+        compiler_params=params,
+        cost_estimate=cost(BOTH_QUERIES * LATE_ROWS + LATE_QUERIES * 2 * EARLY_ROWS),
+        name="late",
+    )(mine, other, *late_mine, early)
     found = pl.pallas_call(
-        compare_kernel,
+        last_kernel,
         out_shape=jax.ShapeDtypeStruct((8 * OWNERS, 128), jnp.float32),
-        in_specs=[pl.BlockSpec(memory_space=pl.ANY)] * (2 * CHIPS),
+        in_specs=[anywhere] * (2 * len(LATE)) + [vmem] * 3,
         out_specs=vmem,
-        scratch_shapes=[
-            pltpu.VMEM((2 * CHIPS * BLOCK, width), jnp.bfloat16),
-            pltpu.VMEM((2 * CHIPS * BLOCK, 128), jnp.float32),
-            pltpu.SemaphoreType.DMA((2 * CHIPS,)),
-        ],
+        scratch_shapes=keys_scratch(2 * LATE_ROWS, 2 * len(LATE)),
         compiler_params=params,
-        name="compare",
-    )(*blocks, *other)
+        name="last",
+    )(*late_mine, *late_other, early, late, over)
     back = lax.all_to_all(
         found.reshape(OWNERS, 8, 128), "owner", split_axis=0, concat_axis=0, tiled=True
     )

time: 75.3 us -> 123 us (1.63)
  Pallas kernels: 4.82 us -> 50.6 us
  starting transfers between devices: 48.3 us -> 42.7 us
  waiting for transfers between devices: 19.9 us -> 24.6 us
  local copies, waits for them, and re-layouts: 0.58 us -> 3.49 us
    pallas_call x1 -> x4, Pallas kernels: 0.78 us -> 46.6 us  [the longest x1 45.8 us: meet(): pl.pallas_call(join_kernel, out_shape=jax.ShapeDtypeStruct((EARLY_ROWS, w...]
    all_to_all x1, starting transfers between devices: 28.2 us -> 18 us  [meet(): lax.all_to_all(found.reshape(OWNERS, 8, 128), 'owner', split_axis=0, conc...]
    ppermute x7, starting transfers between devices: 14.6 us -> 22.7 us  [meet(): blocks[k] = lax.ppermute(blocks[k], 'owner', route)]
    ppermute x7, waiting for transfers between devices: 13 us -> 17.7 us  [meet(): blocks[k] = lax.ppermute(blocks[k], 'owner', route)]
    ppermute x8 -> x3, starting transfers between devices: 5.51 us -> 2.08 us  [the longest x2 1.33 us: meet(): late_other = [lax.ppermute(block, 'owner', swap) for block in late_mine]]
    unnamed x8 -> x22, local copies, waits for them, and re-layouts: 0.58 us -> 3.49 us
  transfers between devices with their start and end apart: 16 -> 11, of which waited for: 5 -> 5; matrix products, arithmetic and copies ran while one was open for 0% -> 0% of each run, Pallas kernels for 0% -> 0%
where the time goes in v2:
time: 123 us
  Pallas kernels  50.6 us (41%)
  starting transfers between devices  42.7 us (35%)
  waiting for transfers between devices  24.6 us (20%)
  local copies, waits for them, and re-layouts  3.49 us (3%)
    pallas_call x1, Pallas kernels, meet(): pl.pallas_call(join_kernel, out_shape=jax.ShapeDtypeStruct((EARLY_ROWS, w...  45.8 us
    ppermute x7, starting transfers between devices, meet(): blocks[k] = lax.ppermute(blocks[k], 'owner', route)  22.7 us
    all_to_all x1, starting transfers between devices, meet(): lax.all_to_all(found.reshape(OWNERS, 8, 128), 'owner', split_axis=0, conc...  18 us
    ppermute x7, waiting for transfers between devices, meet(): blocks[k] = lax.ppermute(blocks[k], 'owner', route)  17.7 us
    all_to_all x1, waiting for transfers between devices, meet(): lax.all_to_all(found.reshape(OWNERS, 8, 128), 'owner', split_axis=0, conc...  6.9 us
    unnamed x22, local copies, waits for them, and re-layouts  3.49 us
    pallas_call x1, Pallas kernels, meet(): pl.pallas_call(pack_kernel, out_shape=[jax.ShapeDtypeStruct((BLOCK, width...  2.86 us
  transfers between devices with their start and end apart: 11, of which 5 were waited for; matrix products, arithmetic and copies ran while one was open for 0% of the time, Pallas kernels for 0%

profile of v2, /device:TPU:0, one launch (start us, length us, event | category | flops | bytes accessed | tf_op | source)
XLA Modules:
  0.0 122.6 jit_solution(16970589243835172391)
XLA Ops:
  0.0 2.9 %pack.1 = (bf16[160,768]{1,0:T(8,128)(2,1)S(1)}, bf16[160,768]{1,0:T(8,128)(2,1)S(1)}, bf16[160,768]{1,0:T(8,128)(2,1)S(1)}, bf16[160,768]{1,0:T(8,128)(2,1)S(1)...) custom-call(bf16[512,768]{1,0:T(8,128)(2,1)} %x_ref.1, ...), custom_call_target="tpu_custom_call" | custom-call | tf_op jit(solution)/shard_map/pack/pallas_call | solution.py:260
  2.9 0.0 copy-start.1
  2.9 0.7 copy-done.1
  3.6 0.7 collective-permute-start.13
  4.2 7.7 %collective-permute-start.14 = (bf16[160,768]{1,0:T(8,128)(2,1)S(1)}, bf16[160,768]{1,0:T(8,128)(2,1)S(1)}, u32[]{:S(2)}, u32[]{:S(2)}) collective-permute-start(bf16[160,768]{1,0:T(8,128)(2,1)S(1)} %get-tuple-element.1186), channel_id=1, source_target_pairs={{0,4},{1,5},{2,6},{3,7},{12,8},{13,9},{14,10},{15,11},{16,20},{17,... | collective-permute-start | bytes 737288 | tf_op jit(solution)/shard_map/ppermute | solution.py:274
  11.9 1.3 %collective-permute-start.15 = (bf16[160,768]{1,0:T(8,128)(2,1)S(1)}, bf16[160,768]{1,0:T(8,128)(2,1)S(1)}, u32[]{:S(2)}, u32[]{:S(2)}) collective-permute-start(bf16[160,768]{1,0:T(8,128)(2,1)S(1)} %get-tuple-element.1187), channel_id=1, source_target_pairs={{0,6},{1,7},{2,4},{3,5},{12,10},{13,11},{14,8},{15,9},{16,22},{17,... | collective-permute-start | bytes 737288 | tf_op jit(solution)/shard_map/ppermute | solution.py:274
  13.3 0.7 collective-permute-start.16
  13.9 0.7 collective-permute-start.17
  14.6 0.0 collective-permute-done.13.refs_1_
  14.6 0.0 copy-start.4
  14.6 3.7 %collective-permute-done.14.refs_2_ = bf16[160,768]{1,0:T(8,128)(2,1)S(1)} collective-permute-done((bf16[160,768]{1,0:T(8,128)(2,1)S(1)}, bf16[160,768]{1,0:T(8,128)(2,1)S(1)}, u32[]{:S(2)}, u32[]{:S(2)}) %collective-permute-start.14) | collective-permute-done | bytes 245792 | tf_op jit(solution)/shard_map/ppermute | solution.py:274
  18.3 0.0 copy-start.5
  18.3 5.8 %collective-permute-done.15.refs_3_ = bf16[160,768]{1,0:T(8,128)(2,1)S(1)} collective-permute-done((bf16[160,768]{1,0:T(8,128)(2,1)S(1)}, bf16[160,768]{1,0:T(8,128)(2,1)S(1)}, u32[]{:S(2)}, u32[]{:S(2)}) %collective-permute-start.15) | collective-permute-done | bytes 245792 | tf_op jit(solution)/shard_map/ppermute | solution.py:274
  24.2 0.0 copy-start.6
  24.2 0.0 collective-permute-done.16.refs_4_
  24.2 0.0 copy-start.7
  24.2 0.0 collective-permute-done.17.refs_5_
  24.2 0.0 copy-start.8
  24.2 0.0 copy-done.4
  24.2 0.0 copy-done.5
  24.2 0.6 copy-done.6
  24.8 0.1 copy-done.7
  25.0 0.1 copy-done.8
  25.0 45.8 %join.1.mine_ref = bf16[960,768]{1,0:T(8,128)(2,1)} custom-call(bf16[160,768]{1,0:T(8,128)(2,1)} %copy-done.1, bf16[160,768]{1,0:T(8,128)(2,1)} %copy-done.4, bf16[160,768]{1,0:T(8,128)(2,1)} %copy-done.5, bf16[160,768]{1,0:T(8,128)(2,1)} %copy-done.6, bf16[160,768]{1,0:T(8,128)(2,1)} %copy-done.7, bf16[160,768]{1,0:T(8,128)(2,1)} %copy-done.8), custom_call_target="tpu_custom_call" | custom-call | tf_op jit(solution)/shard_map/join/pallas_call | solution.py:290
  70.9 0.8 collective-permute-start.18
  71.6 9.4 %collective-permute-start.9 = (bf16[160,768]{1,0:T(8,128)(2,1)S(1)}, bf16[160,768]{1,0:T(8,128)(2,1)S(1)}, u32[]{:S(2)}, u32[]{:S(2)}) collective-permute-start(bf16[160,768]{1,0:T(8,128)(2,1)S(1)} %get-tuple-element.1182), channel_id=1, source_target_pairs={{0,8},{1,9},{2,10},{3,11},{12,4},{13,5},{14,6},{15,7},{16,24},{17,... | collective-permute-start | bytes 737288 | tf_op jit(solution)/shard_map/ppermute | solution.py:274
  81.0 2.2 %collective-permute-start.10 = (bf16[160,768]{1,0:T(8,128)(2,1)S(1)}, bf16[160,768]{1,0:T(8,128)(2,1)S(1)}, u32[]{:S(2)}, u32[]{:S(2)}) collective-permute-start(bf16[160,768]{1,0:T(8,128)(2,1)S(1)} %get-tuple-element.1183), channel_id=1, source_target_pairs={{0,10},{1,11},{2,8},{3,9},{12,6},{13,7},{14,4},{15,5},{16,26},{17,... | collective-permute-start | bytes 737288 | tf_op jit(solution)/shard_map/ppermute | solution.py:274
  83.3 4.0 %collective-permute-done.9.first_ref.refs_0_ = bf16[160,768]{1,0:T(8,128)(2,1)S(1)} collective-permute-done((bf16[160,768]{1,0:T(8,128)(2,1)S(1)}, bf16[160,768]{1,0:T(8,128)(2,1)S(1)}, u32[]{:S(2)}, u32[]{:S(2)}) %collective-permute-start.9) | collective-permute-done | bytes 245792 | tf_op jit(solution)/shard_map/ppermute | solution.py:274
  87.3 0.7 collective-permute-start.11
  87.9 4.2 %collective-permute-done.10.second_ref.refs_1_ = bf16[160,768]{1,0:T(8,128)(2,1)S(1)} collective-permute-done((bf16[160,768]{1,0:T(8,128)(2,1)S(1)}, bf16[160,768]{1,0:T(8,128)(2,1)S(1)}, u32[]{:S(2)}, u32[]{:S(2)}) %collective-permute-start.10) | collective-permute-done | bytes 245792 | tf_op jit(solution)/shard_map/ppermute | solution.py:274
  92.1 0.7 collective-permute-start.12
  92.8 0.0 collective-permute-done.18.other_ref
  92.8 0.0 copy-start
  92.8 1.4 %copy-done = bf16[960,768]{1,0:T(8,128)(2,1)S(1)} copy-done((bf16[960,768]{1,0:T(8,128)(2,1)S(1)}, bf16[960,768]{1,0:T(8,128)(2,1)}, u32[]{:S(2)}) %copy-start) | copy-done | bytes 1474584
  94.2 0.0 copy-start.2
  94.2 0.0 copy-start.9
  94.3 0.0 copy-start.10
  94.3 0.1 late.1
  94.3 0.0 collective-permute-done.11.refs_2_
  94.3 0.0 collective-permute-done.12.refs_3_
  94.3 0.7 last.1
  95.0 18.0 %all-to-all-start.4 = ((f32[16,8,128]{2,1,0:T(8,128)}), f32[16,8,128]{2,1,0:T(8,128)S(1)}, u32[]{:S(2)}, u32[]{:S(2)}) async-start(f32[16,8,128]{2,1,0:T(8,128)} %bitcast.12), calls=%async_computation.4 | async-start | bytes 131072 | tf_op jit(solution)/shard_map/all_to_all | solution.py:336
  113.0 6.9 %all-to-all-done.4 = f32[16,8,128]{2,1,0:T(8,128)S(1)} async-done(((f32[16,8,128]{2,1,0:T(8,128)}), f32[16,8,128]{2,1,0:T(8,128)S(1)}, u32[]{:S(2)}, u32[]{:S(2)}) %all-to-all-start.4) | async-done | bytes 65568 | tf_op jit(solution)/shard_map/all_to_all | solution.py:336
  119.9 1.2 unpack.1
  121.7 0.0 copy-done.2
  121.7 0.0 copy-done.9
  121.8 0.0 copy-done.10
  121.8 0.2 conditional.1
  122.0 0.0 copy-start.11
  122.0 0.6 copy-done.11
  (1 shorter events, 0.0 us)
Async XLA Ops:
  2.9 0.7 copy-start.1
  3.6 11.1 %collective-permute-start.13 = (bf16[160,768]{1,0:T(8,128)(2,1)S(1)}, bf16[160,768]{1,0:T(8,128)(2,1)S(1)}, u32[]{:S(2)}, u32[]{:S(2)}) collective-permute-start(bf16[160,768]{1,0:T(8,128)(2,1)S(1)} %get-tuple-element.1185), channel_id=1, source_target_pairs={{4,6},{5,7},{6,4},{7,5},{8,10},{9,11},{10,8},{11,9},{20,22},{21,23... | collective-permute-start | bytes 737288 | tf_op jit(solution)/shard_map/ppermute | solution.py:274
  4.2 14.1 %collective-permute-start.14 = (bf16[160,768]{1,0:T(8,128)(2,1)S(1)}, bf16[160,768]{1,0:T(8,128)(2,1)S(1)}, u32[]{:S(2)}, u32[]{:S(2)}) collective-permute-start(bf16[160,768]{1,0:T(8,128)(2,1)S(1)} %get-tuple-element.1186), channel_id=1, source_target_pairs={{0,4},{1,5},{2,6},{3,7},{12,8},{13,9},{14,10},{15,11},{16,20},{17,... | collective-permute-start | bytes 737288 | tf_op jit(solution)/shard_map/ppermute | solution.py:274
  11.9 12.2 %collective-permute-start.15 = (bf16[160,768]{1,0:T(8,128)(2,1)S(1)}, bf16[160,768]{1,0:T(8,128)(2,1)S(1)}, u32[]{:S(2)}, u32[]{:S(2)}) collective-permute-start(bf16[160,768]{1,0:T(8,128)(2,1)S(1)} %get-tuple-element.1187), channel_id=1, source_target_pairs={{0,6},{1,7},{2,4},{3,5},{12,10},{13,11},{14,8},{15,9},{16,22},{17,... | collective-permute-start | bytes 737288 | tf_op jit(solution)/shard_map/ppermute | solution.py:274
  13.3 10.9 %collective-permute-start.16 = (bf16[160,768]{1,0:T(8,128)(2,1)S(1)}, bf16[160,768]{1,0:T(8,128)(2,1)S(1)}, u32[]{:S(2)}, u32[]{:S(2)}) collective-permute-start(bf16[160,768]{1,0:T(8,128)(2,1)S(1)} %get-tuple-element.1188), channel_id=1, source_target_pairs={{4,8},{5,9},{6,10},{7,11},{8,4},{9,5},{10,6},{11,7},{20,24},{21,25... | collective-permute-start | bytes 737288 | tf_op jit(solution)/shard_map/ppermute | solution.py:274
  13.9 10.2 %collective-permute-start.17 = (bf16[160,768]{1,0:T(8,128)(2,1)S(1)}, bf16[160,768]{1,0:T(8,128)(2,1)S(1)}, u32[]{:S(2)}, u32[]{:S(2)}) collective-permute-start(bf16[160,768]{1,0:T(8,128)(2,1)S(1)} %get-tuple-element.1189), channel_id=1, source_target_pairs={{4,10},{5,11},{6,8},{7,9},{8,6},{9,7},{10,4},{11,5},{20,26},{21,27... | collective-permute-start | bytes 737288 | tf_op jit(solution)/shard_map/ppermute | solution.py:274
  14.6 9.6 %copy-start.4 = (bf16[160,768]{1,0:T(8,128)(2,1)}, bf16[160,768]{1,0:T(8,128)(2,1)S(1)}, u32[]{:S(2)}) copy-start(bf16[160,768]{1,0:T(8,128)(2,1)S(1)} %collective-permute-done.13.refs_1_) | copy-start | bytes 737284
  18.3 5.9 %copy-start.5 = (bf16[160,768]{1,0:T(8,128)(2,1)}, bf16[160,768]{1,0:T(8,128)(2,1)S(1)}, u32[]{:S(2)}) copy-start(bf16[160,768]{1,0:T(8,128)(2,1)S(1)} %collective-permute-done.14.refs_2_) | copy-start | bytes 737284
  24.2 0.7 copy-start.6
  24.2 0.8 copy-start.7
  24.2 0.9 copy-start.8
  70.9 22.0 %collective-permute-start.18 = (bf16[960,768]{1,0:T(8,128)(2,1)}, bf16[960,768]{1,0:T(8,128)(2,1)S(1)}, u32[]{:S(2)}, u32[]{:S(2)}) collective-permute-start(bf16[960,768]{1,0:T(8,128)(2,1)} %join.1.mine_ref), channel_id=1, source_target_pairs={{4,5},{5,4},{6,7},{7,6},{8,9},{9,8},{10,11},{11,10},{20,21},{21,20... | collective-permute-start | bytes 4423688 | tf_op jit(solution)/shard_map/ppermute | solution.py:298
  71.6 15.7 %collective-permute-start.9 = (bf16[160,768]{1,0:T(8,128)(2,1)S(1)}, bf16[160,768]{1,0:T(8,128)(2,1)S(1)}, u32[]{:S(2)}, u32[]{:S(2)}) collective-permute-start(bf16[160,768]{1,0:T(8,128)(2,1)S(1)} %get-tuple-element.1182), channel_id=1, source_target_pairs={{0,8},{1,9},{2,10},{3,11},{12,4},{13,5},{14,6},{15,7},{16,24},{17,... | collective-permute-start | bytes 737288 | tf_op jit(solution)/shard_map/ppermute | solution.py:274
  81.0 11.1 %collective-permute-start.10 = (bf16[160,768]{1,0:T(8,128)(2,1)S(1)}, bf16[160,768]{1,0:T(8,128)(2,1)S(1)}, u32[]{:S(2)}, u32[]{:S(2)}) collective-permute-start(bf16[160,768]{1,0:T(8,128)(2,1)S(1)} %get-tuple-element.1183), channel_id=1, source_target_pairs={{0,10},{1,11},{2,8},{3,9},{12,6},{13,7},{14,4},{15,5},{16,26},{17,... | collective-permute-start | bytes 737288 | tf_op jit(solution)/shard_map/ppermute | solution.py:274
  87.3 7.1 %collective-permute-start.11 = (bf16[160,768]{1,0:T(8,128)(2,1)S(1)}, bf16[160,768]{1,0:T(8,128)(2,1)S(1)}, u32[]{:S(2)}, u32[]{:S(2)}) collective-permute-start(bf16[160,768]{1,0:T(8,128)(2,1)S(1)} %collective-permute-done.9.first_ref.refs_0_), channel_id=1, source_target_pairs={{4,5},{5,4},{6,7},{7,6},{8,9},{9,8},{10,11},{11,10},{20,21},{21,20... | collective-permute-start | bytes 737288 | tf_op jit(solution)/shard_map/ppermute | solution.py:300
  92.1 2.2 %collective-permute-start.12 = (bf16[160,768]{1,0:T(8,128)(2,1)S(1)}, bf16[160,768]{1,0:T(8,128)(2,1)S(1)}, u32[]{:S(2)}, u32[]{:S(2)}) collective-permute-start(bf16[160,768]{1,0:T(8,128)(2,1)S(1)} %collective-permute-done.10.second_ref.refs_1_), channel_id=1, source_target_pairs={{4,5},{5,4},{6,7},{7,6},{8,9},{9,8},{10,11},{11,10},{20,21},{21,20... | collective-permute-start | bytes 737288 | tf_op jit(solution)/shard_map/ppermute | solution.py:300
  92.8 1.4 %copy-start = (bf16[960,768]{1,0:T(8,128)(2,1)S(1)}, bf16[960,768]{1,0:T(8,128)(2,1)}, u32[]{:S(2)}) copy-start(bf16[960,768]{1,0:T(8,128)(2,1)} %join.1.mine_ref) | copy-start | bytes 4423684
  94.2 27.5 %copy-start.2 = (bf16[512,768]{1,0:T(8,128)(2,1)S(1)}, bf16[512,768]{1,0:T(8,128)(2,1)}, u32[]{:S(2)}) copy-start(bf16[512,768]{1,0:T(8,128)(2,1)} %x_ref.1) | copy-start | bytes 2359300
  94.2 27.5 %copy-start.9 = (s32[512]{0:T(512)S(1)}, s32[512]{0:T(512)}, u32[]{:S(2)}) copy-start(s32[512]{0:T(512)} %param.22) | copy-start | bytes 6148
  94.3 27.5 %copy-start.10 = (s32[512]{0:T(512)S(1)}, s32[512]{0:T(512)}, u32[]{:S(2)}) copy-start(s32[512]{0:T(512)} %param.23) | copy-start | bytes 6148
  95.0 24.9 %all-to-all-start.4 = ((f32[16,8,128]{2,1,0:T(8,128)}), f32[16,8,128]{2,1,0:T(8,128)S(1)}, u32[]{:S(2)}, u32[]{:S(2)}) async-start(f32[16,8,128]{2,1,0:T(8,128)} %bitcast.12), calls=%async_computation.4 | async-start | bytes 131072 | tf_op jit(solution)/shard_map/all_to_all | solution.py:336
  122.0 0.6 copy-start.11

commit v3 on v0

--- a/solution.py
+++ b/solution.py
@@ -1,7 +1,266 @@
+import functools
+
 import jax
 import jax.numpy as jnp
 from jax import lax
+from jax.experimental import pallas as pl
+from jax.experimental.pallas import tpu as pltpu
 from jax.sharding import PartitionSpec as P
+
+OWNERS = 16
+CHIPS = 8
+HOMES = (2, 3, 4, 5)
+HOME_ROUNDS = (0, 1, 6, 7)
+OUTER_ROUNDS = (2, 3, 4, 5)
+BLOCK = 160
+CAP = 156
+META = 16
+HELD = CHIPS * BLOCK
+VMEM_LIMIT = 48 * 1024 * 1024
+NT = (((1,), (1,)), ((), ()))
+
+
+def is_home(chip):
+    return (chip >= HOMES[0]) & (chip <= HOMES[-1])
+
+
+def pack_kernel(x_ref, cluster_ref, rank_ref, *outs):
+    slot_ref = outs[len(HOMES)]
+    chip = lax.axis_index("owner") // 2
+    values = x_ref[...].astype(jnp.float32)
+    unit = (values * lax.rsqrt(jnp.sum(values * values, axis=1, keepdims=True) + 1e-06)).astype(
+        jnp.bfloat16
+    )
+    rows, width = unit.shape
+    cluster = cluster_ref[...]
+    rank = rank_ref[...]
+    home = jnp.where(
+        cluster < OWNERS // 2,
+        3,
+        jnp.where(cluster < OWNERS, 4, jnp.where(cluster == OWNERS, 2, 5)),
+    )
+    number = lax.broadcasted_iota(jnp.int32, (8, rows), 0)
+    member = number + HOMES[0] == home
+    upper = (
+        lax.broadcasted_iota(jnp.int32, (rows, rows), 0)
+        < lax.broadcasted_iota(jnp.int32, (rows, rows), 1)
+    ).astype(jnp.float32).astype(jnp.bfloat16)
+    before = jnp.dot(
+        member.astype(jnp.float32).astype(jnp.bfloat16), upper, preferred_element_type=jnp.float32
+    )
+    slot = jnp.where(member, before.astype(jnp.int32), -1)
+    slot_ref[...] = slot
+    over = (jnp.max(slot) >= CAP).astype(jnp.float32)
+    line = lax.broadcasted_iota(jnp.int32, (META, rows), 0)
+    first = META - (BLOCK - CAP)
+    meta = jnp.where(
+        line == first,
+        cluster + 1,
+        jnp.where(line == first + 1, rank >> 6, jnp.where(line == first + 2, rank & 63, 0)),
+    )
+    meta = meta.astype(jnp.float32).astype(jnp.bfloat16)
+    place = lax.broadcasted_iota(jnp.int32, (256, rows), 0)
+    for n in range(len(HOMES)):
+        k = jnp.where(is_home(chip), HOME_ROUNDS[n], OUTER_ROUNDS[n])
+        mine = slot_ref[pl.ds((chip ^ k) - HOMES[0], 1), :]
+        hot = ((place == mine) & (place < CAP)).astype(jnp.float32).astype(jnp.bfloat16)
+        block = jnp.dot(hot[:BLOCK], unit, preferred_element_type=jnp.float32)
+        outs[n][...] = block.astype(jnp.bfloat16)
+        tail = lax.dot_general(meta, hot, NT, preferred_element_type=jnp.float32)
+        row = lax.broadcasted_iota(jnp.int32, (META, 256), 0)
+        tail = jnp.where(row == META - 1, over, tail)
+        tail = jnp.where(row >= first, tail, block[BLOCK - META :, :256])
+        outs[n][BLOCK - META :, :256] = tail.astype(jnp.bfloat16)
+
+
+def fill_codes(keys, codes):
+    eye = (
+        lax.broadcasted_iota(jnp.int32, (BLOCK, 256), 0)
+        == lax.broadcasted_iota(jnp.int32, (BLOCK, 256), 1)
+    ).astype(jnp.float32).astype(jnp.bfloat16)
+    lane = lax.broadcasted_iota(jnp.int32, (1, META), 1)
+    first = META - (BLOCK - CAP)
+    scale = jnp.where(
+        lane == first, 4096.0, jnp.where(lane == first + 1, 64.0, jnp.where(lane == first + 2, 1.0, 0.0))
+    )
+    over = jnp.zeros((1, 128), jnp.float32)
+    for n in range(CHIPS):
+        meta = keys[(n + 1) * BLOCK - META : (n + 1) * BLOCK, :256]
+        over = jnp.maximum(over, meta[META - 1 :, :128].astype(jnp.float32))
+        columns = lax.dot_general(eye, meta, NT, preferred_element_type=jnp.float32)
+        code = jnp.sum(columns * scale, axis=1, keepdims=True)
+        codes[n * BLOCK : (n + 1) * BLOCK] = jnp.broadcast_to(code, (BLOCK, 128))
+    return over
+
+
+def best_of(keys, codes, query, top):
+    size = query.shape[0]
+    step = HELD // 2
+    base = jnp.floor(top * (1.0 / 4096.0)) * 4096.0
+    best = jnp.full((8, size), -1.0, jnp.float32)
+    for start in range(0, HELD, step):
+        score = lax.dot_general(
+            keys[start : start + step], query, NT, preferred_element_type=jnp.float32
+        )
+        code = jnp.concatenate([codes[start : start + step]] * (size // 128), axis=1)
+        score = jnp.where((code >= base) & (code < top), score, -1.0)
+        best = jnp.maximum(best, jnp.max(score.reshape(step // 8, 8, size), axis=0))
+    return best
+
+
+def join_kernel(*refs):
+    blocks, out_ref, sems = refs[:-2], refs[-2], refs[-1]
+    copies = [
+        pltpu.make_async_copy(ref, out_ref.at[pl.ds(n * BLOCK, BLOCK)], sems.at[n])
+        for n, ref in enumerate(blocks)
+    ]
+    for copy in copies:
+        copy.start()
+    for copy in copies:
+        copy.wait()
+
+
+def own_kernel(mine_ref, best_ref, top_ref, over_ref, codes):
+    @pl.when(is_home(lax.axis_index("owner") // 2))
+    def _():
+        over_ref[...] = jnp.broadcast_to(fill_codes(mine_ref, codes), over_ref.shape)
+        for at in range(0, HELD, 256):
+            top = jnp.transpose(codes[at : at + 256])[:8]
+            top_ref[:, at : at + 256] = top
+            best_ref[:, at : at + 256] = best_of(
+                mine_ref, codes, mine_ref[at : at + 256], top[:1]
+            )
+
+
+def other_kernel(mine_ref, other_ref, best_ref, top_ref, over_ref, out_ref, codes):
+    me = lax.axis_index("owner")
+    chip = me // 2
+    core = me % 2
+
+    @pl.when(is_home(chip))
+    def _():
+        over = jnp.max(jnp.maximum(fill_codes(other_ref, codes), over_ref[:1]))
+        found = [
+            jnp.maximum(
+                best_ref[:, at : at + 256],
+                best_of(other_ref, codes, mine_ref[at : at + 256], top_ref[:1, at : at + 256]),
+            )
+            for at in range(0, HELD, 256)
+        ]
+        found = jnp.max(jnp.concatenate(found, axis=1), axis=0, keepdims=True)
+        found = jnp.broadcast_to(found, (8, HELD))
+        lane = lax.broadcasted_iota(jnp.int32, (1, 128), 1)
+        for k in range(CHIPS):
+            start = k * BLOCK
+            base = min(start // 128 * 128, HELD - 256)
+            size = min(384, HELD - base)
+            part = found[:, base : base + size]
+            if start > base:
+                part = pltpu.roll(part, size - (start - base), 1)
+            row = 8 * (2 * (chip ^ k) + core)
+            out_ref[pl.ds(row, 1), :] = part[:1, :128]
+            out_ref[pl.ds(row + 1, 1), :] = jnp.where(lane >= CAP - 128, over, part[:1, 128:256])
+
+
+def unpack_kernel(back_ref, slot_ref, best_ref, over_ref):
+    core = lax.axis_index("owner") % 2
+    rows = slot_ref.shape[1]
+    place = lax.broadcasted_iota(jnp.int32, (128, rows), 0)
+    row = lax.broadcasted_iota(jnp.int32, (8, 128), 0)
+    total = jnp.zeros((8, rows), jnp.float32)
+    over = jnp.zeros((8, 128), jnp.float32)
+    for n, home in enumerate(HOMES):
+        part = back_ref[pl.ds(pl.multiple_of(8 * (2 * home + core), 8), 8), :]
+        over = jnp.maximum(over, part)
+        for half in range(2):
+            value = part[half : half + 1]
+            high = value.astype(jnp.bfloat16).astype(jnp.float32)
+            middle = (value - high).astype(jnp.bfloat16).astype(jnp.float32)
+            low = value - high - middle
+            split = jnp.where(row == 0, high, jnp.where(row == 1, middle, jnp.where(row == 2, low, 0.0)))
+            hot = (place + 128 * half == slot_ref[n : n + 1]) & (place + 128 * half < BLOCK)
+            total = total + jnp.dot(
+                split.astype(jnp.bfloat16),
+                hot.astype(jnp.float32).astype(jnp.bfloat16),
+                preferred_element_type=jnp.float32,
+            )
+    best_ref[...] = jnp.sum(total, axis=0, keepdims=True)
+    over_ref[0, 0] = (over[1, BLOCK - 1 - 128] > 0.0).astype(jnp.int32)
+
+
+def meet(embeds, clusters, ranks):
+    rows, width = embeds.shape
+    vmem = pl.BlockSpec(memory_space=pltpu.VMEM)
+    params = pltpu.CompilerParams(vmem_limit_bytes=VMEM_LIMIT)
+    *sent, slot = pl.pallas_call(
+        pack_kernel,
+        out_shape=[jax.ShapeDtypeStruct((BLOCK, width), jnp.bfloat16)] * len(HOMES)
+        + [jax.ShapeDtypeStruct((8, rows), jnp.int32)],
+        in_specs=[vmem] * 3,
+        out_specs=[vmem] * (len(HOMES) + 1),
+        compiler_params=params,
+        name="pack",
+    )(embeds, clusters.reshape(1, rows), ranks.reshape(1, rows))
+    blocks = {0: sent[0]}
+    for k in range(1, CHIPS):
+        route = [
+            (2 * s + c, 2 * (s ^ k) + c) for s in range(CHIPS) if s ^ k in HOMES for c in range(2)
+        ]
+        rounds = HOME_ROUNDS if k in HOME_ROUNDS else OUTER_ROUNDS
+        blocks[k] = lax.ppermute(sent[rounds.index(k)], "owner", route)
+    swap = [(2 * h + c, 2 * h + 1 - c) for h in HOMES for c in range(2)]
+    anywhere = pl.BlockSpec(memory_space=pl.ANY)
+
+    line = jax.ShapeDtypeStruct((8, HELD), jnp.float32)
+    codes = [pltpu.VMEM((HELD, 128), jnp.float32)]
+    cost = pl.CostEstimate(
+        flops=2 * HELD * HELD * width, bytes_accessed=2 * HELD * width, transcendentals=0
+    )
+    mine = pl.pallas_call(
+        join_kernel,
+        out_shape=jax.ShapeDtypeStruct((HELD, width), jnp.bfloat16),
+        in_specs=[anywhere] * CHIPS,
+        out_specs=vmem,
+        scratch_shapes=[pltpu.SemaphoreType.DMA((CHIPS,))],
+        compiler_params=params,
+        name="join",
+    )(*[blocks[k] for k in range(CHIPS)])
+    other = lax.ppermute(mine, "owner", swap)
+    best, top, over = pl.pallas_call(
+        own_kernel,
+        out_shape=[line, line, jax.ShapeDtypeStruct((8, 128), jnp.float32)],
+        in_specs=[vmem],
+        out_specs=[vmem] * 3,
+        scratch_shapes=codes,
+        compiler_params=params,
+        cost_estimate=cost,
+        name="own",
+    )(mine)
+    found = pl.pallas_call(
+        other_kernel,
+        out_shape=jax.ShapeDtypeStruct((8 * OWNERS, 128), jnp.float32),
+        in_specs=[vmem] * 5,
+        out_specs=vmem,
+        scratch_shapes=codes,
+        compiler_params=params,
+        cost_estimate=cost,
+        name="other",
+    )(mine, other, best, top, over)
+    back = lax.all_to_all(
+        found.reshape(OWNERS, 8, 128), "owner", split_axis=0, concat_axis=0, tiled=True
+    )
+    best, over = pl.pallas_call(
+        unpack_kernel,
+        out_shape=[
+            jax.ShapeDtypeStruct((1, rows), jnp.float32),
+            jax.ShapeDtypeStruct((1, 1), jnp.int32),
+        ],
+        in_specs=[vmem] * 2,
+        out_specs=[vmem, pl.BlockSpec(memory_space=pltpu.SMEM)],
+        compiler_params=params,
+        name="unpack",
+    )(back.reshape(8 * OWNERS, 128), slot)
+    return best.reshape(rows), over[0, 0] > 0
 
 
 def as_sent(array):
@@ -53,12 +312,12 @@
     return lax.fori_loop(0, query_total // query_size, query_block, best)
 
 
-def local(embeds, clusters, ranks):
+def route_rows(embeds, clusters, ranks):
     count = lax.axis_size("owner")
     rows, width = embeds.shape
     slots = max(2, 2 * rows // count)
     total = count * slots
-    large_cap = total // 2
+    large_cap = total
     values = embeds.astype(jnp.float32)
     unit = (values * lax.rsqrt(jnp.sum(values * values, axis=1, keepdims=True) + 1e-06)).astype(
         jnp.bfloat16
@@ -115,6 +374,14 @@
     return returned.reshape(total)[place]
 
 
+def local(embeds, clusters, ranks):
+    if lax.axis_size("owner") != OWNERS:
+        return route_rows(embeds, clusters, ranks)
+    best, over = meet(embeds, clusters, ranks)
+    return lax.cond(over, lambda *args: route_rows(*args[:3]), lambda *args: args[3],
+                    embeds, clusters, ranks, best)
+
+
 def solution(mesh):
     return jax.shard_map(
         local,

time: 225 us -> 62.7 us (0.28)
  waiting for transfers between devices: 121 us -> 18.9 us
  local copies, waits for them, and re-layouts: 35.1 us -> 0.59 us
  matrix products: 15.4 us -> 0 us
  other arithmetic: 14.9 us -> 0 us
  Pallas kernels: 0 us -> 6.16 us
    all_to_all x4 -> x1, waiting for transfers between devices: 61.8 us -> 6.9 us  [meet(): lax.all_to_all(found.reshape(OWNERS, 8, 128), 'owner', split_axis=0, conc...]
    ppermute x9 -> x8, waiting for transfers between devices: 58.8 us -> 12 us  [the longest x7 12 us: meet(): blocks[k] = lax.ppermute(sent[rounds.index(k)], 'owner', route)]
    scatter x5 -> x0, local copies, waits for them, and re-layouts: 19.3 us -> none  [the longest x1 5.31 us: local(): jnp.zeros((large_cap, width), jnp.bfloat16).at[large_place]]
    dot_general x11 -> x0, matrix products: 15.4 us -> none  [key_block(): jnp.einsum('qd,kd->qk', query_unit, key_unit, preferred_element_type=jnp....]
    gather x2 -> x0, local copies, waits for them, and re-layouts: 10.3 us -> none  [the longest x1 6.87 us: local(): picked = large_best[jnp.clip(large_position, 0, large_cap - 1)]]
    all_to_all x4 -> x1, starting transfers between devices: 25 us -> 17.8 us  [meet(): lax.all_to_all(found.reshape(OWNERS, 8, 128), 'owner', split_axis=0, conc...]
    pallas_call x0 -> x5, Pallas kernels: none -> 6.16 us  [the longest x1 2.6 us: meet(): pl.pallas_call(join_kernel, out_shape=jax.ShapeDtypeStruct((HELD, width),...]
    ppermute x9 -> x8, starting transfers between devices: 12.6 us -> 17.9 us  [the longest x7 17.1 us: meet(): blocks[k] = lax.ppermute(sent[rounds.index(k)], 'owner', route)]
  transfers between devices with their start and end apart: 13 -> 9, of which waited for: 8 -> 4; matrix products, arithmetic and copies ran while one was open for 15% -> 0% of each run, Pallas kernels for 0% -> 0%
where the time goes in v3:
time: 62.7 us; the launch traced here: 62.4 us
  starting transfers between devices  35.7 us (57%)
  waiting for transfers between devices  18.9 us (30%)
  Pallas kernels  6.16 us (10%)
  between operations  0.84 us (1%)
    all_to_all x1, starting transfers between devices, meet(): lax.all_to_all(found.reshape(OWNERS, 8, 128), 'owner', split_axis=0, conc...  17.8 us
    ppermute x7, starting transfers between devices, meet(): blocks[k] = lax.ppermute(sent[rounds.index(k)], 'owner', route)  17.1 us
    ppermute x7, waiting for transfers between devices, meet(): blocks[k] = lax.ppermute(sent[rounds.index(k)], 'owner', route)  12 us
    all_to_all x1, waiting for transfers between devices, meet(): lax.all_to_all(found.reshape(OWNERS, 8, 128), 'owner', split_axis=0, conc...  6.9 us
    pallas_call x1, Pallas kernels, meet(): pl.pallas_call(join_kernel, out_shape=jax.ShapeDtypeStruct((HELD, width),...  2.6 us
    pallas_call x1, Pallas kernels, meet(): pl.pallas_call(pack_kernel, out_shape=[jax.ShapeDtypeStruct((BLOCK, width...  2.22 us
  transfers between devices with their start and end apart: 9, of which 4 were waited for; matrix products, arithmetic and copies ran while one was open for 0% of the time, Pallas kernels for 0%

profile of v3, /device:TPU:0, one launch (start us, length us, event | category | flops | bytes accessed | tf_op | source)
XLA Modules:
  0.0 62.4 jit_solution(17509020071524848377)
XLA Ops:
  0.0 2.2 %pack.1 = (bf16[160,768]{1,0:T(8,128)(2,1)S(1)}, bf16[160,768]{1,0:T(8,128)(2,1)S(1)}, bf16[160,768]{1,0:T(8,128)(2,1)S(1)}, bf16[160,768]{1,0:T(8,128)(2,1)S(1)}, s32[8,512]{1,0:T(8,128)S(1)}) custom-call(bf16[512,768]{1,0:T(8,128)(2,1)} %x_ref.1, s32[1,512]{1,0:T(1,128)} %bitcast.58, s32[1,512]{1,0:T(1,128)} %bitcast.59), custom_call_target="tpu_custom_call" | custom-call | tf_op jit(solution)/shard_map/pack/pallas_call | solution.py:195
  2.2 0.7 %collective-permute-start.9 = (bf16[160,768]{1,0:T(8,128)(2,1)S(1)}, bf16[160,768]{1,0:T(8,128)(2,1)S(1)}, u32[]{:S(2)}, u32[]{:S(2)}) collective-permute-start(bf16[160,768]{1,0:T(8,128)(2,1)S(1)} %get-tuple-element.1178), channel_id=1, source_target_pairs={{4,6},{5,7},{6,4},{7,5},{8,10},{9,11},{10,8},{11,9},{20,22},{21,23... | collective-permute-start | bytes 737288 | tf_op jit(solution)/shard_map/ppermute | solution.py:210
  2.9 7.7 %collective-permute-start.10 = (bf16[160,768]{1,0:T(8,128)(2,1)S(1)}, bf16[160,768]{1,0:T(8,128)(2,1)S(1)}, u32[]{:S(2)}, u32[]{:S(2)}) collective-permute-start(bf16[160,768]{1,0:T(8,128)(2,1)S(1)} %get-tuple-element.1177.refs_0_), channel_id=1, source_target_pairs={{0,4},{1,5},{2,6},{3,7},{12,8},{13,9},{14,10},{15,11},{16,20},{17,... | collective-permute-start | bytes 737288 | tf_op jit(solution)/shard_map/ppermute | solution.py:210
  10.6 1.3 %collective-permute-start.11 = (bf16[160,768]{1,0:T(8,128)(2,1)S(1)}, bf16[160,768]{1,0:T(8,128)(2,1)S(1)}, u32[]{:S(2)}, u32[]{:S(2)}) collective-permute-start(bf16[160,768]{1,0:T(8,128)(2,1)S(1)} %get-tuple-element.1178), channel_id=1, source_target_pairs={{0,6},{1,7},{2,4},{3,5},{12,10},{13,11},{14,8},{15,9},{16,22},{17,... | collective-permute-start | bytes 737288 | tf_op jit(solution)/shard_map/ppermute | solution.py:210
  11.9 2.3 %collective-permute-start.12 = (bf16[160,768]{1,0:T(8,128)(2,1)S(1)}, bf16[160,768]{1,0:T(8,128)(2,1)S(1)}, u32[]{:S(2)}, u32[]{:S(2)}) collective-permute-start(bf16[160,768]{1,0:T(8,128)(2,1)S(1)} %get-tuple-element.1179), channel_id=1, source_target_pairs={{0,8},{1,9},{2,10},{3,11},{12,4},{13,5},{14,6},{15,7},{16,24},{17,... | collective-permute-start | bytes 737288 | tf_op jit(solution)/shard_map/ppermute | solution.py:210
  14.2 0.7 %collective-permute-start.14 = (bf16[160,768]{1,0:T(8,128)(2,1)S(1)}, bf16[160,768]{1,0:T(8,128)(2,1)S(1)}, u32[]{:S(2)}, u32[]{:S(2)}) collective-permute-start(bf16[160,768]{1,0:T(8,128)(2,1)S(1)} %get-tuple-element.1179), channel_id=1, source_target_pairs={{4,8},{5,9},{6,10},{7,11},{8,4},{9,5},{10,6},{11,7},{20,24},{21,25... | collective-permute-start | bytes 737288 | tf_op jit(solution)/shard_map/ppermute | solution.py:210
  14.9 0.0 collective-permute-done.9.refs_1_
  14.9 3.8 %collective-permute-start.13 = (bf16[160,768]{1,0:T(8,128)(2,1)S(1)}, bf16[160,768]{1,0:T(8,128)(2,1)S(1)}, u32[]{:S(2)}, u32[]{:S(2)}) collective-permute-start(bf16[160,768]{1,0:T(8,128)(2,1)S(1)} %get-tuple-element.1180), channel_id=1, source_target_pairs={{0,10},{1,11},{2,8},{3,9},{12,6},{13,7},{14,4},{15,5},{16,26},{17,... | collective-permute-start | bytes 737288 | tf_op jit(solution)/shard_map/ppermute | solution.py:210
  18.7 0.0 collective-permute-done.10.refs_2_
  18.7 0.7 %collective-permute-start.15 = (bf16[160,768]{1,0:T(8,128)(2,1)S(1)}, bf16[160,768]{1,0:T(8,128)(2,1)S(1)}, u32[]{:S(2)}, u32[]{:S(2)}) collective-permute-start(bf16[160,768]{1,0:T(8,128)(2,1)S(1)} %get-tuple-element.1180), channel_id=1, source_target_pairs={{4,10},{5,11},{6,8},{7,9},{8,6},{9,7},{10,4},{11,5},{20,26},{21,27... | collective-permute-start | bytes 737288 | tf_op jit(solution)/shard_map/ppermute | solution.py:210
  19.4 2.8 %collective-permute-done.11.refs_3_ = bf16[160,768]{1,0:T(8,128)(2,1)S(1)} collective-permute-done((bf16[160,768]{1,0:T(8,128)(2,1)S(1)}, bf16[160,768]{1,0:T(8,128)(2,1)S(1)}, u32[]{:S(2)}, u32[]{:S(2)}) %collective-permute-start.11) | collective-permute-done | bytes 245792 | tf_op jit(solution)/shard_map/ppermute | solution.py:210
  22.2 5.3 %collective-permute-done.12.refs_4_ = bf16[160,768]{1,0:T(8,128)(2,1)S(1)} collective-permute-done((bf16[160,768]{1,0:T(8,128)(2,1)S(1)}, bf16[160,768]{1,0:T(8,128)(2,1)S(1)}, u32[]{:S(2)}, u32[]{:S(2)}) %collective-permute-start.12) | collective-permute-done | bytes 245792 | tf_op jit(solution)/shard_map/ppermute | solution.py:210
  27.6 3.8 %collective-permute-done.13.refs_5_ = bf16[160,768]{1,0:T(8,128)(2,1)S(1)} collective-permute-done((bf16[160,768]{1,0:T(8,128)(2,1)S(1)}, bf16[160,768]{1,0:T(8,128)(2,1)S(1)}, u32[]{:S(2)}, u32[]{:S(2)}) %collective-permute-start.13) | collective-permute-done | bytes 245792 | tf_op jit(solution)/shard_map/ppermute | solution.py:210
  31.4 0.0 collective-permute-done.14.refs_6_
  31.4 0.0 collective-permute-done.15.refs_7_
  31.4 2.6 %join.1.mine_ref = bf16[1280,768]{1,0:T(8,128)(2,1)S(1)} custom-call(bf16[160,768]{1,0:T(8,128)(2,1)S(1)} %get-tuple-element.1177.refs_0_, bf16[160,768]{1,0:T(8,128)(2,1)S(1)} %collective-permute-done.9.refs_1_, bf16[160,768]{1,0:T(8,128)(2,1)S(1)} %collective-permute-done.10.refs_2_, bf16[160,768]{1,0:T(8,128)(2,1)S(1)} %collective-permute-done.11.refs_3_, ...), custom_call_target="tpu_custom_call" | custom-call | tf_op jit(solution)/shard_map/join/pallas_call | solution.py:219
  34.0 0.8 %collective-permute-start.16 = (bf16[1280,768]{1,0:T(8,128)(2,1)S(1)}, bf16[1280,768]{1,0:T(8,128)(2,1)S(1)}, u32[]{:S(2)}, u32[]{:S(2)}) collective-permute-start(bf16[1280,768]{1,0:T(8,128)(2,1)S(1)} %join.1.mine_ref), channel_id=1, source_target_pairs={{4,5},{5,4},{6,7},{7,6},{8,9},{9,8},{10,11},{11,10},{20,21},{21,20... | collective-permute-start | bytes 5898248 | tf_op jit(solution)/shard_map/ppermute | solution.py:228
  34.8 0.0 collective-permute-done.16.other_ref
  34.8 0.0 copy-start
  34.8 0.0 copy-start.2
  34.8 0.0 copy-start.3
  34.9 0.6 %other.1 = f32[128,128]{1,0:T(8,128)} custom-call(bf16[1280,768]{1,0:T(8,128)(2,1)S(1)} %join.1.mine_ref, bf16[1280,768]{1,0:T(8,128)(2,1)S(1)} %collective-permute-done.16.other_ref, f32[8,1280]{1,0:T(8,128)S(1)} %get-tuple-element.1181.best_ref, f32[8,1280]{1,0:T(8,128)S(1)} %get-tuple-element.1182.top_ref, f32[8,128]{1,0:T(8,128)S(1)} %get-tuple-element.1183.over_ref), custom_call_target="tpu_custom_call" | custom-call | flops 2516582400 | bytes 1966080 | tf_op jit(solution)/shard_map/other/pallas_call | solution.py:239
  35.5 17.8 %all-to-all-start.4 = ((f32[16,8,128]{2,1,0:T(8,128)}), f32[16,8,128]{2,1,0:T(8,128)S(1)}, u32[]{:S(2)}, u32[]{:S(2)}) async-start(f32[16,8,128]{2,1,0:T(8,128)} %bitcast.12), calls=%async_computation.4 | async-start | bytes 131072 | tf_op jit(solution)/shard_map/all_to_all | solution.py:249
  53.3 6.9 %all-to-all-done.4 = f32[16,8,128]{2,1,0:T(8,128)S(1)} async-done(((f32[16,8,128]{2,1,0:T(8,128)}), f32[16,8,128]{2,1,0:T(8,128)S(1)}, u32[]{:S(2)}, u32[]{:S(2)}) %all-to-all-start.4) | async-done | bytes 65568 | tf_op jit(solution)/shard_map/all_to_all | solution.py:249
  60.2 0.7 %unpack.1 = (f32[1,512]{1,0:T(1,128)S(1)}, s32[1,1]{1,0:T(1,128)}) custom-call(f32[128,128]{1,0:T(8,128)S(1)} %bitcast.55, s32[8,512]{1,0:T(8,128)S(1)} %get-tuple-element.1184.slot_ref), custom_call_target="tpu_custom_call" | custom-call | tf_op jit(solution)/shard_map/unpack/pallas_call | solution.py:252
  61.5 0.0 copy-done
  61.5 0.0 copy-done.2
  61.5 0.0 copy-done.3
  61.6 0.2 conditional.1
  61.8 0.0 copy-start.4
  61.8 0.6 copy-done.4
  (1 shorter events, 0.0 us)
Async XLA Ops:
  2.2 12.7 %collective-permute-start.9 = (bf16[160,768]{1,0:T(8,128)(2,1)S(1)}, bf16[160,768]{1,0:T(8,128)(2,1)S(1)}, u32[]{:S(2)}, u32[]{:S(2)}) collective-permute-start(bf16[160,768]{1,0:T(8,128)(2,1)S(1)} %get-tuple-element.1178), channel_id=1, source_target_pairs={{4,6},{5,7},{6,4},{7,5},{8,10},{9,11},{10,8},{11,9},{20,22},{21,23... | collective-permute-start | bytes 737288 | tf_op jit(solution)/shard_map/ppermute | solution.py:210
  2.9 15.8 %collective-permute-start.10 = (bf16[160,768]{1,0:T(8,128)(2,1)S(1)}, bf16[160,768]{1,0:T(8,128)(2,1)S(1)}, u32[]{:S(2)}, u32[]{:S(2)}) collective-permute-start(bf16[160,768]{1,0:T(8,128)(2,1)S(1)} %get-tuple-element.1177.refs_0_), channel_id=1, source_target_pairs={{0,4},{1,5},{2,6},{3,7},{12,8},{13,9},{14,10},{15,11},{16,20},{17,... | collective-permute-start | bytes 737288 | tf_op jit(solution)/shard_map/ppermute | solution.py:210
  10.6 11.6 %collective-permute-start.11 = (bf16[160,768]{1,0:T(8,128)(2,1)S(1)}, bf16[160,768]{1,0:T(8,128)(2,1)S(1)}, u32[]{:S(2)}, u32[]{:S(2)}) collective-permute-start(bf16[160,768]{1,0:T(8,128)(2,1)S(1)} %get-tuple-element.1178), channel_id=1, source_target_pairs={{0,6},{1,7},{2,4},{3,5},{12,10},{13,11},{14,8},{15,9},{16,22},{17,... | collective-permute-start | bytes 737288 | tf_op jit(solution)/shard_map/ppermute | solution.py:210
  11.9 15.6 %collective-permute-start.12 = (bf16[160,768]{1,0:T(8,128)(2,1)S(1)}, bf16[160,768]{1,0:T(8,128)(2,1)S(1)}, u32[]{:S(2)}, u32[]{:S(2)}) collective-permute-start(bf16[160,768]{1,0:T(8,128)(2,1)S(1)} %get-tuple-element.1179), channel_id=1, source_target_pairs={{0,8},{1,9},{2,10},{3,11},{12,4},{13,5},{14,6},{15,7},{16,24},{17,... | collective-permute-start | bytes 737288 | tf_op jit(solution)/shard_map/ppermute | solution.py:210
  14.2 17.1 %collective-permute-start.14 = (bf16[160,768]{1,0:T(8,128)(2,1)S(1)}, bf16[160,768]{1,0:T(8,128)(2,1)S(1)}, u32[]{:S(2)}, u32[]{:S(2)}) collective-permute-start(bf16[160,768]{1,0:T(8,128)(2,1)S(1)} %get-tuple-element.1179), channel_id=1, source_target_pairs={{4,8},{5,9},{6,10},{7,11},{8,4},{9,5},{10,6},{11,7},{20,24},{21,25... | collective-permute-start | bytes 737288 | tf_op jit(solution)/shard_map/ppermute | solution.py:210
  14.9 16.4 %collective-permute-start.13 = (bf16[160,768]{1,0:T(8,128)(2,1)S(1)}, bf16[160,768]{1,0:T(8,128)(2,1)S(1)}, u32[]{:S(2)}, u32[]{:S(2)}) collective-permute-start(bf16[160,768]{1,0:T(8,128)(2,1)S(1)} %get-tuple-element.1180), channel_id=1, source_target_pairs={{0,10},{1,11},{2,8},{3,9},{12,6},{13,7},{14,4},{15,5},{16,26},{17,... | collective-permute-start | bytes 737288 | tf_op jit(solution)/shard_map/ppermute | solution.py:210
  18.7 12.6 %collective-permute-start.15 = (bf16[160,768]{1,0:T(8,128)(2,1)S(1)}, bf16[160,768]{1,0:T(8,128)(2,1)S(1)}, u32[]{:S(2)}, u32[]{:S(2)}) collective-permute-start(bf16[160,768]{1,0:T(8,128)(2,1)S(1)} %get-tuple-element.1180), channel_id=1, source_target_pairs={{4,10},{5,11},{6,8},{7,9},{8,6},{9,7},{10,4},{11,5},{20,26},{21,27... | collective-permute-start | bytes 737288 | tf_op jit(solution)/shard_map/ppermute | solution.py:210
  34.0 0.8 %collective-permute-start.16 = (bf16[1280,768]{1,0:T(8,128)(2,1)S(1)}, bf16[1280,768]{1,0:T(8,128)(2,1)S(1)}, u32[]{:S(2)}, u32[]{:S(2)}) collective-permute-start(bf16[1280,768]{1,0:T(8,128)(2,1)S(1)} %join.1.mine_ref), channel_id=1, source_target_pairs={{4,5},{5,4},{6,7},{7,6},{8,9},{9,8},{10,11},{11,10},{20,21},{21,20... | collective-permute-start | bytes 5898248 | tf_op jit(solution)/shard_map/ppermute | solution.py:228
  34.8 26.7 %copy-start = (bf16[512,768]{1,0:T(8,128)(2,1)S(1)}, bf16[512,768]{1,0:T(8,128)(2,1)}, u32[]{:S(2)}) copy-start(bf16[512,768]{1,0:T(8,128)(2,1)} %x_ref.1) | copy-start | bytes 2359300
  34.8 26.7 %copy-start.2 = (s32[512]{0:T(512)S(1)}, s32[512]{0:T(512)}, u32[]{:S(2)}) copy-start(s32[512]{0:T(512)} %param.22) | copy-start | bytes 6148
  34.8 26.7 %copy-start.3 = (s32[512]{0:T(512)S(1)}, s32[512]{0:T(512)}, u32[]{:S(2)}) copy-start(s32[512]{0:T(512)} %param.23) | copy-start | bytes 6148
  35.5 24.7 %all-to-all-start.4 = ((f32[16,8,128]{2,1,0:T(8,128)}), f32[16,8,128]{2,1,0:T(8,128)S(1)}, u32[]{:S(2)}, u32[]{:S(2)}) async-start(f32[16,8,128]{2,1,0:T(8,128)} %bitcast.12), calls=%async_computation.4 | async-start | bytes 131072 | tf_op jit(solution)/shard_map/all_to_all | solution.py:249
  61.8 0.6 copy-start.4

commit v4 on v3

--- a/solution.py
+++ b/solution.py
@@ -12,6 +12,7 @@
 HOMES = (2, 3, 4, 5)
 HOME_ROUNDS = (0, 1, 6, 7)
 OUTER_ROUNDS = (2, 3, 4, 5)
+ORDER = (0,1,3,6,7,4,5,2)
 BLOCK = 160
 CAP = 156
 META = 16
@@ -109,15 +110,9 @@
 
 
 def join_kernel(*refs):
-    blocks, out_ref, sems = refs[:-2], refs[-2], refs[-1]
-    copies = [
-        pltpu.make_async_copy(ref, out_ref.at[pl.ds(n * BLOCK, BLOCK)], sems.at[n])
-        for n, ref in enumerate(blocks)
-    ]
-    for copy in copies:
-        copy.start()
-    for copy in copies:
-        copy.wait()
+    blocks, out_ref = refs[:-1], refs[-1]
+    for n, ref in enumerate(blocks):
+        out_ref[n * BLOCK : (n + 1) * BLOCK] = ref[...]
 
 
 def own_kernel(mine_ref, best_ref, top_ref, over_ref, codes):
@@ -150,8 +145,8 @@
         found = jnp.max(jnp.concatenate(found, axis=1), axis=0, keepdims=True)
         found = jnp.broadcast_to(found, (8, HELD))
         lane = lax.broadcasted_iota(jnp.int32, (1, 128), 1)
-        for k in range(CHIPS):
-            start = k * BLOCK
+        for n, k in enumerate(ORDER):
+            start = n * BLOCK
             base = min(start // 128 * 128, HELD - 256)
             size = min(384, HELD - base)
             part = found[:, base : base + size]
@@ -209,7 +204,6 @@
         rounds = HOME_ROUNDS if k in HOME_ROUNDS else OUTER_ROUNDS
         blocks[k] = lax.ppermute(sent[rounds.index(k)], "owner", route)
     swap = [(2 * h + c, 2 * h + 1 - c) for h in HOMES for c in range(2)]
-    anywhere = pl.BlockSpec(memory_space=pl.ANY)
 
     line = jax.ShapeDtypeStruct((8, HELD), jnp.float32)
     codes = [pltpu.VMEM((HELD, 128), jnp.float32)]
@@ -219,12 +213,11 @@
     mine = pl.pallas_call(
         join_kernel,
         out_shape=jax.ShapeDtypeStruct((HELD, width), jnp.bfloat16),
-        in_specs=[anywhere] * CHIPS,
+        in_specs=[vmem] * CHIPS,
         out_specs=vmem,
-        scratch_shapes=[pltpu.SemaphoreType.DMA((CHIPS,))],
         compiler_params=params,
         name="join",
-    )(*[blocks[k] for k in range(CHIPS)])
+    )(*[blocks[k] for k in ORDER])
     other = lax.ppermute(mine, "owner", swap)
     best, top, over = pl.pallas_call(
         own_kernel,

time: 62.7 us -> 57.7 us (0.920)
  waiting for transfers between devices: 18.9 us -> 15.2 us
  Pallas kernels: 6.16 us -> 3.68 us
  starting transfers between devices: 35.7 us -> 36.8 us
    ppermute x7, starting transfers between devices: 17.1 us -> 23.1 us  [meet(): blocks[k] = lax.ppermute(sent[rounds.index(k)], 'owner', route)]
    all_to_all x1, starting transfers between devices: 17.8 us -> 12.9 us  [meet(): lax.all_to_all(found.reshape(OWNERS, 8, 128), 'owner', split_axis=0, conc...]
    ppermute x7, waiting for transfers between devices: 12 us -> 8.27 us  [meet(): blocks[k] = lax.ppermute(sent[rounds.index(k)], 'owner', route)]
    pallas_call x1, Pallas kernels: 2.6 us -> 0.13 us  [meet(): pl.pallas_call(join_kernel, out_shape=jax.ShapeDtypeStruct((HELD, width),...]
  transfers between devices with their start and end apart: 9 -> 9, of which waited for: 4 -> 3; matrix products, arithmetic and copies ran while one was open for 0% -> 0% of each run, Pallas kernels for 0% -> 0%
where the time goes in v4:
time: 57.7 us; the launch traced here: 57.3 us
  starting transfers between devices  36.8 us (64%)
  waiting for transfers between devices  15.2 us (26%)
  Pallas kernels  3.68 us (6%)
  between operations  0.86 us (1%)
  local copies, waits for them, and re-layouts  0.59 us (1%)
    ppermute x7, starting transfers between devices, meet(): blocks[k] = lax.ppermute(sent[rounds.index(k)], 'owner', route)  23.1 us
    all_to_all x1, starting transfers between devices, meet(): lax.all_to_all(found.reshape(OWNERS, 8, 128), 'owner', split_axis=0, conc...  12.9 us
    ppermute x7, waiting for transfers between devices, meet(): blocks[k] = lax.ppermute(sent[rounds.index(k)], 'owner', route)  8.27 us
    all_to_all x1, waiting for transfers between devices, meet(): lax.all_to_all(found.reshape(OWNERS, 8, 128), 'owner', split_axis=0, conc...  6.9 us
    pallas_call x1, Pallas kernels, meet(): pl.pallas_call(pack_kernel, out_shape=[jax.ShapeDtypeStruct((BLOCK, width...  2.22 us
  transfers between devices with their start and end apart: 9, of which 3 were waited for; matrix products, arithmetic and copies ran while one was open for 0% of the time, Pallas kernels for 0%

profile of v4, /device:TPU:0, one launch (start us, length us, event | category | flops | bytes accessed | tf_op | source)
XLA Modules:
  0.0 57.3 jit_solution(2025541437670273605)
XLA Ops:
  0.0 2.2 %pack.1 = (bf16[160,768]{1,0:T(8,128)(2,1)S(1)}, bf16[160,768]{1,0:T(8,128)(2,1)S(1)}, bf16[160,768]{1,0:T(8,128)(2,1)S(1)}, bf16[160,768]{1,0:T(8,128)(2,1)S(1)}, s32[8,512]{1,0:T(8,128)S(1)}) custom-call(bf16[512,768]{1,0:T(8,128)(2,1)} %x_ref.1, s32[1,512]{1,0:T(1,128)} %bitcast.58, s32[1,512]{1,0:T(1,128)} %bitcast.59), custom_call_target="tpu_custom_call" | custom-call | tf_op jit(solution)/shard_map/pack/pallas_call | solution.py:190
  2.2 0.7 %collective-permute-start.9 = (bf16[160,768]{1,0:T(8,128)(2,1)S(1)}, bf16[160,768]{1,0:T(8,128)(2,1)S(1)}, u32[]{:S(2)}, u32[]{:S(2)}) collective-permute-start(bf16[160,768]{1,0:T(8,128)(2,1)S(1)} %get-tuple-element.1178), channel_id=1, source_target_pairs={{4,6},{5,7},{6,4},{7,5},{8,10},{9,11},{10,8},{11,9},{20,22},{21,23... | collective-permute-start | bytes 737288 | tf_op jit(solution)/shard_map/ppermute | solution.py:205
  2.9 7.6 %collective-permute-start.10 = (bf16[160,768]{1,0:T(8,128)(2,1)S(1)}, bf16[160,768]{1,0:T(8,128)(2,1)S(1)}, u32[]{:S(2)}, u32[]{:S(2)}) collective-permute-start(bf16[160,768]{1,0:T(8,128)(2,1)S(1)} %get-tuple-element.1178), channel_id=1, source_target_pairs={{0,6},{1,7},{2,4},{3,5},{12,10},{13,11},{14,8},{15,9},{16,22},{17,... | collective-permute-start | bytes 737288 | tf_op jit(solution)/shard_map/ppermute | solution.py:205
  10.6 0.7 %collective-permute-start.11 = (bf16[160,768]{1,0:T(8,128)(2,1)S(1)}, bf16[160,768]{1,0:T(8,128)(2,1)S(1)}, u32[]{:S(2)}, u32[]{:S(2)}) collective-permute-start(bf16[160,768]{1,0:T(8,128)(2,1)S(1)} %get-tuple-element.1179), channel_id=1, source_target_pairs={{4,8},{5,9},{6,10},{7,11},{8,4},{9,5},{10,6},{11,7},{20,24},{21,25... | collective-permute-start | bytes 737288 | tf_op jit(solution)/shard_map/ppermute | solution.py:205
  11.2 4.0 %collective-permute-start.13 = (bf16[160,768]{1,0:T(8,128)(2,1)S(1)}, bf16[160,768]{1,0:T(8,128)(2,1)S(1)}, u32[]{:S(2)}, u32[]{:S(2)}) collective-permute-start(bf16[160,768]{1,0:T(8,128)(2,1)S(1)} %get-tuple-element.1179), channel_id=1, source_target_pairs={{0,8},{1,9},{2,10},{3,11},{12,4},{13,5},{14,6},{15,7},{16,24},{17,... | collective-permute-start | bytes 737288 | tf_op jit(solution)/shard_map/ppermute | solution.py:205
  15.3 0.7 %collective-permute-start.12 = (bf16[160,768]{1,0:T(8,128)(2,1)S(1)}, bf16[160,768]{1,0:T(8,128)(2,1)S(1)}, u32[]{:S(2)}, u32[]{:S(2)}) collective-permute-start(bf16[160,768]{1,0:T(8,128)(2,1)S(1)} %get-tuple-element.1180), channel_id=1, source_target_pairs={{4,10},{5,11},{6,8},{7,9},{8,6},{9,7},{10,4},{11,5},{20,26},{21,27... | collective-permute-start | bytes 737288 | tf_op jit(solution)/shard_map/ppermute | solution.py:205
  16.0 0.0 collective-permute-done.9.refs_1_
  16.0 8.1 %collective-permute-start.14 = (bf16[160,768]{1,0:T(8,128)(2,1)S(1)}, bf16[160,768]{1,0:T(8,128)(2,1)S(1)}, u32[]{:S(2)}, u32[]{:S(2)}) collective-permute-start(bf16[160,768]{1,0:T(8,128)(2,1)S(1)} %get-tuple-element.1180), channel_id=1, source_target_pairs={{0,10},{1,11},{2,8},{3,9},{12,6},{13,7},{14,4},{15,5},{16,26},{17,... | collective-permute-start | bytes 737288 | tf_op jit(solution)/shard_map/ppermute | solution.py:205
  24.1 0.0 collective-permute-done.10.refs_2_
  24.1 1.3 %collective-permute-start.15 = (bf16[160,768]{1,0:T(8,128)(2,1)S(1)}, bf16[160,768]{1,0:T(8,128)(2,1)S(1)}, u32[]{:S(2)}, u32[]{:S(2)}) collective-permute-start(bf16[160,768]{1,0:T(8,128)(2,1)S(1)} %get-tuple-element.1177.refs_0_), channel_id=1, source_target_pairs={{0,4},{1,5},{2,6},{3,7},{12,8},{13,9},{14,10},{15,11},{16,20},{17,... | collective-permute-start | bytes 737288 | tf_op jit(solution)/shard_map/ppermute | solution.py:205
  25.4 0.0 collective-permute-done.11.refs_3_
  25.4 0.0 collective-permute-done.12.refs_4_
  25.4 0.0 collective-permute-done.13.refs_5_
  25.4 5.0 %collective-permute-done.14.refs_6_ = bf16[160,768]{1,0:T(8,128)(2,1)S(1)} collective-permute-done((bf16[160,768]{1,0:T(8,128)(2,1)S(1)}, bf16[160,768]{1,0:T(8,128)(2,1)S(1)}, u32[]{:S(2)}, u32[]{:S(2)}) %collective-permute-start.14) | collective-permute-done | bytes 245792 | tf_op jit(solution)/shard_map/ppermute | solution.py:205
  30.4 3.2 %collective-permute-done.15.refs_7_ = bf16[160,768]{1,0:T(8,128)(2,1)S(1)} collective-permute-done((bf16[160,768]{1,0:T(8,128)(2,1)S(1)}, bf16[160,768]{1,0:T(8,128)(2,1)S(1)}, u32[]{:S(2)}, u32[]{:S(2)}) %collective-permute-start.15) | collective-permute-done | bytes 245792 | tf_op jit(solution)/shard_map/ppermute | solution.py:205
  33.7 0.1 join.1.mine_ref
  33.8 0.8 %collective-permute-start.16 = (bf16[1280,768]{1,0:T(8,128)(2,1)S(1)}, bf16[1280,768]{1,0:T(8,128)(2,1)S(1)}, u32[]{:S(2)}, u32[]{:S(2)}) collective-permute-start(bf16[1280,768]{1,0:T(8,128)(2,1)S(1)} %join.1.mine_ref), channel_id=1, source_target_pairs={{4,5},{5,4},{6,7},{7,6},{8,9},{9,8},{10,11},{11,10},{20,21},{21,20... | collective-permute-start | bytes 5898248 | tf_op jit(solution)/shard_map/ppermute | solution.py:221
  34.6 0.0 collective-permute-done.16.other_ref
  34.6 0.0 copy-start
  34.6 0.0 copy-start.2
  34.7 0.0 copy-start.3
  34.7 0.6 %other.1 = f32[128,128]{1,0:T(8,128)} custom-call(bf16[1280,768]{1,0:T(8,128)(2,1)S(1)} %join.1.mine_ref, bf16[1280,768]{1,0:T(8,128)(2,1)S(1)} %collective-permute-done.16.other_ref, f32[8,1280]{1,0:T(8,128)S(1)} %get-tuple-element.1181.best_ref, f32[8,1280]{1,0:T(8,128)S(1)} %get-tuple-element.1182.top_ref, f32[8,128]{1,0:T(8,128)S(1)} %get-tuple-element.1183.over_ref), custom_call_target="tpu_custom_call" | custom-call | flops 2516582400 | bytes 1966080 | tf_op jit(solution)/shard_map/other/pallas_call | solution.py:232
  35.3 12.9 %all-to-all-start.4 = ((f32[16,8,128]{2,1,0:T(8,128)}), f32[16,8,128]{2,1,0:T(8,128)S(1)}, u32[]{:S(2)}, u32[]{:S(2)}) async-start(f32[16,8,128]{2,1,0:T(8,128)} %bitcast.12), calls=%async_computation.4 | async-start | bytes 131072 | tf_op jit(solution)/shard_map/all_to_all | solution.py:242
  48.2 6.9 %all-to-all-done.4 = f32[16,8,128]{2,1,0:T(8,128)S(1)} async-done(((f32[16,8,128]{2,1,0:T(8,128)}), f32[16,8,128]{2,1,0:T(8,128)S(1)}, u32[]{:S(2)}, u32[]{:S(2)}) %all-to-all-start.4) | async-done | bytes 65568 | tf_op jit(solution)/shard_map/all_to_all | solution.py:242
  55.1 0.7 %unpack.1 = (f32[1,512]{1,0:T(1,128)S(1)}, s32[1,1]{1,0:T(1,128)}) custom-call(f32[128,128]{1,0:T(8,128)S(1)} %bitcast.55, s32[8,512]{1,0:T(8,128)S(1)} %get-tuple-element.1184.slot_ref), custom_call_target="tpu_custom_call" | custom-call | tf_op jit(solution)/shard_map/unpack/pallas_call | solution.py:245
  56.5 0.0 copy-done
  56.5 0.0 copy-done.2
  56.5 0.0 copy-done.3
  56.5 0.2 conditional.1
  56.7 0.0 copy-start.4
  56.8 0.6 copy-done.4
  (1 shorter events, 0.0 us)
Async XLA Ops:
  2.2 13.8 %collective-permute-start.9 = (bf16[160,768]{1,0:T(8,128)(2,1)S(1)}, bf16[160,768]{1,0:T(8,128)(2,1)S(1)}, u32[]{:S(2)}, u32[]{:S(2)}) collective-permute-start(bf16[160,768]{1,0:T(8,128)(2,1)S(1)} %get-tuple-element.1178), channel_id=1, source_target_pairs={{4,6},{5,7},{6,4},{7,5},{8,10},{9,11},{10,8},{11,9},{20,22},{21,23... | collective-permute-start | bytes 737288 | tf_op jit(solution)/shard_map/ppermute | solution.py:205
  2.9 21.1 %collective-permute-start.10 = (bf16[160,768]{1,0:T(8,128)(2,1)S(1)}, bf16[160,768]{1,0:T(8,128)(2,1)S(1)}, u32[]{:S(2)}, u32[]{:S(2)}) collective-permute-start(bf16[160,768]{1,0:T(8,128)(2,1)S(1)} %get-tuple-element.1178), channel_id=1, source_target_pairs={{0,6},{1,7},{2,4},{3,5},{12,10},{13,11},{14,8},{15,9},{16,22},{17,... | collective-permute-start | bytes 737288 | tf_op jit(solution)/shard_map/ppermute | solution.py:205
  10.6 14.8 %collective-permute-start.11 = (bf16[160,768]{1,0:T(8,128)(2,1)S(1)}, bf16[160,768]{1,0:T(8,128)(2,1)S(1)}, u32[]{:S(2)}, u32[]{:S(2)}) collective-permute-start(bf16[160,768]{1,0:T(8,128)(2,1)S(1)} %get-tuple-element.1179), channel_id=1, source_target_pairs={{4,8},{5,9},{6,10},{7,11},{8,4},{9,5},{10,6},{11,7},{20,24},{21,25... | collective-permute-start | bytes 737288 | tf_op jit(solution)/shard_map/ppermute | solution.py:205
  11.2 14.2 %collective-permute-start.13 = (bf16[160,768]{1,0:T(8,128)(2,1)S(1)}, bf16[160,768]{1,0:T(8,128)(2,1)S(1)}, u32[]{:S(2)}, u32[]{:S(2)}) collective-permute-start(bf16[160,768]{1,0:T(8,128)(2,1)S(1)} %get-tuple-element.1179), channel_id=1, source_target_pairs={{0,8},{1,9},{2,10},{3,11},{12,4},{13,5},{14,6},{15,7},{16,24},{17,... | collective-permute-start | bytes 737288 | tf_op jit(solution)/shard_map/ppermute | solution.py:205
  15.3 10.1 %collective-permute-start.12 = (bf16[160,768]{1,0:T(8,128)(2,1)S(1)}, bf16[160,768]{1,0:T(8,128)(2,1)S(1)}, u32[]{:S(2)}, u32[]{:S(2)}) collective-permute-start(bf16[160,768]{1,0:T(8,128)(2,1)S(1)} %get-tuple-element.1180), channel_id=1, source_target_pairs={{4,10},{5,11},{6,8},{7,9},{8,6},{9,7},{10,4},{11,5},{20,26},{21,27... | collective-permute-start | bytes 737288 | tf_op jit(solution)/shard_map/ppermute | solution.py:205
  16.0 14.4 %collective-permute-start.14 = (bf16[160,768]{1,0:T(8,128)(2,1)S(1)}, bf16[160,768]{1,0:T(8,128)(2,1)S(1)}, u32[]{:S(2)}, u32[]{:S(2)}) collective-permute-start(bf16[160,768]{1,0:T(8,128)(2,1)S(1)} %get-tuple-element.1180), channel_id=1, source_target_pairs={{0,10},{1,11},{2,8},{3,9},{12,6},{13,7},{14,4},{15,5},{16,26},{17,... | collective-permute-start | bytes 737288 | tf_op jit(solution)/shard_map/ppermute | solution.py:205
  24.1 9.6 %collective-permute-start.15 = (bf16[160,768]{1,0:T(8,128)(2,1)S(1)}, bf16[160,768]{1,0:T(8,128)(2,1)S(1)}, u32[]{:S(2)}, u32[]{:S(2)}) collective-permute-start(bf16[160,768]{1,0:T(8,128)(2,1)S(1)} %get-tuple-element.1177.refs_0_), channel_id=1, source_target_pairs={{0,4},{1,5},{2,6},{3,7},{12,8},{13,9},{14,10},{15,11},{16,20},{17,... | collective-permute-start | bytes 737288 | tf_op jit(solution)/shard_map/ppermute | solution.py:205
  33.8 0.8 %collective-permute-start.16 = (bf16[1280,768]{1,0:T(8,128)(2,1)S(1)}, bf16[1280,768]{1,0:T(8,128)(2,1)S(1)}, u32[]{:S(2)}, u32[]{:S(2)}) collective-permute-start(bf16[1280,768]{1,0:T(8,128)(2,1)S(1)} %join.1.mine_ref), channel_id=1, source_target_pairs={{4,5},{5,4},{6,7},{7,6},{8,9},{9,8},{10,11},{11,10},{20,21},{21,20... | collective-permute-start | bytes 5898248 | tf_op jit(solution)/shard_map/ppermute | solution.py:221
  34.6 21.9 %copy-start = (bf16[512,768]{1,0:T(8,128)(2,1)S(1)}, bf16[512,768]{1,0:T(8,128)(2,1)}, u32[]{:S(2)}) copy-start(bf16[512,768]{1,0:T(8,128)(2,1)} %x_ref.1) | copy-start | bytes 2359300
  34.6 21.9 %copy-start.2 = (s32[512]{0:T(512)S(1)}, s32[512]{0:T(512)}, u32[]{:S(2)}) copy-start(s32[512]{0:T(512)} %param.22) | copy-start | bytes 6148
  34.7 21.8 %copy-start.3 = (s32[512]{0:T(512)S(1)}, s32[512]{0:T(512)}, u32[]{:S(2)}) copy-start(s32[512]{0:T(512)} %param.23) | copy-start | bytes 6148
  35.3 19.8 %all-to-all-start.4 = ((f32[16,8,128]{2,1,0:T(8,128)}), f32[16,8,128]{2,1,0:T(8,128)S(1)}, u32[]{:S(2)}, u32[]{:S(2)}) async-start(f32[16,8,128]{2,1,0:T(8,128)} %bitcast.12), calls=%async_computation.4 | async-start | bytes 131072 | tf_op jit(solution)/shard_map/all_to_all | solution.py:242
  56.7 0.6 %copy-start.4 = (f32[512]{0:T(512)}, f32[512]{0:T(512)S(1)}, u32[]{:S(2)}) copy-start(f32[512]{0:T(512)S(1)} %get-tuple-element.2167) | copy-start | bytes 6148

commit v5 on v4

--- a/solution.py
+++ b/solution.py
@@ -10,9 +10,9 @@
 OWNERS = 16
 CHIPS = 8
 HOMES = (2, 3, 4, 5)
-HOME_ROUNDS = (0, 1, 6, 7)
-OUTER_ROUNDS = (2, 3, 4, 5)
-ORDER = (0,1,3,6,7,4,5,2)
+HOME_ROUNDS = (0, 6)
+OUTER_ROUNDS = (2, 4)
+ORDER = (2,6,4,0)
 BLOCK = 160
 CAP = 156
 META = 16
@@ -25,9 +25,10 @@
     return (chip >= HOMES[0]) & (chip <= HOMES[-1])
 
 
-def pack_kernel(x_ref, cluster_ref, rank_ref, *outs):
-    slot_ref = outs[len(HOMES)]
-    chip = lax.axis_index("owner") // 2
+def pack_kernel(x_ref, cluster_ref, rank_ref, keep_ref, give_ref, slot_ref):
+    me = lax.axis_index("owner")
+    chip = me // 2
+    core = me % 2
     values = x_ref[...].astype(jnp.float32)
     unit = (values * lax.rsqrt(jnp.sum(values * values, axis=1, keepdims=True) + 1e-06)).astype(
         jnp.bfloat16
@@ -61,17 +62,18 @@
     )
     meta = meta.astype(jnp.float32).astype(jnp.bfloat16)
     place = lax.broadcasted_iota(jnp.int32, (256, rows), 0)
-    for n in range(len(HOMES)):
-        k = jnp.where(is_home(chip), HOME_ROUNDS[n], OUTER_ROUNDS[n])
+    for n in range(4):
+        out_ref, to_core, at = (keep_ref, give_ref)[n // 2], core ^ (n // 2), n % 2 * BLOCK
+        k = jnp.where(is_home(chip), HOME_ROUNDS[n % 2], OUTER_ROUNDS[n % 2]) | to_core
         mine = slot_ref[pl.ds((chip ^ k) - HOMES[0], 1), :]
         hot = ((place == mine) & (place < CAP)).astype(jnp.float32).astype(jnp.bfloat16)
         block = jnp.dot(hot[:BLOCK], unit, preferred_element_type=jnp.float32)
-        outs[n][...] = block.astype(jnp.bfloat16)
+        out_ref[at : at + BLOCK] = block.astype(jnp.bfloat16)
         tail = lax.dot_general(meta, hot, NT, preferred_element_type=jnp.float32)
         row = lax.broadcasted_iota(jnp.int32, (META, 256), 0)
         tail = jnp.where(row == META - 1, over, tail)
         tail = jnp.where(row >= first, tail, block[BLOCK - META :, :256])
-        outs[n][BLOCK - META :, :256] = tail.astype(jnp.bfloat16)
+        out_ref[at + BLOCK - META : at + BLOCK, :256] = tail.astype(jnp.bfloat16)
 
 
 def fill_codes(keys, codes):
@@ -109,10 +111,22 @@
     return best
 
 
-def join_kernel(*refs):
+def pair_kernel(keep_ref, got_ref, first_ref, second_ref):
+    first_ref[:BLOCK] = keep_ref[:BLOCK]
+    first_ref[BLOCK:] = got_ref[:BLOCK]
+    second_ref[:BLOCK] = keep_ref[BLOCK:]
+    second_ref[BLOCK:] = got_ref[BLOCK:]
+
+
+def join_kernel(mine_ref, *refs):
     blocks, out_ref = refs[:-1], refs[-1]
     for n, ref in enumerate(blocks):
-        out_ref[n * BLOCK : (n + 1) * BLOCK] = ref[...]
+        out_ref[n * 2 * BLOCK : (n + 1) * 2 * BLOCK] = ref[...]
+
+    @pl.when(lax.axis_index("owner") % 2 == 0)
+    def _():
+        at = ORDER.index(0) * 2 * BLOCK
+        out_ref[at : at + 2 * BLOCK] = mine_ref[...]
 
 
 def own_kernel(mine_ref, best_ref, top_ref, over_ref, codes):
@@ -145,27 +159,30 @@
         found = jnp.max(jnp.concatenate(found, axis=1), axis=0, keepdims=True)
         found = jnp.broadcast_to(found, (8, HELD))
         lane = lax.broadcasted_iota(jnp.int32, (1, 128), 1)
-        for n, k in enumerate(ORDER):
+        for n in range(CHIPS):
             start = n * BLOCK
+            to_chip = chip ^ (ORDER[n // 2] | core)
+            to_core = core ^ (n % 2)
             base = min(start // 128 * 128, HELD - 256)
             size = min(384, HELD - base)
             part = found[:, base : base + size]
             if start > base:
                 part = pltpu.roll(part, size - (start - base), 1)
-            row = 8 * (2 * (chip ^ k) + core)
+            row = 8 * (2 * to_chip + to_core)
             out_ref[pl.ds(row, 1), :] = part[:1, :128]
             out_ref[pl.ds(row + 1, 1), :] = jnp.where(lane >= CAP - 128, over, part[:1, 128:256])
 
 
 def unpack_kernel(back_ref, slot_ref, best_ref, over_ref):
-    core = lax.axis_index("owner") % 2
+    chip = lax.axis_index("owner") // 2
     rows = slot_ref.shape[1]
     place = lax.broadcasted_iota(jnp.int32, (128, rows), 0)
     row = lax.broadcasted_iota(jnp.int32, (8, 128), 0)
     total = jnp.zeros((8, rows), jnp.float32)
     over = jnp.zeros((8, 128), jnp.float32)
     for n, home in enumerate(HOMES):
-        part = back_ref[pl.ds(pl.multiple_of(8 * (2 * home + core), 8), 8), :]
+        held = 2 * home + ((chip ^ home) & 1)
+        part = back_ref[pl.ds(pl.multiple_of(8 * held, 8), 8), :]
         over = jnp.maximum(over, part)
         for half in range(2):
             value = part[half : half + 1]
@@ -187,24 +204,33 @@
     rows, width = embeds.shape
     vmem = pl.BlockSpec(memory_space=pltpu.VMEM)
     params = pltpu.CompilerParams(vmem_limit_bytes=VMEM_LIMIT)
-    *sent, slot = pl.pallas_call(
+    two_blocks = jax.ShapeDtypeStruct((2 * BLOCK, width), jnp.bfloat16)
+    keep, give, slot = pl.pallas_call(
         pack_kernel,
-        out_shape=[jax.ShapeDtypeStruct((BLOCK, width), jnp.bfloat16)] * len(HOMES)
-        + [jax.ShapeDtypeStruct((8, rows), jnp.int32)],
+        out_shape=[two_blocks, two_blocks, jax.ShapeDtypeStruct((8, rows), jnp.int32)],
         in_specs=[vmem] * 3,
-        out_specs=[vmem] * (len(HOMES) + 1),
+        out_specs=[vmem] * 3,
         compiler_params=params,
         name="pack",
     )(embeds, clusters.reshape(1, rows), ranks.reshape(1, rows))
-    blocks = {0: sent[0]}
-    for k in range(1, CHIPS):
-        route = [
-            (2 * s + c, 2 * (s ^ k) + c) for s in range(CHIPS) if s ^ k in HOMES for c in range(2)
-        ]
-        rounds = HOME_ROUNDS if k in HOME_ROUNDS else OUTER_ROUNDS
-        blocks[k] = lax.ppermute(sent[rounds.index(k)], "owner", route)
+    got = lax.ppermute(give, "owner", [(n, n ^ 1) for n in range(OWNERS)])
+    first, second = pl.pallas_call(
+        pair_kernel,
+        out_shape=[two_blocks] * 2,
+        in_specs=[vmem] * 2,
+        out_specs=[vmem] * 2,
+        compiler_params=params,
+        name="pair",
+    )(keep, got)
+
+    def carry(pair, k, cores=(0, 1)):
+        chips = [s for s in range(CHIPS) if (s in HOMES) == (k in HOME_ROUNDS)]
+        return lax.ppermute(
+            pair, "owner", [(2 * s + c, 2 * (s ^ (k | c)) + c) for s in chips for c in cores]
+        )
+
+    pairs = {6: carry(second, 6), 4: carry(second, 4), 2: carry(first, 2), 0: carry(first, 0, (1,))}
     swap = [(2 * h + c, 2 * h + 1 - c) for h in HOMES for c in range(2)]
-
     line = jax.ShapeDtypeStruct((8, HELD), jnp.float32)
     codes = [pltpu.VMEM((HELD, 128), jnp.float32)]
     cost = pl.CostEstimate(
@@ -213,11 +239,11 @@
     mine = pl.pallas_call(
         join_kernel,
         out_shape=jax.ShapeDtypeStruct((HELD, width), jnp.bfloat16),
-        in_specs=[vmem] * CHIPS,
+        in_specs=[vmem] * (1 + len(ORDER)),
         out_specs=vmem,
         compiler_params=params,
         name="join",
-    )(*[blocks[k] for k in ORDER])
+    )(first, *[pairs[k] for k in ORDER])
     other = lax.ppermute(mine, "owner", swap)
     best, top, over = pl.pallas_call(
         own_kernel,

time: 57.7 us -> 57 us (0.988)
  starting transfers between devices: 36.8 us -> 26.3 us
  waiting for transfers between devices: 15.2 us -> 25 us
    ppermute x7 -> x5, starting transfers between devices: 23.1 us -> 10.8 us  [the longest x4 10.2 us: carry(): lax.ppermute(pair, 'owner', [(2 * s + c, 2 * (s ^ (k | c)) + c) for s in...]
    ppermute x7 -> x5, waiting for transfers between devices: 8.27 us -> 18.1 us  [the longest x4 16.6 us: carry(): lax.ppermute(pair, 'owner', [(2 * s + c, 2 * (s ^ (k | c)) + c) for s in...]
    all_to_all x1, starting transfers between devices: 12.9 us -> 14.8 us  [meet(): lax.all_to_all(found.reshape(OWNERS, 8, 128), 'owner', split_axis=0, conc...]
    pallas_call x1 -> x2, Pallas kernels: 2.22 us -> 2.28 us  [the longest x1 2.22 us: meet(): pl.pallas_call(pack_kernel, out_shape=[two_blocks, two_blocks, jax.ShapeD...]
  transfers between devices with their start and end apart: 9 -> 7, of which waited for: 3 -> 4; matrix products, arithmetic and copies ran while one was open for 0% -> 0% of each run, Pallas kernels for 0% -> 0%
where the time goes in v5:
time: 57 us; the launch traced here: 56.7 us
  starting transfers between devices  26.3 us (46%)
  waiting for transfers between devices  25 us (44%)
  Pallas kernels  3.78 us (7%)
  between operations  0.8 us (1%)
  local copies, waits for them, and re-layouts  0.59 us (1%)
    ppermute x4, waiting for transfers between devices, carry(): lax.ppermute(pair, 'owner', [(2 * s + c, 2 * (s ^ (k | c)) + c) for s in...  16.6 us
    all_to_all x1, starting transfers between devices, meet(): lax.all_to_all(found.reshape(OWNERS, 8, 128), 'owner', split_axis=0, conc...  14.8 us
    ppermute x4, starting transfers between devices, carry(): lax.ppermute(pair, 'owner', [(2 * s + c, 2 * (s ^ (k | c)) + c) for s in...  10.2 us
    all_to_all x1, waiting for transfers between devices, meet(): lax.all_to_all(found.reshape(OWNERS, 8, 128), 'owner', split_axis=0, conc...  6.9 us
    pallas_call x1, Pallas kernels, meet(): pl.pallas_call(pack_kernel, out_shape=[two_blocks, two_blocks, jax.ShapeD...  2.22 us
    ppermute x1, waiting for transfers between devices, meet(): got = lax.ppermute(give, 'owner', [(n, n ^ 1) for n in range(OWNERS)])  1.49 us
  transfers between devices with their start and end apart: 7, of which 4 were waited for; matrix products, arithmetic and copies ran while one was open for 0% of the time, Pallas kernels for 0%

profile of v5, /device:TPU:0, one launch (start us, length us, event | category | flops | bytes accessed | tf_op | source)
XLA Modules:
  0.0 56.7 jit_solution(15793996954258571948)
XLA Ops:
  0.0 2.2 %pack.1 = (bf16[320,768]{1,0:T(8,128)(2,1)S(1)}, bf16[320,768]{1,0:T(8,128)(2,1)S(1)}, s32[8,512]{1,0:T(8,128)S(1)}) custom-call(bf16[512,768]{1,0:T(8,128)(2,1)} %x_ref.1, s32[1,512]{1,0:T(1,128)} %bitcast.58, s32[1,512]{1,0:T(1,128)} %bitcast.59), custom_call_target="tpu_custom_call" | custom-call | tf_op jit(solution)/shard_map/pack/pallas_call | solution.py:208
  2.2 0.5 collective-permute-start.9
  2.7 1.5 %collective-permute-done.9.got_ref = bf16[320,768]{1,0:T(8,128)(2,1)S(1)} collective-permute-done((bf16[320,768]{1,0:T(8,128)(2,1)S(1)}, bf16[320,768]{1,0:T(8,128)(2,1)S(1)}, u32[]{:S(2)}, u32[]{:S(2)}) %collective-permute-start.9) | collective-permute-done | bytes 491552 | tf_op jit(solution)/shard_map/ppermute | solution.py:216
  4.2 0.1 pair.1
  4.3 4.9 %collective-permute-start.10 = (bf16[320,768]{1,0:T(8,128)(2,1)S(1)}, bf16[320,768]{1,0:T(8,128)(2,1)S(1)}, u32[]{:S(2)}, u32[]{:S(2)}) collective-permute-start(bf16[320,768]{1,0:T(8,128)(2,1)S(1)} %get-tuple-element.1179.mine_ref), channel_id=1, source_target_pairs={{0,4},{1,7},{2,6},{3,5},{12,8},{13,11},{14,10},{15,9},{16,20},{17,... | collective-permute-start | bytes 1474568 | tf_op jit(solution)/shard_map/ppermute | solution.py:228
  9.2 0.7 %collective-permute-start.11 = (bf16[320,768]{1,0:T(8,128)(2,1)S(1)}, bf16[320,768]{1,0:T(8,128)(2,1)S(1)}, u32[]{:S(2)}, u32[]{:S(2)}) collective-permute-start(bf16[320,768]{1,0:T(8,128)(2,1)S(1)} %get-tuple-element.1180), channel_id=1, source_target_pairs={{4,8},{5,11},{6,10},{7,9},{8,4},{9,7},{10,6},{11,5},{20,24},{21,27... | collective-permute-start | bytes 1474568 | tf_op jit(solution)/shard_map/ppermute | solution.py:228
  9.9 4.0 %collective-permute-start.12 = (bf16[320,768]{1,0:T(8,128)(2,1)S(1)}, bf16[320,768]{1,0:T(8,128)(2,1)S(1)}, u32[]{:S(2)}, u32[]{:S(2)}) collective-permute-start(bf16[320,768]{1,0:T(8,128)(2,1)S(1)} %get-tuple-element.1180), channel_id=1, source_target_pairs={{0,8},{1,11},{2,10},{3,9},{12,4},{13,7},{14,6},{15,5},{16,24},{17,... | collective-permute-start | bytes 1474568 | tf_op jit(solution)/shard_map/ppermute | solution.py:228
  13.9 0.7 %collective-permute-start.13 = (bf16[320,768]{1,0:T(8,128)(2,1)S(1)}, bf16[320,768]{1,0:T(8,128)(2,1)S(1)}, u32[]{:S(2)}, u32[]{:S(2)}) collective-permute-start(bf16[320,768]{1,0:T(8,128)(2,1)S(1)} %get-tuple-element.1179.mine_ref), channel_id=1, source_target_pairs={{5,7},{7,5},{9,11},{11,9},{21,23},{23,21},{25,27},{27,25}} | collective-permute-start | bytes 1474568 | tf_op jit(solution)/shard_map/ppermute | solution.py:228
  14.6 6.1 %collective-permute-done.10.refs_0_ = bf16[320,768]{1,0:T(8,128)(2,1)S(1)} collective-permute-done((bf16[320,768]{1,0:T(8,128)(2,1)S(1)}, bf16[320,768]{1,0:T(8,128)(2,1)S(1)}, u32[]{:S(2)}, u32[]{:S(2)}) %collective-permute-start.10) | collective-permute-done | bytes 491552 | tf_op jit(solution)/shard_map/ppermute | solution.py:228
  20.6 0.0 collective-permute-done.11.refs_1_
  20.6 10.6 %collective-permute-done.12.refs_2_ = bf16[320,768]{1,0:T(8,128)(2,1)S(1)} collective-permute-done((bf16[320,768]{1,0:T(8,128)(2,1)S(1)}, bf16[320,768]{1,0:T(8,128)(2,1)S(1)}, u32[]{:S(2)}, u32[]{:S(2)}) %collective-permute-start.12) | collective-permute-done | bytes 491552 | tf_op jit(solution)/shard_map/ppermute | solution.py:228
  31.2 0.0 collective-permute-done.13.refs_3_
  31.2 0.2 join.1.mine_ref
  31.4 0.8 %collective-permute-start.14 = (bf16[1280,768]{1,0:T(8,128)(2,1)S(1)}, bf16[1280,768]{1,0:T(8,128)(2,1)S(1)}, u32[]{:S(2)}, u32[]{:S(2)}) collective-permute-start(bf16[1280,768]{1,0:T(8,128)(2,1)S(1)} %join.1.mine_ref), channel_id=1, source_target_pairs={{4,5},{5,4},{6,7},{7,6},{8,9},{9,8},{10,11},{11,10},{20,21},{21,20... | collective-permute-start | bytes 5898248 | tf_op jit(solution)/shard_map/ppermute | solution.py:247
  32.2 0.0 collective-permute-done.14.other_ref
  32.2 0.0 copy-start
  32.2 0.0 copy-start.2
  32.2 0.0 copy-start.3
  32.2 0.6 %other.1 = f32[128,128]{1,0:T(8,128)} custom-call(bf16[1280,768]{1,0:T(8,128)(2,1)S(1)} %join.1.mine_ref, bf16[1280,768]{1,0:T(8,128)(2,1)S(1)} %collective-permute-done.14.other_ref, f32[8,1280]{1,0:T(8,128)S(1)} %get-tuple-element.1181.best_ref, f32[8,1280]{1,0:T(8,128)S(1)} %get-tuple-element.1182.top_ref, f32[8,128]{1,0:T(8,128)S(1)} %get-tuple-element.1183.over_ref), custom_call_target="tpu_custom_call" | custom-call | flops 2516582400 | bytes 1966080 | tf_op jit(solution)/shard_map/other/pallas_call | solution.py:258
  32.9 14.8 %all-to-all-start.4 = ((f32[16,8,128]{2,1,0:T(8,128)}), f32[16,8,128]{2,1,0:T(8,128)S(1)}, u32[]{:S(2)}, u32[]{:S(2)}) async-start(f32[16,8,128]{2,1,0:T(8,128)} %bitcast.12), calls=%async_computation.4 | async-start | bytes 131072 | tf_op jit(solution)/shard_map/all_to_all | solution.py:268
  47.7 6.9 %all-to-all-done.4 = f32[16,8,128]{2,1,0:T(8,128)S(1)} async-done(((f32[16,8,128]{2,1,0:T(8,128)}), f32[16,8,128]{2,1,0:T(8,128)S(1)}, u32[]{:S(2)}, u32[]{:S(2)}) %all-to-all-start.4) | async-done | bytes 65568 | tf_op jit(solution)/shard_map/all_to_all | solution.py:268
  54.6 0.7 %unpack.1 = (f32[1,512]{1,0:T(1,128)S(1)}, s32[1,1]{1,0:T(1,128)}) custom-call(f32[128,128]{1,0:T(8,128)S(1)} %bitcast.55, s32[8,512]{1,0:T(8,128)S(1)} %get-tuple-element.1184.slot_ref), custom_call_target="tpu_custom_call" | custom-call | tf_op jit(solution)/shard_map/unpack/pallas_call | solution.py:271
  55.9 0.0 copy-done
  55.9 0.0 copy-done.2
  55.9 0.0 copy-done.3
  55.9 0.2 conditional.1
  56.1 0.0 copy-start.4
  56.2 0.6 %copy-done.4 = f32[512]{0:T(512)} copy-done((f32[512]{0:T(512)}, f32[512]{0:T(512)S(1)}, u32[]{:S(2)}) %copy-start.4) | copy-done | bytes 2072
  (1 shorter events, 0.0 us)
Async XLA Ops:
  2.2 2.0 %collective-permute-start.9 = (bf16[320,768]{1,0:T(8,128)(2,1)S(1)}, bf16[320,768]{1,0:T(8,128)(2,1)S(1)}, u32[]{:S(2)}, u32[]{:S(2)}) collective-permute-start(bf16[320,768]{1,0:T(8,128)(2,1)S(1)} %get-tuple-element.1178), channel_id=1, source_target_pairs={{0,1},{1,0},{2,3},{3,2},{4,5},{5,4},{6,7},{7,6},{8,9},{9,8},{10,11... | collective-permute-start | bytes 1474568 | tf_op jit(solution)/shard_map/ppermute | solution.py:216
  4.3 16.3 %collective-permute-start.10 = (bf16[320,768]{1,0:T(8,128)(2,1)S(1)}, bf16[320,768]{1,0:T(8,128)(2,1)S(1)}, u32[]{:S(2)}, u32[]{:S(2)}) collective-permute-start(bf16[320,768]{1,0:T(8,128)(2,1)S(1)} %get-tuple-element.1179.mine_ref), channel_id=1, source_target_pairs={{0,4},{1,7},{2,6},{3,5},{12,8},{13,11},{14,10},{15,9},{16,20},{17,... | collective-permute-start | bytes 1474568 | tf_op jit(solution)/shard_map/ppermute | solution.py:228
  9.2 11.4 %collective-permute-start.11 = (bf16[320,768]{1,0:T(8,128)(2,1)S(1)}, bf16[320,768]{1,0:T(8,128)(2,1)S(1)}, u32[]{:S(2)}, u32[]{:S(2)}) collective-permute-start(bf16[320,768]{1,0:T(8,128)(2,1)S(1)} %get-tuple-element.1180), channel_id=1, source_target_pairs={{4,8},{5,11},{6,10},{7,9},{8,4},{9,7},{10,6},{11,5},{20,24},{21,27... | collective-permute-start | bytes 1474568 | tf_op jit(solution)/shard_map/ppermute | solution.py:228
  9.9 21.3 %collective-permute-start.12 = (bf16[320,768]{1,0:T(8,128)(2,1)S(1)}, bf16[320,768]{1,0:T(8,128)(2,1)S(1)}, u32[]{:S(2)}, u32[]{:S(2)}) collective-permute-start(bf16[320,768]{1,0:T(8,128)(2,1)S(1)} %get-tuple-element.1180), channel_id=1, source_target_pairs={{0,8},{1,11},{2,10},{3,9},{12,4},{13,7},{14,6},{15,5},{16,24},{17,... | collective-permute-start | bytes 1474568 | tf_op jit(solution)/shard_map/ppermute | solution.py:228
  13.9 17.3 %collective-permute-start.13 = (bf16[320,768]{1,0:T(8,128)(2,1)S(1)}, bf16[320,768]{1,0:T(8,128)(2,1)S(1)}, u32[]{:S(2)}, u32[]{:S(2)}) collective-permute-start(bf16[320,768]{1,0:T(8,128)(2,1)S(1)} %get-tuple-element.1179.mine_ref), channel_id=1, source_target_pairs={{5,7},{7,5},{9,11},{11,9},{21,23},{23,21},{25,27},{27,25}} | collective-permute-start | bytes 1474568 | tf_op jit(solution)/shard_map/ppermute | solution.py:228
  31.4 0.8 %collective-permute-start.14 = (bf16[1280,768]{1,0:T(8,128)(2,1)S(1)}, bf16[1280,768]{1,0:T(8,128)(2,1)S(1)}, u32[]{:S(2)}, u32[]{:S(2)}) collective-permute-start(bf16[1280,768]{1,0:T(8,128)(2,1)S(1)} %join.1.mine_ref), channel_id=1, source_target_pairs={{4,5},{5,4},{6,7},{7,6},{8,9},{9,8},{10,11},{11,10},{20,21},{21,20... | collective-permute-start | bytes 5898248 | tf_op jit(solution)/shard_map/ppermute | solution.py:247
  32.2 23.7 %copy-start = (bf16[512,768]{1,0:T(8,128)(2,1)S(1)}, bf16[512,768]{1,0:T(8,128)(2,1)}, u32[]{:S(2)}) copy-start(bf16[512,768]{1,0:T(8,128)(2,1)} %x_ref.1) | copy-start | bytes 2359300
  32.2 23.7 %copy-start.2 = (s32[512]{0:T(512)S(1)}, s32[512]{0:T(512)}, u32[]{:S(2)}) copy-start(s32[512]{0:T(512)} %param.22) | copy-start | bytes 6148
  32.2 23.7 %copy-start.3 = (s32[512]{0:T(512)S(1)}, s32[512]{0:T(512)}, u32[]{:S(2)}) copy-start(s32[512]{0:T(512)} %param.23) | copy-start | bytes 6148
  32.9 21.7 %all-to-all-start.4 = ((f32[16,8,128]{2,1,0:T(8,128)}), f32[16,8,128]{2,1,0:T(8,128)S(1)}, u32[]{:S(2)}, u32[]{:S(2)}) async-start(f32[16,8,128]{2,1,0:T(8,128)} %bitcast.12), calls=%async_computation.4 | async-start | bytes 131072 | tf_op jit(solution)/shard_map/all_to_all | solution.py:268
  56.1 0.6 %copy-start.4 = (f32[512]{0:T(512)}, f32[512]{0:T(512)S(1)}, u32[]{:S(2)}) copy-start(f32[512]{0:T(512)S(1)} %get-tuple-element.2163) | copy-start | bytes 6148

commit v6 on v5

--- a/solution.py
+++ b/solution.py
@@ -25,7 +25,26 @@
     return (chip >= HOMES[0]) & (chip <= HOMES[-1])
 
 
-def pack_kernel(x_ref, cluster_ref, rank_ref, keep_ref, give_ref, slot_ref):
+def pack_rows(unit_ref, meta_ref, slot_ref, chip, to_core, out_ref):
+    rows = slot_ref.shape[1]
+    first = META - (BLOCK - CAP)
+    place = lax.broadcasted_iota(jnp.int32, (256, rows), 0)
+    over = (jnp.max(slot_ref[...]) >= CAP).astype(jnp.float32)
+    for n in range(2):
+        at = n * BLOCK
+        k = jnp.where(is_home(chip), HOME_ROUNDS[n], OUTER_ROUNDS[n]) | to_core
+        mine = slot_ref[pl.ds((chip ^ k) - HOMES[0], 1), :]
+        hot = ((place == mine) & (place < CAP)).astype(jnp.float32).astype(jnp.bfloat16)
+        block = jnp.dot(hot[:BLOCK], unit_ref[...], preferred_element_type=jnp.float32)
+        out_ref[at : at + BLOCK] = block.astype(jnp.bfloat16)
+        tail = lax.dot_general(meta_ref[...], hot, NT, preferred_element_type=jnp.float32)
+        row = lax.broadcasted_iota(jnp.int32, (META, 256), 0)
+        tail = jnp.where(row == META - 1, over, tail)
+        tail = jnp.where(row >= first, tail, block[BLOCK - META :, :256])
+        out_ref[at + BLOCK - META : at + BLOCK, :256] = tail.astype(jnp.bfloat16)
+
+
+def pack_kernel(x_ref, cluster_ref, rank_ref, give_ref, slot_ref, unit_ref, meta_ref):
     me = lax.axis_index("owner")
     chip = me // 2
     core = me % 2
@@ -52,7 +71,6 @@
     )
     slot = jnp.where(member, before.astype(jnp.int32), -1)
     slot_ref[...] = slot
-    over = (jnp.max(slot) >= CAP).astype(jnp.float32)
     line = lax.broadcasted_iota(jnp.int32, (META, rows), 0)
     first = META - (BLOCK - CAP)
     meta = jnp.where(
@@ -61,19 +79,14 @@
         jnp.where(line == first + 1, rank >> 6, jnp.where(line == first + 2, rank & 63, 0)),
     )
     meta = meta.astype(jnp.float32).astype(jnp.bfloat16)
-    place = lax.broadcasted_iota(jnp.int32, (256, rows), 0)
-    for n in range(4):
-        out_ref, to_core, at = (keep_ref, give_ref)[n // 2], core ^ (n // 2), n % 2 * BLOCK
-        k = jnp.where(is_home(chip), HOME_ROUNDS[n % 2], OUTER_ROUNDS[n % 2]) | to_core
-        mine = slot_ref[pl.ds((chip ^ k) - HOMES[0], 1), :]
-        hot = ((place == mine) & (place < CAP)).astype(jnp.float32).astype(jnp.bfloat16)
-        block = jnp.dot(hot[:BLOCK], unit, preferred_element_type=jnp.float32)
-        out_ref[at : at + BLOCK] = block.astype(jnp.bfloat16)
-        tail = lax.dot_general(meta, hot, NT, preferred_element_type=jnp.float32)
-        row = lax.broadcasted_iota(jnp.int32, (META, 256), 0)
-        tail = jnp.where(row == META - 1, over, tail)
-        tail = jnp.where(row >= first, tail, block[BLOCK - META :, :256])
-        out_ref[at + BLOCK - META : at + BLOCK, :256] = tail.astype(jnp.bfloat16)
+    unit_ref[...] = unit
+    meta_ref[...] = meta
+    pack_rows(unit_ref, meta_ref, slot_ref, chip, core ^ 1, give_ref)
+
+
+def keep_kernel(unit_ref, meta_ref, slot_ref, keep_ref):
+    me = lax.axis_index("owner")
+    pack_rows(unit_ref, meta_ref, slot_ref, me // 2, me % 2, keep_ref)
 
 
 def fill_codes(keys, codes):
@@ -205,15 +218,31 @@
     vmem = pl.BlockSpec(memory_space=pltpu.VMEM)
     params = pltpu.CompilerParams(vmem_limit_bytes=VMEM_LIMIT)
     two_blocks = jax.ShapeDtypeStruct((2 * BLOCK, width), jnp.bfloat16)
-    keep, give, slot = pl.pallas_call(
+    give, slot, unit, meta = pl.pallas_call(
         pack_kernel,
-        out_shape=[two_blocks, two_blocks, jax.ShapeDtypeStruct((8, rows), jnp.int32)],
+        out_shape=[
+            two_blocks,
+            jax.ShapeDtypeStruct((8, rows), jnp.int32),
+            jax.ShapeDtypeStruct((rows, width), jnp.bfloat16),
+            jax.ShapeDtypeStruct((META, rows), jnp.bfloat16),
+        ],
         in_specs=[vmem] * 3,
-        out_specs=[vmem] * 3,
+        out_specs=[vmem] * 4,
         compiler_params=params,
         name="pack",
     )(embeds, clusters.reshape(1, rows), ranks.reshape(1, rows))
     got = lax.ppermute(give, "owner", [(n, n ^ 1) for n in range(OWNERS)])
+    keep = pl.pallas_call(
+        keep_kernel,
+        out_shape=two_blocks,
+        in_specs=[vmem] * 3,
+        out_specs=vmem,
+        compiler_params=params,
+        cost_estimate=pl.CostEstimate(
+            flops=4 * BLOCK * rows * width, bytes_accessed=4 * rows * width, transcendentals=0
+        ),
+        name="keep",
+    )(unit, meta, slot)
     first, second = pl.pallas_call(
         pair_kernel,
         out_shape=[two_blocks] * 2,

time: 57 us -> 56.7 us (level)
    pallas_call x1 -> x2, Pallas kernels: 2.22 us -> 2.38 us  [the longest x1 1.88 us: meet(): pl.pallas_call(pack_kernel, out_shape=[two_blocks, jax.ShapeDtypeStruct((...]
  transfers between devices with their start and end apart: 7 -> 7, of which waited for: 4 -> 4; matrix products, arithmetic and copies ran while one was open for 0% -> 0% of each run, Pallas kernels for 0% -> 1%
where the time goes in v6:
time: 56.7 us; the launch traced here: 56.4 us
  starting transfers between devices  26.3 us (46%)
  waiting for transfers between devices  24.5 us (43%)
  Pallas kernels  3.94 us (7%)
  between operations  0.81 us (1%)
  local copies, waits for them, and re-layouts  0.59 us (1%)
    ppermute x4, waiting for transfers between devices, carry(): lax.ppermute(pair, 'owner', [(2 * s + c, 2 * (s ^ (k | c)) + c) for s in...  16.6 us
    all_to_all x1, starting transfers between devices, meet(): lax.all_to_all(found.reshape(OWNERS, 8, 128), 'owner', split_axis=0, conc...  14.8 us
    ppermute x4, starting transfers between devices, carry(): lax.ppermute(pair, 'owner', [(2 * s + c, 2 * (s ^ (k | c)) + c) for s in...  10.2 us
    all_to_all x1, waiting for transfers between devices, meet(): lax.all_to_all(found.reshape(OWNERS, 8, 128), 'owner', split_axis=0, conc...  6.9 us
    pallas_call x1, Pallas kernels, meet(): pl.pallas_call(pack_kernel, out_shape=[two_blocks, jax.ShapeDtypeStruct((...  1.88 us
  transfers between devices with their start and end apart: 7, of which 4 were waited for; matrix products, arithmetic and copies ran while one was open for 0% of the time, Pallas kernels for 1%

profile of v6, /device:TPU:0, one launch (start us, length us, event | category | flops | bytes accessed | tf_op | source)
XLA Modules:
  0.0 56.4 jit_solution(11766511754814476939)
XLA Ops:
  0.0 1.9 %pack.1 = (bf16[320,768]{1,0:T(8,128)(2,1)S(1)}, s32[8,512]{1,0:T(8,128)S(1)}, bf16[512,768]{1,0:T(8,128)(2,1)S(1)}, bf16[16,512]{1,0:T(8,128)(2,1)S(1)}) custom-call(bf16[512,768]{1,0:T(8,128)(2,1)} %x_ref.1, s32[1,512]{1,0:T(1,128)} %bitcast.58, s32[1,512]{1,0:T(1,128)} %bitcast.59), custom_call_target="tpu_custom_call" | custom-call | tf_op jit(solution)/shard_map/pack/pallas_call | solution.py:221
  1.9 0.5 collective-permute-start.9
  2.4 0.5 keep.1.keep_ref
  2.9 1.0 %collective-permute-done.9.got_ref = bf16[320,768]{1,0:T(8,128)(2,1)S(1)} collective-permute-done((bf16[320,768]{1,0:T(8,128)(2,1)S(1)}, bf16[320,768]{1,0:T(8,128)(2,1)S(1)}, u32[]{:S(2)}, u32[]{:S(2)}) %collective-permute-start.9) | collective-permute-done | bytes 491552 | tf_op jit(solution)/shard_map/ppermute | solution.py:234
  3.9 0.1 pair.1
  4.0 4.9 %collective-permute-start.10 = (bf16[320,768]{1,0:T(8,128)(2,1)S(1)}, bf16[320,768]{1,0:T(8,128)(2,1)S(1)}, u32[]{:S(2)}, u32[]{:S(2)}) collective-permute-start(bf16[320,768]{1,0:T(8,128)(2,1)S(1)} %get-tuple-element.1182.mine_ref), channel_id=1, source_target_pairs={{0,4},{1,7},{2,6},{3,5},{12,8},{13,11},{14,10},{15,9},{16,20},{17,... | collective-permute-start | bytes 1474568 | tf_op jit(solution)/shard_map/ppermute | solution.py:257
  8.8 0.7 %collective-permute-start.11 = (bf16[320,768]{1,0:T(8,128)(2,1)S(1)}, bf16[320,768]{1,0:T(8,128)(2,1)S(1)}, u32[]{:S(2)}, u32[]{:S(2)}) collective-permute-start(bf16[320,768]{1,0:T(8,128)(2,1)S(1)} %get-tuple-element.1183), channel_id=1, source_target_pairs={{4,8},{5,11},{6,10},{7,9},{8,4},{9,7},{10,6},{11,5},{20,24},{21,27... | collective-permute-start | bytes 1474568 | tf_op jit(solution)/shard_map/ppermute | solution.py:257
  9.5 4.0 %collective-permute-start.12 = (bf16[320,768]{1,0:T(8,128)(2,1)S(1)}, bf16[320,768]{1,0:T(8,128)(2,1)S(1)}, u32[]{:S(2)}, u32[]{:S(2)}) collective-permute-start(bf16[320,768]{1,0:T(8,128)(2,1)S(1)} %get-tuple-element.1183), channel_id=1, source_target_pairs={{0,8},{1,11},{2,10},{3,9},{12,4},{13,7},{14,6},{15,5},{16,24},{17,... | collective-permute-start | bytes 1474568 | tf_op jit(solution)/shard_map/ppermute | solution.py:257
  13.5 0.7 %collective-permute-start.13 = (bf16[320,768]{1,0:T(8,128)(2,1)S(1)}, bf16[320,768]{1,0:T(8,128)(2,1)S(1)}, u32[]{:S(2)}, u32[]{:S(2)}) collective-permute-start(bf16[320,768]{1,0:T(8,128)(2,1)S(1)} %get-tuple-element.1182.mine_ref), channel_id=1, source_target_pairs={{5,7},{7,5},{9,11},{11,9},{21,23},{23,21},{25,27},{27,25}} | collective-permute-start | bytes 1474568 | tf_op jit(solution)/shard_map/ppermute | solution.py:257
  14.2 6.1 %collective-permute-done.10.refs_0_ = bf16[320,768]{1,0:T(8,128)(2,1)S(1)} collective-permute-done((bf16[320,768]{1,0:T(8,128)(2,1)S(1)}, bf16[320,768]{1,0:T(8,128)(2,1)S(1)}, u32[]{:S(2)}, u32[]{:S(2)}) %collective-permute-start.10) | collective-permute-done | bytes 491552 | tf_op jit(solution)/shard_map/ppermute | solution.py:257
  20.3 0.0 collective-permute-done.11.refs_1_
  20.3 10.6 %collective-permute-done.12.refs_2_ = bf16[320,768]{1,0:T(8,128)(2,1)S(1)} collective-permute-done((bf16[320,768]{1,0:T(8,128)(2,1)S(1)}, bf16[320,768]{1,0:T(8,128)(2,1)S(1)}, u32[]{:S(2)}, u32[]{:S(2)}) %collective-permute-start.12) | collective-permute-done | bytes 491552 | tf_op jit(solution)/shard_map/ppermute | solution.py:257
  30.9 0.0 collective-permute-done.13.refs_3_
  30.9 0.2 join.1.mine_ref
  31.0 0.8 %collective-permute-start.14 = (bf16[1280,768]{1,0:T(8,128)(2,1)S(1)}, bf16[1280,768]{1,0:T(8,128)(2,1)S(1)}, u32[]{:S(2)}, u32[]{:S(2)}) collective-permute-start(bf16[1280,768]{1,0:T(8,128)(2,1)S(1)} %join.1.mine_ref), channel_id=1, source_target_pairs={{4,5},{5,4},{6,7},{7,6},{8,9},{9,8},{10,11},{11,10},{20,21},{21,20... | collective-permute-start | bytes 5898248 | tf_op jit(solution)/shard_map/ppermute | solution.py:276
  31.9 0.0 collective-permute-done.14.other_ref
  31.9 0.0 copy-start
  31.9 0.0 copy-start.2
  31.9 0.0 copy-start.3
  31.9 0.6 %other.1 = f32[128,128]{1,0:T(8,128)} custom-call(bf16[1280,768]{1,0:T(8,128)(2,1)S(1)} %join.1.mine_ref, bf16[1280,768]{1,0:T(8,128)(2,1)S(1)} %collective-permute-done.14.other_ref, f32[8,1280]{1,0:T(8,128)S(1)} %get-tuple-element.1184.best_ref, f32[8,1280]{1,0:T(8,128)S(1)} %get-tuple-element.1185.top_ref, f32[8,128]{1,0:T(8,128)S(1)} %get-tuple-element.1186.over_ref), custom_call_target="tpu_custom_call" | custom-call | flops 2516582400 | bytes 1966080 | tf_op jit(solution)/shard_map/other/pallas_call | solution.py:287
  32.5 14.8 %all-to-all-start.4 = ((f32[16,8,128]{2,1,0:T(8,128)}), f32[16,8,128]{2,1,0:T(8,128)S(1)}, u32[]{:S(2)}, u32[]{:S(2)}) async-start(f32[16,8,128]{2,1,0:T(8,128)} %bitcast.12), calls=%async_computation.4 | async-start | bytes 131072 | tf_op jit(solution)/shard_map/all_to_all | solution.py:297
  47.4 6.9 %all-to-all-done.4 = f32[16,8,128]{2,1,0:T(8,128)S(1)} async-done(((f32[16,8,128]{2,1,0:T(8,128)}), f32[16,8,128]{2,1,0:T(8,128)S(1)}, u32[]{:S(2)}, u32[]{:S(2)}) %all-to-all-start.4) | async-done | bytes 65568 | tf_op jit(solution)/shard_map/all_to_all | solution.py:297
  54.2 0.7 %unpack.1 = (f32[1,512]{1,0:T(1,128)S(1)}, s32[1,1]{1,0:T(1,128)}) custom-call(f32[128,128]{1,0:T(8,128)S(1)} %bitcast.55, s32[8,512]{1,0:T(8,128)S(1)} %get-tuple-element.1180.slot_ref), custom_call_target="tpu_custom_call" | custom-call | tf_op jit(solution)/shard_map/unpack/pallas_call | solution.py:300
  55.6 0.0 copy-done
  55.6 0.0 copy-done.2
  55.6 0.0 copy-done.3
  55.6 0.2 conditional.1
  55.8 0.0 copy-start.4
  55.9 0.6 %copy-done.4 = f32[512]{0:T(512)} copy-done((f32[512]{0:T(512)}, f32[512]{0:T(512)S(1)}, u32[]{:S(2)}) %copy-start.4) | copy-done | bytes 2072
  (1 shorter events, 0.0 us)
Async XLA Ops:
  1.9 2.0 %collective-permute-start.9 = (bf16[320,768]{1,0:T(8,128)(2,1)S(1)}, bf16[320,768]{1,0:T(8,128)(2,1)S(1)}, u32[]{:S(2)}, u32[]{:S(2)}) collective-permute-start(bf16[320,768]{1,0:T(8,128)(2,1)S(1)} %get-tuple-element.1181), channel_id=1, source_target_pairs={{0,1},{1,0},{2,3},{3,2},{4,5},{5,4},{6,7},{7,6},{8,9},{9,8},{10,11... | collective-permute-start | bytes 1474568 | tf_op jit(solution)/shard_map/ppermute | solution.py:234
  4.0 16.3 %collective-permute-start.10 = (bf16[320,768]{1,0:T(8,128)(2,1)S(1)}, bf16[320,768]{1,0:T(8,128)(2,1)S(1)}, u32[]{:S(2)}, u32[]{:S(2)}) collective-permute-start(bf16[320,768]{1,0:T(8,128)(2,1)S(1)} %get-tuple-element.1182.mine_ref), channel_id=1, source_target_pairs={{0,4},{1,7},{2,6},{3,5},{12,8},{13,11},{14,10},{15,9},{16,20},{17,... | collective-permute-start | bytes 1474568 | tf_op jit(solution)/shard_map/ppermute | solution.py:257
  8.8 11.4 %collective-permute-start.11 = (bf16[320,768]{1,0:T(8,128)(2,1)S(1)}, bf16[320,768]{1,0:T(8,128)(2,1)S(1)}, u32[]{:S(2)}, u32[]{:S(2)}) collective-permute-start(bf16[320,768]{1,0:T(8,128)(2,1)S(1)} %get-tuple-element.1183), channel_id=1, source_target_pairs={{4,8},{5,11},{6,10},{7,9},{8,4},{9,7},{10,6},{11,5},{20,24},{21,27... | collective-permute-start | bytes 1474568 | tf_op jit(solution)/shard_map/ppermute | solution.py:257
  9.5 21.3 %collective-permute-start.12 = (bf16[320,768]{1,0:T(8,128)(2,1)S(1)}, bf16[320,768]{1,0:T(8,128)(2,1)S(1)}, u32[]{:S(2)}, u32[]{:S(2)}) collective-permute-start(bf16[320,768]{1,0:T(8,128)(2,1)S(1)} %get-tuple-element.1183), channel_id=1, source_target_pairs={{0,8},{1,11},{2,10},{3,9},{12,4},{13,7},{14,6},{15,5},{16,24},{17,... | collective-permute-start | bytes 1474568 | tf_op jit(solution)/shard_map/ppermute | solution.py:257
  13.5 17.3 %collective-permute-start.13 = (bf16[320,768]{1,0:T(8,128)(2,1)S(1)}, bf16[320,768]{1,0:T(8,128)(2,1)S(1)}, u32[]{:S(2)}, u32[]{:S(2)}) collective-permute-start(bf16[320,768]{1,0:T(8,128)(2,1)S(1)} %get-tuple-element.1182.mine_ref), channel_id=1, source_target_pairs={{5,7},{7,5},{9,11},{11,9},{21,23},{23,21},{25,27},{27,25}} | collective-permute-start | bytes 1474568 | tf_op jit(solution)/shard_map/ppermute | solution.py:257
  31.0 0.8 %collective-permute-start.14 = (bf16[1280,768]{1,0:T(8,128)(2,1)S(1)}, bf16[1280,768]{1,0:T(8,128)(2,1)S(1)}, u32[]{:S(2)}, u32[]{:S(2)}) collective-permute-start(bf16[1280,768]{1,0:T(8,128)(2,1)S(1)} %join.1.mine_ref), channel_id=1, source_target_pairs={{4,5},{5,4},{6,7},{7,6},{8,9},{9,8},{10,11},{11,10},{20,21},{21,20... | collective-permute-start | bytes 5898248 | tf_op jit(solution)/shard_map/ppermute | solution.py:276
  31.9 23.7 %copy-start = (bf16[512,768]{1,0:T(8,128)(2,1)S(1)}, bf16[512,768]{1,0:T(8,128)(2,1)}, u32[]{:S(2)}) copy-start(bf16[512,768]{1,0:T(8,128)(2,1)} %x_ref.1) | copy-start | bytes 2359300
  31.9 23.7 %copy-start.2 = (s32[512]{0:T(512)S(1)}, s32[512]{0:T(512)}, u32[]{:S(2)}) copy-start(s32[512]{0:T(512)} %param.22) | copy-start | bytes 6148
  31.9 23.7 %copy-start.3 = (s32[512]{0:T(512)S(1)}, s32[512]{0:T(512)}, u32[]{:S(2)}) copy-start(s32[512]{0:T(512)} %param.23) | copy-start | bytes 6148
  32.5 21.7 %all-to-all-start.4 = ((f32[16,8,128]{2,1,0:T(8,128)}), f32[16,8,128]{2,1,0:T(8,128)S(1)}, u32[]{:S(2)}, u32[]{:S(2)}) async-start(f32[16,8,128]{2,1,0:T(8,128)} %bitcast.12), calls=%async_computation.4 | async-start | bytes 131072 | tf_op jit(solution)/shard_map/all_to_all | solution.py:297
  55.8 0.6 %copy-start.4 = (f32[512]{0:T(512)}, f32[512]{0:T(512)S(1)}, u32[]{:S(2)}) copy-start(f32[512]{0:T(512)S(1)} %get-tuple-element.2165) | copy-start | bytes 6148

commit v7 on v6

--- a/solution.py
+++ b/solution.py
@@ -12,12 +12,12 @@
 HOMES = (2, 3, 4, 5)
 HOME_ROUNDS = (0, 6)
 OUTER_ROUNDS = (2, 4)
-ORDER = (2,6,4,0)
+ORDER = (2, 6, 4, 0)
 BLOCK = 160
 CAP = 156
 META = 16
 HELD = CHIPS * BLOCK
-VMEM_LIMIT = 48 * 1024 * 1024
+VMEM_LIMIT = 28 * 1024 * 1024
 NT = (((1,), (1,)), ((), ()))
 
 
@@ -89,7 +89,7 @@
     pack_rows(unit_ref, meta_ref, slot_ref, me // 2, me % 2, keep_ref)
 
 
-def fill_codes(keys, codes):
+def fill_codes(keys, codes, blocks):
     eye = (
         lax.broadcasted_iota(jnp.int32, (BLOCK, 256), 0)
         == lax.broadcasted_iota(jnp.int32, (BLOCK, 256), 1)
@@ -100,7 +100,7 @@
         lane == first, 4096.0, jnp.where(lane == first + 1, 64.0, jnp.where(lane == first + 2, 1.0, 0.0))
     )
     over = jnp.zeros((1, 128), jnp.float32)
-    for n in range(CHIPS):
+    for n in range(blocks):
         meta = keys[(n + 1) * BLOCK - META : (n + 1) * BLOCK, :256]
         over = jnp.maximum(over, meta[META - 1 :, :128].astype(jnp.float32))
         columns = lax.dot_general(eye, meta, NT, preferred_element_type=jnp.float32)
@@ -111,10 +111,11 @@
 
 def best_of(keys, codes, query, top):
     size = query.shape[0]
-    step = HELD // 2
+    total = keys.shape[0]
+    step = total // 2
     base = jnp.floor(top * (1.0 / 4096.0)) * 4096.0
     best = jnp.full((8, size), -1.0, jnp.float32)
-    for start in range(0, HELD, step):
+    for start in range(0, total, step):
         score = lax.dot_general(
             keys[start : start + step], query, NT, preferred_element_type=jnp.float32
         )
@@ -131,8 +132,13 @@
     second_ref[BLOCK:] = got_ref[BLOCK:]
 
 
-def join_kernel(mine_ref, *refs):
-    blocks, out_ref = refs[:-1], refs[-1]
+def halve_kernel(pair_ref, one_ref, two_ref):
+    one_ref[...] = pair_ref[:BLOCK]
+    two_ref[...] = pair_ref[BLOCK:]
+
+
+def join_kernel(mine_ref, one_ref, two_ref, *refs):
+    blocks, (out_ref, late_ref) = refs[:-2], refs[-2:]
     for n, ref in enumerate(blocks):
         out_ref[n * 2 * BLOCK : (n + 1) * 2 * BLOCK] = ref[...]
 
@@ -141,11 +147,15 @@
         at = ORDER.index(0) * 2 * BLOCK
         out_ref[at : at + 2 * BLOCK] = mine_ref[...]
 
+    out_ref[HELD : HELD + BLOCK] = one_ref[...]
+    out_ref[HELD + BLOCK :] = two_ref[...]
+    late_ref[...] = out_ref[2 * BLOCK : HELD]
+
 
 def own_kernel(mine_ref, best_ref, top_ref, over_ref, codes):
     @pl.when(is_home(lax.axis_index("owner") // 2))
     def _():
-        over_ref[...] = jnp.broadcast_to(fill_codes(mine_ref, codes), over_ref.shape)
+        over_ref[...] = jnp.broadcast_to(fill_codes(mine_ref, codes, CHIPS + 2), over_ref.shape)
         for at in range(0, HELD, 256):
             top = jnp.transpose(codes[at : at + 256])[:8]
             top_ref[:, at : at + 256] = top
@@ -161,7 +171,7 @@
 
     @pl.when(is_home(chip))
     def _():
-        over = jnp.max(jnp.maximum(fill_codes(other_ref, codes), over_ref[:1]))
+        over = jnp.max(jnp.maximum(fill_codes(other_ref, codes, CHIPS - 2), over_ref[:1]))
         found = [
             jnp.maximum(
                 best_ref[:, at : at + 256],
@@ -261,19 +271,31 @@
     pairs = {6: carry(second, 6), 4: carry(second, 4), 2: carry(first, 2), 0: carry(first, 0, (1,))}
     swap = [(2 * h + c, 2 * h + 1 - c) for h in HOMES for c in range(2)]
     line = jax.ShapeDtypeStruct((8, HELD), jnp.float32)
-    codes = [pltpu.VMEM((HELD, 128), jnp.float32)]
+    codes = [pltpu.VMEM((HELD + 2 * BLOCK, 128), jnp.float32)]
     cost = pl.CostEstimate(
         flops=2 * HELD * HELD * width, bytes_accessed=2 * HELD * width, transcendentals=0
     )
-    mine = pl.pallas_call(
+    halves = pl.pallas_call(
+        halve_kernel,
+        out_shape=[jax.ShapeDtypeStruct((BLOCK, width), jnp.bfloat16)] * 2,
+        in_specs=[vmem],
+        out_specs=[vmem] * 2,
+        compiler_params=params,
+        name="halve",
+    )(pairs[2])
+    halves = [lax.ppermute(block, "owner", swap) for block in halves]
+    mine, late = pl.pallas_call(
         join_kernel,
-        out_shape=jax.ShapeDtypeStruct((HELD, width), jnp.bfloat16),
-        in_specs=[vmem] * (1 + len(ORDER)),
-        out_specs=vmem,
+        out_shape=[
+            jax.ShapeDtypeStruct((HELD + 2 * BLOCK, width), jnp.bfloat16),
+            jax.ShapeDtypeStruct((HELD - 2 * BLOCK, width), jnp.bfloat16),
+        ],
+        in_specs=[vmem] * (3 + len(ORDER)),
+        out_specs=[vmem] * 2,
         compiler_params=params,
         name="join",
-    )(first, *[pairs[k] for k in ORDER])
-    other = lax.ppermute(mine, "owner", swap)
+    )(first, *halves, *[pairs[k] for k in ORDER])
+    other = lax.ppermute(late, "owner", swap)
     best, top, over = pl.pallas_call(
         own_kernel,
         out_shape=[line, line, jax.ShapeDtypeStruct((8, 128), jnp.float32)],

time: 56.7 us -> 56.5 us (level)
  waiting for transfers between devices: 24.5 us -> 23.1 us
  starting transfers between devices: 26.3 us -> 27.3 us
    ppermute x4, waiting for transfers between devices: 16.6 us -> 15.2 us  [carry(): lax.ppermute(pair, 'owner', [(2 * s + c, 2 * (s ^ (k | c)) + c) for s in...]
    ppermute x1 -> x3, starting transfers between devices: 0.79 us -> 2.11 us  [the longest x2 1.35 us: meet(): halves = [lax.ppermute(block, 'owner', swap) for block in halves]]
  transfers between devices with their start and end apart: 7 -> 9, of which waited for: 4 -> 4; matrix products, arithmetic and copies ran while one was open for 0% -> 0% of each run, Pallas kernels for 1% -> 1%
where the time goes in v7:
time: 56.5 us; the launch traced here: 56.2 us
  starting transfers between devices  27.3 us (48%)
  waiting for transfers between devices  23.1 us (41%)
  Pallas kernels  4.1 us (7%)
  between operations  0.84 us (1%)
  local copies, waits for them, and re-layouts  0.59 us (1%)
    ppermute x4, waiting for transfers between devices, carry(): lax.ppermute(pair, 'owner', [(2 * s + c, 2 * (s ^ (k | c)) + c) for s in...  15.2 us
    all_to_all x1, starting transfers between devices, meet(): lax.all_to_all(found.reshape(OWNERS, 8, 128), 'owner', split_axis=0, conc...  14.4 us
    ppermute x4, starting transfers between devices, carry(): lax.ppermute(pair, 'owner', [(2 * s + c, 2 * (s ^ (k | c)) + c) for s in...  10.2 us
    all_to_all x1, waiting for transfers between devices, meet(): lax.all_to_all(found.reshape(OWNERS, 8, 128), 'owner', split_axis=0, conc...  6.9 us
    pallas_call x1, Pallas kernels, meet(): pl.pallas_call(pack_kernel, out_shape=[two_blocks, jax.ShapeDtypeStruct((...  1.88 us
    ppermute x2, starting transfers between devices, meet(): halves = [lax.ppermute(block, 'owner', swap) for block in halves]  1.35 us
  transfers between devices with their start and end apart: 9, of which 4 were waited for; matrix products, arithmetic and copies ran while one was open for 0% of the time, Pallas kernels for 1%

profile of v7, /device:TPU:0, one launch (start us, length us, event | category | flops | bytes accessed | tf_op | source)
XLA Modules:
  0.0 56.2 jit_solution(16856802648458955460)
XLA Ops:
  0.0 1.9 %pack.1 = (bf16[320,768]{1,0:T(8,128)(2,1)S(1)}, s32[8,512]{1,0:T(8,128)S(1)}, bf16[512,768]{1,0:T(8,128)(2,1)S(1)}, bf16[16,512]{1,0:T(8,128)(2,1)S(1)}) custom-call(bf16[512,768]{1,0:T(8,128)(2,1)} %x_ref.1, s32[1,512]{1,0:T(1,128)} %bitcast.58, s32[1,512]{1,0:T(1,128)} %bitcast.59), custom_call_target="tpu_custom_call" | custom-call | tf_op jit(solution)/shard_map/pack/pallas_call | solution.py:231
  1.9 0.5 collective-permute-start.9
  2.4 0.5 keep.1.keep_ref
  2.9 1.0 %collective-permute-done.9.got_ref = bf16[320,768]{1,0:T(8,128)(2,1)S(1)} collective-permute-done((bf16[320,768]{1,0:T(8,128)(2,1)S(1)}, bf16[320,768]{1,0:T(8,128)(2,1)S(1)}, u32[]{:S(2)}, u32[]{:S(2)}) %collective-permute-start.9) | collective-permute-done | bytes 491552 | tf_op jit(solution)/shard_map/ppermute | solution.py:244
  3.9 0.1 pair.1
  4.0 4.9 %collective-permute-start.10 = (bf16[320,768]{1,0:T(8,128)(2,1)S(1)}, bf16[320,768]{1,0:T(8,128)(2,1)S(1)}, u32[]{:S(2)}, u32[]{:S(2)}) collective-permute-start(bf16[320,768]{1,0:T(8,128)(2,1)S(1)} %get-tuple-element.1186.mine_ref), channel_id=1, source_target_pairs={{0,4},{1,7},{2,6},{3,5},{12,8},{13,11},{14,10},{15,9},{16,20},{17,... | collective-permute-start | bytes 1474568 | tf_op jit(solution)/shard_map/ppermute | solution.py:267
  8.8 0.7 %collective-permute-start.13 = (bf16[320,768]{1,0:T(8,128)(2,1)S(1)}, bf16[320,768]{1,0:T(8,128)(2,1)S(1)}, u32[]{:S(2)}, u32[]{:S(2)}) collective-permute-start(bf16[320,768]{1,0:T(8,128)(2,1)S(1)} %get-tuple-element.1189), channel_id=1, source_target_pairs={{4,8},{5,11},{6,10},{7,9},{8,4},{9,7},{10,6},{11,5},{20,24},{21,27... | collective-permute-start | bytes 1474568 | tf_op jit(solution)/shard_map/ppermute | solution.py:267
  9.5 4.0 %collective-permute-start.14 = (bf16[320,768]{1,0:T(8,128)(2,1)S(1)}, bf16[320,768]{1,0:T(8,128)(2,1)S(1)}, u32[]{:S(2)}, u32[]{:S(2)}) collective-permute-start(bf16[320,768]{1,0:T(8,128)(2,1)S(1)} %get-tuple-element.1189), channel_id=1, source_target_pairs={{0,8},{1,11},{2,10},{3,9},{12,4},{13,7},{14,6},{15,5},{16,24},{17,... | collective-permute-start | bytes 1474568 | tf_op jit(solution)/shard_map/ppermute | solution.py:267
  13.5 0.7 %collective-permute-start.15 = (bf16[320,768]{1,0:T(8,128)(2,1)S(1)}, bf16[320,768]{1,0:T(8,128)(2,1)S(1)}, u32[]{:S(2)}, u32[]{:S(2)}) collective-permute-start(bf16[320,768]{1,0:T(8,128)(2,1)S(1)} %get-tuple-element.1186.mine_ref), channel_id=1, source_target_pairs={{5,7},{7,5},{9,11},{11,9},{21,23},{23,21},{25,27},{27,25}} | collective-permute-start | bytes 1474568 | tf_op jit(solution)/shard_map/ppermute | solution.py:267
  14.2 6.1 %collective-permute-done.10.pair_ref.refs_0_ = bf16[320,768]{1,0:T(8,128)(2,1)S(1)} collective-permute-done((bf16[320,768]{1,0:T(8,128)(2,1)S(1)}, bf16[320,768]{1,0:T(8,128)(2,1)S(1)}, u32[]{:S(2)}, u32[]{:S(2)}) %collective-permute-start.10) | collective-permute-done | bytes 491552 | tf_op jit(solution)/shard_map/ppermute | solution.py:267
  20.3 0.7 %collective-permute-start.11 = (bf16[160,768]{1,0:T(8,128)(2,1)S(1)}, bf16[160,768]{1,0:T(8,128)(2,1)S(1)}, u32[]{:S(2)}, u32[]{:S(2)}) collective-permute-start(bf16[160,768]{1,0:T(8,128)(2,1)S(1)} %get-tuple-element.1187), channel_id=1, source_target_pairs={{4,5},{5,4},{6,7},{7,6},{8,9},{9,8},{10,11},{11,10},{20,21},{21,20... | collective-permute-start | bytes 737288 | tf_op jit(solution)/shard_map/ppermute | solution.py:286
  21.0 0.7 %collective-permute-start.12 = (bf16[160,768]{1,0:T(8,128)(2,1)S(1)}, bf16[160,768]{1,0:T(8,128)(2,1)S(1)}, u32[]{:S(2)}, u32[]{:S(2)}) collective-permute-start(bf16[160,768]{1,0:T(8,128)(2,1)S(1)} %get-tuple-element.1188), channel_id=1, source_target_pairs={{4,5},{5,4},{6,7},{7,6},{8,9},{9,8},{10,11},{11,10},{20,21},{21,20... | collective-permute-start | bytes 737288 | tf_op jit(solution)/shard_map/ppermute | solution.py:286
  21.7 0.0 collective-permute-done.13.refs_1_
  21.7 9.2 %collective-permute-done.14.refs_2_ = bf16[320,768]{1,0:T(8,128)(2,1)S(1)} collective-permute-done((bf16[320,768]{1,0:T(8,128)(2,1)S(1)}, bf16[320,768]{1,0:T(8,128)(2,1)S(1)}, u32[]{:S(2)}, u32[]{:S(2)}) %collective-permute-start.14) | collective-permute-done | bytes 491552 | tf_op jit(solution)/shard_map/ppermute | solution.py:267
  30.9 0.0 collective-permute-done.15.refs_3_
  30.9 0.0 collective-permute-done.11.one_ref
  30.9 0.0 collective-permute-done.12.two_ref
  30.9 0.3 join.1
  31.2 0.8 %collective-permute-start.16 = (bf16[960,768]{1,0:T(8,128)(2,1)S(1)}, bf16[960,768]{1,0:T(8,128)(2,1)S(1)}, u32[]{:S(2)}, u32[]{:S(2)}) collective-permute-start(bf16[960,768]{1,0:T(8,128)(2,1)S(1)} %get-tuple-element.1191), channel_id=1, source_target_pairs={{4,5},{5,4},{6,7},{7,6},{8,9},{9,8},{10,11},{11,10},{20,21},{21,20... | collective-permute-start | bytes 4423688 | tf_op jit(solution)/shard_map/ppermute | solution.py:298
  32.0 0.0 collective-permute-done.16.other_ref
  32.0 0.0 copy-start
  32.0 0.0 copy-start.2
  32.0 0.0 copy-start.3
  32.0 0.6 %other.1 = f32[128,128]{1,0:T(8,128)} custom-call(bf16[1600,768]{1,0:T(8,128)(2,1)S(1)} %get-tuple-element.1190.mine_ref, bf16[960,768]{1,0:T(8,128)(2,1)S(1)} %collective-permute-done.16.other_ref, f32[8,1280]{1,0:T(8,128)S(1)} %get-tuple-element.1192.best_ref, f32[8,1280]{1,0:T(8,128)S(1)} %get-tuple-element.1193.top_ref, ...), custom_call_target="tpu_custom_call" | custom-call | flops 2516582400 | bytes 1966080 | tf_op jit(solution)/shard_map/other/pallas_call | solution.py:309
  32.6 14.4 %all-to-all-start.4 = ((f32[16,8,128]{2,1,0:T(8,128)}), f32[16,8,128]{2,1,0:T(8,128)S(1)}, u32[]{:S(2)}, u32[]{:S(2)}) async-start(f32[16,8,128]{2,1,0:T(8,128)} %bitcast.12), calls=%async_computation.4 | async-start | bytes 131072 | tf_op jit(solution)/shard_map/all_to_all | solution.py:319
  47.1 6.9 %all-to-all-done.4 = f32[16,8,128]{2,1,0:T(8,128)S(1)} async-done(((f32[16,8,128]{2,1,0:T(8,128)}), f32[16,8,128]{2,1,0:T(8,128)S(1)}, u32[]{:S(2)}, u32[]{:S(2)}) %all-to-all-start.4) | async-done | bytes 65568 | tf_op jit(solution)/shard_map/all_to_all | solution.py:319
  54.0 0.7 %unpack.1 = (f32[1,512]{1,0:T(1,128)S(1)}, s32[1,1]{1,0:T(1,128)}) custom-call(f32[128,128]{1,0:T(8,128)S(1)} %bitcast.55, s32[8,512]{1,0:T(8,128)S(1)} %get-tuple-element.1184.slot_ref), custom_call_target="tpu_custom_call" | custom-call | tf_op jit(solution)/shard_map/unpack/pallas_call | solution.py:322
  55.3 0.0 copy-done
  55.3 0.0 copy-done.2
  55.3 0.0 copy-done.3
  55.3 0.2 conditional.1
  55.6 0.0 copy-start.4
  55.6 0.6 %copy-done.4 = f32[512]{0:T(512)} copy-done((f32[512]{0:T(512)}, f32[512]{0:T(512)S(1)}, u32[]{:S(2)}) %copy-start.4) | copy-done | bytes 2072
  (2 shorter events, 0.1 us)
Async XLA Ops:
  1.9 2.0 %collective-permute-start.9 = (bf16[320,768]{1,0:T(8,128)(2,1)S(1)}, bf16[320,768]{1,0:T(8,128)(2,1)S(1)}, u32[]{:S(2)}, u32[]{:S(2)}) collective-permute-start(bf16[320,768]{1,0:T(8,128)(2,1)S(1)} %get-tuple-element.1185), channel_id=1, source_target_pairs={{0,1},{1,0},{2,3},{3,2},{4,5},{5,4},{6,7},{7,6},{8,9},{9,8},{10,11... | collective-permute-start | bytes 1474568 | tf_op jit(solution)/shard_map/ppermute | solution.py:244
  4.0 16.3 %collective-permute-start.10 = (bf16[320,768]{1,0:T(8,128)(2,1)S(1)}, bf16[320,768]{1,0:T(8,128)(2,1)S(1)}, u32[]{:S(2)}, u32[]{:S(2)}) collective-permute-start(bf16[320,768]{1,0:T(8,128)(2,1)S(1)} %get-tuple-element.1186.mine_ref), channel_id=1, source_target_pairs={{0,4},{1,7},{2,6},{3,5},{12,8},{13,11},{14,10},{15,9},{16,20},{17,... | collective-permute-start | bytes 1474568 | tf_op jit(solution)/shard_map/ppermute | solution.py:267
  8.8 12.8 %collective-permute-start.13 = (bf16[320,768]{1,0:T(8,128)(2,1)S(1)}, bf16[320,768]{1,0:T(8,128)(2,1)S(1)}, u32[]{:S(2)}, u32[]{:S(2)}) collective-permute-start(bf16[320,768]{1,0:T(8,128)(2,1)S(1)} %get-tuple-element.1189), channel_id=1, source_target_pairs={{4,8},{5,11},{6,10},{7,9},{8,4},{9,7},{10,6},{11,5},{20,24},{21,27... | collective-permute-start | bytes 1474568 | tf_op jit(solution)/shard_map/ppermute | solution.py:267
  9.5 21.3 %collective-permute-start.14 = (bf16[320,768]{1,0:T(8,128)(2,1)S(1)}, bf16[320,768]{1,0:T(8,128)(2,1)S(1)}, u32[]{:S(2)}, u32[]{:S(2)}) collective-permute-start(bf16[320,768]{1,0:T(8,128)(2,1)S(1)} %get-tuple-element.1189), channel_id=1, source_target_pairs={{0,8},{1,11},{2,10},{3,9},{12,4},{13,7},{14,6},{15,5},{16,24},{17,... | collective-permute-start | bytes 1474568 | tf_op jit(solution)/shard_map/ppermute | solution.py:267
  13.5 17.3 %collective-permute-start.15 = (bf16[320,768]{1,0:T(8,128)(2,1)S(1)}, bf16[320,768]{1,0:T(8,128)(2,1)S(1)}, u32[]{:S(2)}, u32[]{:S(2)}) collective-permute-start(bf16[320,768]{1,0:T(8,128)(2,1)S(1)} %get-tuple-element.1186.mine_ref), channel_id=1, source_target_pairs={{5,7},{7,5},{9,11},{11,9},{21,23},{23,21},{25,27},{27,25}} | collective-permute-start | bytes 1474568 | tf_op jit(solution)/shard_map/ppermute | solution.py:267
  20.3 10.6 %collective-permute-start.11 = (bf16[160,768]{1,0:T(8,128)(2,1)S(1)}, bf16[160,768]{1,0:T(8,128)(2,1)S(1)}, u32[]{:S(2)}, u32[]{:S(2)}) collective-permute-start(bf16[160,768]{1,0:T(8,128)(2,1)S(1)} %get-tuple-element.1187), channel_id=1, source_target_pairs={{4,5},{5,4},{6,7},{7,6},{8,9},{9,8},{10,11},{11,10},{20,21},{21,20... | collective-permute-start | bytes 737288 | tf_op jit(solution)/shard_map/ppermute | solution.py:286
  21.0 9.9 %collective-permute-start.12 = (bf16[160,768]{1,0:T(8,128)(2,1)S(1)}, bf16[160,768]{1,0:T(8,128)(2,1)S(1)}, u32[]{:S(2)}, u32[]{:S(2)}) collective-permute-start(bf16[160,768]{1,0:T(8,128)(2,1)S(1)} %get-tuple-element.1188), channel_id=1, source_target_pairs={{4,5},{5,4},{6,7},{7,6},{8,9},{9,8},{10,11},{11,10},{20,21},{21,20... | collective-permute-start | bytes 737288 | tf_op jit(solution)/shard_map/ppermute | solution.py:286
  31.2 0.8 %collective-permute-start.16 = (bf16[960,768]{1,0:T(8,128)(2,1)S(1)}, bf16[960,768]{1,0:T(8,128)(2,1)S(1)}, u32[]{:S(2)}, u32[]{:S(2)}) collective-permute-start(bf16[960,768]{1,0:T(8,128)(2,1)S(1)} %get-tuple-element.1191), channel_id=1, source_target_pairs={{4,5},{5,4},{6,7},{7,6},{8,9},{9,8},{10,11},{11,10},{20,21},{21,20... | collective-permute-start | bytes 4423688 | tf_op jit(solution)/shard_map/ppermute | solution.py:298
  32.0 23.3 %copy-start = (bf16[512,768]{1,0:T(8,128)(2,1)S(1)}, bf16[512,768]{1,0:T(8,128)(2,1)}, u32[]{:S(2)}) copy-start(bf16[512,768]{1,0:T(8,128)(2,1)} %x_ref.1) | copy-start | bytes 2359300
  32.0 23.3 %copy-start.2 = (s32[512]{0:T(512)S(1)}, s32[512]{0:T(512)}, u32[]{:S(2)}) copy-start(s32[512]{0:T(512)} %param.22) | copy-start | bytes 6148
  32.0 23.3 %copy-start.3 = (s32[512]{0:T(512)S(1)}, s32[512]{0:T(512)}, u32[]{:S(2)}) copy-start(s32[512]{0:T(512)} %param.23) | copy-start | bytes 6148
  32.6 21.3 %all-to-all-start.4 = ((f32[16,8,128]{2,1,0:T(8,128)}), f32[16,8,128]{2,1,0:T(8,128)S(1)}, u32[]{:S(2)}, u32[]{:S(2)}) async-start(f32[16,8,128]{2,1,0:T(8,128)} %bitcast.12), calls=%async_computation.4 | async-start | bytes 131072 | tf_op jit(solution)/shard_map/all_to_all | solution.py:319
  55.6 0.6 %copy-start.4 = (f32[512]{0:T(512)}, f32[512]{0:T(512)S(1)}, u32[]{:S(2)}) copy-start(f32[512]{0:T(512)S(1)} %get-tuple-element.2177) | copy-start | bytes 6148

commit v8 on v7

--- a/solution.py
+++ b/solution.py
@@ -109,13 +109,13 @@
     return over
 
 
-def best_of(keys, codes, query, top):
+def best_of(keys, codes, query, top, first=0):
     size = query.shape[0]
     total = keys.shape[0]
-    step = total // 2
+    step = (total - first) // 2
     base = jnp.floor(top * (1.0 / 4096.0)) * 4096.0
     best = jnp.full((8, size), -1.0, jnp.float32)
-    for start in range(0, total, step):
+    for start in range(first, total, step):
         score = lax.dot_general(
             keys[start : start + step], query, NT, preferred_element_type=jnp.float32
         )
@@ -137,8 +137,20 @@
     two_ref[...] = pair_ref[BLOCK:]
 
 
-def join_kernel(mine_ref, one_ref, two_ref, *refs):
-    blocks, (out_ref, late_ref) = refs[:-2], refs[-2:]
+def early_kernel(pair_ref, one_ref, two_ref, best_ref, keys, codes):
+    @pl.when(is_home(lax.axis_index("owner") // 2))
+    def _():
+        keys[: 2 * BLOCK] = pair_ref[...]
+        keys[2 * BLOCK : 3 * BLOCK] = one_ref[...]
+        keys[3 * BLOCK :] = two_ref[...]
+        fill_codes(keys, codes, 4)
+        top = jnp.transpose(codes[:256])[:1]
+        best_ref[...] = best_of(keys, codes, keys[:256], top)
+
+
+def join_kernel(mine_ref, one_ref, two_ref, early_ref, *refs):
+    blocks, (out_ref, late_ref, known_ref) = refs[:-3], refs[-3:]
+    known_ref[...] = early_ref[...]
     for n, ref in enumerate(blocks):
         out_ref[n * 2 * BLOCK : (n + 1) * 2 * BLOCK] = ref[...]
 
@@ -152,16 +164,21 @@
     late_ref[...] = out_ref[2 * BLOCK : HELD]
 
 
-def own_kernel(mine_ref, best_ref, top_ref, over_ref, codes):
+def own_kernel(mine_ref, early_ref, late_ref, best_ref, top_ref, over_ref, codes):
     @pl.when(is_home(lax.axis_index("owner") // 2))
     def _():
         over_ref[...] = jnp.broadcast_to(fill_codes(mine_ref, codes, CHIPS + 2), over_ref.shape)
+        late_codes = codes.at[pl.ds(2 * BLOCK, HELD - 2 * BLOCK)]
         for at in range(0, HELD, 256):
             top = jnp.transpose(codes[at : at + 256])[:8]
             top_ref[:, at : at + 256] = top
-            best_ref[:, at : at + 256] = best_of(
-                mine_ref, codes, mine_ref[at : at + 256], top[:1]
-            )
+            if at == 0:
+                own = best_of(late_ref, late_codes, mine_ref[:256], top[:1])
+                best_ref[:, :256] = jnp.maximum(early_ref[...], own)
+            else:
+                best_ref[:, at : at + 256] = best_of(
+                    mine_ref, codes, mine_ref[at : at + 256], top[:1]
+                )
 
 
 def other_kernel(mine_ref, other_ref, best_ref, top_ref, over_ref, out_ref, codes):
@@ -284,28 +301,42 @@
         name="halve",
     )(pairs[2])
     halves = [lax.ppermute(block, "owner", swap) for block in halves]
-    mine, late = pl.pallas_call(
+    early = pl.pallas_call(
+        early_kernel,
+        out_shape=jax.ShapeDtypeStruct((8, 256), jnp.float32),
+        in_specs=[vmem] * 3,
+        out_specs=vmem,
+        scratch_shapes=[
+            pltpu.VMEM((4 * BLOCK, width), jnp.bfloat16),
+            pltpu.VMEM((4 * BLOCK, 128), jnp.float32),
+        ],
+        compiler_params=params,
+        cost_estimate=pl.CostEstimate(flops=0, bytes_accessed=0, transcendentals=0),
+        name="early",
+    )(pairs[2], *halves)
+    mine, late, early = pl.pallas_call(
         join_kernel,
         out_shape=[
             jax.ShapeDtypeStruct((HELD + 2 * BLOCK, width), jnp.bfloat16),
             jax.ShapeDtypeStruct((HELD - 2 * BLOCK, width), jnp.bfloat16),
+            jax.ShapeDtypeStruct((8, 256), jnp.float32),
         ],
-        in_specs=[vmem] * (3 + len(ORDER)),
-        out_specs=[vmem] * 2,
+        in_specs=[vmem] * (4 + len(ORDER)),
+        out_specs=[vmem] * 3,
         compiler_params=params,
         name="join",
-    )(first, *halves, *[pairs[k] for k in ORDER])
+    )(first, *halves, early, *[pairs[k] for k in ORDER])
     other = lax.ppermute(late, "owner", swap)
     best, top, over = pl.pallas_call(
         own_kernel,
         out_shape=[line, line, jax.ShapeDtypeStruct((8, 128), jnp.float32)],
-        in_specs=[vmem],
+        in_specs=[vmem] * 3,
         out_specs=[vmem] * 3,
         scratch_shapes=codes,
         compiler_params=params,
         cost_estimate=cost,
         name="own",
-    )(mine)
+    )(mine, early, late)
     found = pl.pallas_call(
         other_kernel,
         out_shape=jax.ShapeDtypeStruct((8 * OWNERS, 128), jnp.float32),

time: 56.5 us -> 56.2 us (level)
  no operation moved by 1% of the time
where the time goes in v8:
time: 56.2 us; the launch traced here: 55.9 us
  starting transfers between devices  27 us (48%)
  waiting for transfers between devices  23.1 us (41%)
  Pallas kernels  4.12 us (7%)
  between operations  0.86 us (2%)
  local copies, waits for them, and re-layouts  0.59 us (1%)
    ppermute x4, waiting for transfers between devices, carry(): lax.ppermute(pair, 'owner', [(2 * s + c, 2 * (s ^ (k | c)) + c) for s in...  15.2 us
    all_to_all x1, starting transfers between devices, meet(): lax.all_to_all(found.reshape(OWNERS, 8, 128), 'owner', split_axis=0, conc...  14.1 us
    ppermute x4, starting transfers between devices, carry(): lax.ppermute(pair, 'owner', [(2 * s + c, 2 * (s ^ (k | c)) + c) for s in...  10.2 us
    all_to_all x1, waiting for transfers between devices, meet(): lax.all_to_all(found.reshape(OWNERS, 8, 128), 'owner', split_axis=0, conc...  6.9 us
    pallas_call x1, Pallas kernels, meet(): pl.pallas_call(pack_kernel, out_shape=[two_blocks, jax.ShapeDtypeStruct((...  1.88 us
    ppermute x2, starting transfers between devices, meet(): halves = [lax.ppermute(block, 'owner', swap) for block in halves]  1.35 us
  transfers between devices with their start and end apart: 9, of which 4 were waited for; matrix products, arithmetic and copies ran while one was open for 0% of the time, Pallas kernels for 1%

profile of v8, /device:TPU:0, one launch (start us, length us, event | category | flops | bytes accessed | tf_op | source)
XLA Modules:
  0.0 55.9 jit_solution(16001326223177380886)
XLA Ops:
  0.0 1.9 %pack.1 = (bf16[320,768]{1,0:T(8,128)(2,1)S(1)}, s32[8,512]{1,0:T(8,128)S(1)}, bf16[512,768]{1,0:T(8,128)(2,1)S(1)}, bf16[16,512]{1,0:T(8,128)(2,1)S(1)}) custom-call(bf16[512,768]{1,0:T(8,128)(2,1)} %x_ref.1, s32[1,512]{1,0:T(1,128)} %bitcast.58, s32[1,512]{1,0:T(1,128)} %bitcast.59), custom_call_target="tpu_custom_call" | custom-call | tf_op jit(solution)/shard_map/pack/pallas_call | solution.py:248
  1.9 0.5 collective-permute-start.9
  2.4 0.5 keep.1.keep_ref
  2.9 1.0 %collective-permute-done.9.got_ref = bf16[320,768]{1,0:T(8,128)(2,1)S(1)} collective-permute-done((bf16[320,768]{1,0:T(8,128)(2,1)S(1)}, bf16[320,768]{1,0:T(8,128)(2,1)S(1)}, u32[]{:S(2)}, u32[]{:S(2)}) %collective-permute-start.9) | collective-permute-done | bytes 491552 | tf_op jit(solution)/shard_map/ppermute | solution.py:261
  3.9 0.1 pair.1
  4.0 4.9 %collective-permute-start.10 = (bf16[320,768]{1,0:T(8,128)(2,1)S(1)}, bf16[320,768]{1,0:T(8,128)(2,1)S(1)}, u32[]{:S(2)}, u32[]{:S(2)}) collective-permute-start(bf16[320,768]{1,0:T(8,128)(2,1)S(1)} %get-tuple-element.1187.mine_ref), channel_id=1, source_target_pairs={{0,4},{1,7},{2,6},{3,5},{12,8},{13,11},{14,10},{15,9},{16,20},{17,... | collective-permute-start | bytes 1474568 | tf_op jit(solution)/shard_map/ppermute | solution.py:284
  8.8 0.7 %collective-permute-start.13 = (bf16[320,768]{1,0:T(8,128)(2,1)S(1)}, bf16[320,768]{1,0:T(8,128)(2,1)S(1)}, u32[]{:S(2)}, u32[]{:S(2)}) collective-permute-start(bf16[320,768]{1,0:T(8,128)(2,1)S(1)} %get-tuple-element.1190), channel_id=1, source_target_pairs={{4,8},{5,11},{6,10},{7,9},{8,4},{9,7},{10,6},{11,5},{20,24},{21,27... | collective-permute-start | bytes 1474568 | tf_op jit(solution)/shard_map/ppermute | solution.py:284
  9.5 4.0 %collective-permute-start.14 = (bf16[320,768]{1,0:T(8,128)(2,1)S(1)}, bf16[320,768]{1,0:T(8,128)(2,1)S(1)}, u32[]{:S(2)}, u32[]{:S(2)}) collective-permute-start(bf16[320,768]{1,0:T(8,128)(2,1)S(1)} %get-tuple-element.1190), channel_id=1, source_target_pairs={{0,8},{1,11},{2,10},{3,9},{12,4},{13,7},{14,6},{15,5},{16,24},{17,... | collective-permute-start | bytes 1474568 | tf_op jit(solution)/shard_map/ppermute | solution.py:284
  13.5 0.7 %collective-permute-start.15 = (bf16[320,768]{1,0:T(8,128)(2,1)S(1)}, bf16[320,768]{1,0:T(8,128)(2,1)S(1)}, u32[]{:S(2)}, u32[]{:S(2)}) collective-permute-start(bf16[320,768]{1,0:T(8,128)(2,1)S(1)} %get-tuple-element.1187.mine_ref), channel_id=1, source_target_pairs={{5,7},{7,5},{9,11},{11,9},{21,23},{23,21},{25,27},{27,25}} | collective-permute-start | bytes 1474568 | tf_op jit(solution)/shard_map/ppermute | solution.py:284
  14.2 6.1 %collective-permute-done.10.pair_ref.refs_0_ = bf16[320,768]{1,0:T(8,128)(2,1)S(1)} collective-permute-done((bf16[320,768]{1,0:T(8,128)(2,1)S(1)}, bf16[320,768]{1,0:T(8,128)(2,1)S(1)}, u32[]{:S(2)}, u32[]{:S(2)}) %collective-permute-start.10) | collective-permute-done | bytes 491552 | tf_op jit(solution)/shard_map/ppermute | solution.py:284
  20.3 0.7 %collective-permute-start.11 = (bf16[160,768]{1,0:T(8,128)(2,1)S(1)}, bf16[160,768]{1,0:T(8,128)(2,1)S(1)}, u32[]{:S(2)}, u32[]{:S(2)}) collective-permute-start(bf16[160,768]{1,0:T(8,128)(2,1)S(1)} %get-tuple-element.1188), channel_id=1, source_target_pairs={{4,5},{5,4},{6,7},{7,6},{8,9},{9,8},{10,11},{11,10},{20,21},{21,20... | collective-permute-start | bytes 737288 | tf_op jit(solution)/shard_map/ppermute | solution.py:303
  21.0 0.7 %collective-permute-start.12 = (bf16[160,768]{1,0:T(8,128)(2,1)S(1)}, bf16[160,768]{1,0:T(8,128)(2,1)S(1)}, u32[]{:S(2)}, u32[]{:S(2)}) collective-permute-start(bf16[160,768]{1,0:T(8,128)(2,1)S(1)} %get-tuple-element.1189), channel_id=1, source_target_pairs={{4,5},{5,4},{6,7},{7,6},{8,9},{9,8},{10,11},{11,10},{20,21},{21,20... | collective-permute-start | bytes 737288 | tf_op jit(solution)/shard_map/ppermute | solution.py:303
  21.7 0.0 collective-permute-done.11.one_ref
  21.7 0.0 collective-permute-done.12.two_ref
  21.7 0.0 collective-permute-done.13.refs_1_
  21.7 9.1 %collective-permute-done.14.refs_2_ = bf16[320,768]{1,0:T(8,128)(2,1)S(1)} collective-permute-done((bf16[320,768]{1,0:T(8,128)(2,1)S(1)}, bf16[320,768]{1,0:T(8,128)(2,1)S(1)}, u32[]{:S(2)}, u32[]{:S(2)}) %collective-permute-start.14) | collective-permute-done | bytes 491552 | tf_op jit(solution)/shard_map/ppermute | solution.py:284
  30.9 0.0 collective-permute-done.15.refs_3_
  30.9 0.3 join.1
  31.2 0.8 %collective-permute-start.16 = (bf16[960,768]{1,0:T(8,128)(2,1)S(1)}, bf16[960,768]{1,0:T(8,128)(2,1)S(1)}, u32[]{:S(2)}, u32[]{:S(2)}) collective-permute-start(bf16[960,768]{1,0:T(8,128)(2,1)S(1)} %get-tuple-element.1192.late_ref), channel_id=1, source_target_pairs={{4,5},{5,4},{6,7},{7,6},{8,9},{9,8},{10,11},{11,10},{20,21},{21,20... | collective-permute-start | bytes 4423688 | tf_op jit(solution)/shard_map/ppermute | solution.py:329
  31.9 0.0 collective-permute-done.16.other_ref
  32.0 0.0 copy-start
  32.0 0.0 copy-start.2
  32.0 0.0 copy-start.3
  32.0 0.6 %other.1 = f32[128,128]{1,0:T(8,128)} custom-call(bf16[1600,768]{1,0:T(8,128)(2,1)S(1)} %get-tuple-element.1191.mine_ref, bf16[960,768]{1,0:T(8,128)(2,1)S(1)} %collective-permute-done.16.other_ref, f32[8,1280]{1,0:T(8,128)S(1)} %get-tuple-element.1194.best_ref, f32[8,1280]{1,0:T(8,128)S(1)} %get-tuple-element.1195.top_ref, ...), custom_call_target="tpu_custom_call" | custom-call | flops 2516582400 | bytes 1966080 | tf_op jit(solution)/shard_map/other/pallas_call | solution.py:340
  32.6 14.1 %all-to-all-start.4 = ((f32[16,8,128]{2,1,0:T(8,128)}), f32[16,8,128]{2,1,0:T(8,128)S(1)}, u32[]{:S(2)}, u32[]{:S(2)}) async-start(f32[16,8,128]{2,1,0:T(8,128)} %bitcast.12), calls=%async_computation.4 | async-start | bytes 131072 | tf_op jit(solution)/shard_map/all_to_all | solution.py:350
  46.8 6.9 %all-to-all-done.4 = f32[16,8,128]{2,1,0:T(8,128)S(1)} async-done(((f32[16,8,128]{2,1,0:T(8,128)}), f32[16,8,128]{2,1,0:T(8,128)S(1)}, u32[]{:S(2)}, u32[]{:S(2)}) %all-to-all-start.4) | async-done | bytes 65568 | tf_op jit(solution)/shard_map/all_to_all | solution.py:350
  53.7 0.7 %unpack.1 = (f32[1,512]{1,0:T(1,128)S(1)}, s32[1,1]{1,0:T(1,128)}) custom-call(f32[128,128]{1,0:T(8,128)S(1)} %bitcast.55, s32[8,512]{1,0:T(8,128)S(1)} %get-tuple-element.1185.slot_ref), custom_call_target="tpu_custom_call" | custom-call | tf_op jit(solution)/shard_map/unpack/pallas_call | solution.py:353
  55.0 0.0 copy-done
  55.0 0.0 copy-done.2
  55.0 0.0 copy-done.3
  55.0 0.2 conditional.1
  55.3 0.0 copy-start.4
  55.3 0.6 %copy-done.4 = f32[512]{0:T(512)} copy-done((f32[512]{0:T(512)}, f32[512]{0:T(512)S(1)}, u32[]{:S(2)}) %copy-start.4) | copy-done | bytes 2072
  (3 shorter events, 0.1 us)
Async XLA Ops:
  1.9 2.0 %collective-permute-start.9 = (bf16[320,768]{1,0:T(8,128)(2,1)S(1)}, bf16[320,768]{1,0:T(8,128)(2,1)S(1)}, u32[]{:S(2)}, u32[]{:S(2)}) collective-permute-start(bf16[320,768]{1,0:T(8,128)(2,1)S(1)} %get-tuple-element.1186), channel_id=1, source_target_pairs={{0,1},{1,0},{2,3},{3,2},{4,5},{5,4},{6,7},{7,6},{8,9},{9,8},{10,11... | collective-permute-start | bytes 1474568 | tf_op jit(solution)/shard_map/ppermute | solution.py:261
  4.0 16.3 %collective-permute-start.10 = (bf16[320,768]{1,0:T(8,128)(2,1)S(1)}, bf16[320,768]{1,0:T(8,128)(2,1)S(1)}, u32[]{:S(2)}, u32[]{:S(2)}) collective-permute-start(bf16[320,768]{1,0:T(8,128)(2,1)S(1)} %get-tuple-element.1187.mine_ref), channel_id=1, source_target_pairs={{0,4},{1,7},{2,6},{3,5},{12,8},{13,11},{14,10},{15,9},{16,20},{17,... | collective-permute-start | bytes 1474568 | tf_op jit(solution)/shard_map/ppermute | solution.py:284
  8.8 12.9 %collective-permute-start.13 = (bf16[320,768]{1,0:T(8,128)(2,1)S(1)}, bf16[320,768]{1,0:T(8,128)(2,1)S(1)}, u32[]{:S(2)}, u32[]{:S(2)}) collective-permute-start(bf16[320,768]{1,0:T(8,128)(2,1)S(1)} %get-tuple-element.1190), channel_id=1, source_target_pairs={{4,8},{5,11},{6,10},{7,9},{8,4},{9,7},{10,6},{11,5},{20,24},{21,27... | collective-permute-start | bytes 1474568 | tf_op jit(solution)/shard_map/ppermute | solution.py:284
  9.5 21.3 %collective-permute-start.14 = (bf16[320,768]{1,0:T(8,128)(2,1)S(1)}, bf16[320,768]{1,0:T(8,128)(2,1)S(1)}, u32[]{:S(2)}, u32[]{:S(2)}) collective-permute-start(bf16[320,768]{1,0:T(8,128)(2,1)S(1)} %get-tuple-element.1190), channel_id=1, source_target_pairs={{0,8},{1,11},{2,10},{3,9},{12,4},{13,7},{14,6},{15,5},{16,24},{17,... | collective-permute-start | bytes 1474568 | tf_op jit(solution)/shard_map/ppermute | solution.py:284
  13.5 17.3 %collective-permute-start.15 = (bf16[320,768]{1,0:T(8,128)(2,1)S(1)}, bf16[320,768]{1,0:T(8,128)(2,1)S(1)}, u32[]{:S(2)}, u32[]{:S(2)}) collective-permute-start(bf16[320,768]{1,0:T(8,128)(2,1)S(1)} %get-tuple-element.1187.mine_ref), channel_id=1, source_target_pairs={{5,7},{7,5},{9,11},{11,9},{21,23},{23,21},{25,27},{27,25}} | collective-permute-start | bytes 1474568 | tf_op jit(solution)/shard_map/ppermute | solution.py:284
  20.3 1.4 %collective-permute-start.11 = (bf16[160,768]{1,0:T(8,128)(2,1)S(1)}, bf16[160,768]{1,0:T(8,128)(2,1)S(1)}, u32[]{:S(2)}, u32[]{:S(2)}) collective-permute-start(bf16[160,768]{1,0:T(8,128)(2,1)S(1)} %get-tuple-element.1188), channel_id=1, source_target_pairs={{4,5},{5,4},{6,7},{7,6},{8,9},{9,8},{10,11},{11,10},{20,21},{21,20... | collective-permute-start | bytes 737288 | tf_op jit(solution)/shard_map/ppermute | solution.py:303
  21.0 0.7 %collective-permute-start.12 = (bf16[160,768]{1,0:T(8,128)(2,1)S(1)}, bf16[160,768]{1,0:T(8,128)(2,1)S(1)}, u32[]{:S(2)}, u32[]{:S(2)}) collective-permute-start(bf16[160,768]{1,0:T(8,128)(2,1)S(1)} %get-tuple-element.1189), channel_id=1, source_target_pairs={{4,5},{5,4},{6,7},{7,6},{8,9},{9,8},{10,11},{11,10},{20,21},{21,20... | collective-permute-start | bytes 737288 | tf_op jit(solution)/shard_map/ppermute | solution.py:303
  31.2 0.8 %collective-permute-start.16 = (bf16[960,768]{1,0:T(8,128)(2,1)S(1)}, bf16[960,768]{1,0:T(8,128)(2,1)S(1)}, u32[]{:S(2)}, u32[]{:S(2)}) collective-permute-start(bf16[960,768]{1,0:T(8,128)(2,1)S(1)} %get-tuple-element.1192.late_ref), channel_id=1, source_target_pairs={{4,5},{5,4},{6,7},{7,6},{8,9},{9,8},{10,11},{11,10},{20,21},{21,20... | collective-permute-start | bytes 4423688 | tf_op jit(solution)/shard_map/ppermute | solution.py:329
  32.0 23.1 %copy-start = (bf16[512,768]{1,0:T(8,128)(2,1)S(1)}, bf16[512,768]{1,0:T(8,128)(2,1)}, u32[]{:S(2)}) copy-start(bf16[512,768]{1,0:T(8,128)(2,1)} %x_ref.1) | copy-start | bytes 2359300
  32.0 23.0 %copy-start.2 = (s32[512]{0:T(512)S(1)}, s32[512]{0:T(512)}, u32[]{:S(2)}) copy-start(s32[512]{0:T(512)} %param.22) | copy-start | bytes 6148
  32.0 23.0 %copy-start.3 = (s32[512]{0:T(512)S(1)}, s32[512]{0:T(512)}, u32[]{:S(2)}) copy-start(s32[512]{0:T(512)} %param.23) | copy-start | bytes 6148
  32.6 21.0 %all-to-all-start.4 = ((f32[16,8,128]{2,1,0:T(8,128)}), f32[16,8,128]{2,1,0:T(8,128)S(1)}, u32[]{:S(2)}, u32[]{:S(2)}) async-start(f32[16,8,128]{2,1,0:T(8,128)} %bitcast.12), calls=%async_computation.4 | async-start | bytes 131072 | tf_op jit(solution)/shard_map/all_to_all | solution.py:350
  55.3 0.6 %copy-start.4 = (f32[512]{0:T(512)}, f32[512]{0:T(512)S(1)}, u32[]{:S(2)}) copy-start(f32[512]{0:T(512)S(1)} %get-tuple-element.2179) | copy-start | bytes 6148

commit v9 on v8

--- a/solution.py
+++ b/solution.py
@@ -12,7 +12,7 @@
 HOMES = (2, 3, 4, 5)
 HOME_ROUNDS = (0, 6)
 OUTER_ROUNDS = (2, 4)
-ORDER = (2, 6, 4, 0)
+ORDER = (2, 6, 0, 4)
 BLOCK = 160
 CAP = 156
 META = 16

time: 56.2 us -> 56.2 us (level)
  no operation moved by 1% of the time
where the time goes in v9:
time: 56.2 us; the launch traced here: 55.9 us
  starting transfers between devices  27 us (48%)
  waiting for transfers between devices  23.1 us (41%)
  Pallas kernels  4.12 us (7%)
  between operations  0.87 us (2%)
  local copies, waits for them, and re-layouts  0.59 us (1%)
    ppermute x4, waiting for transfers between devices, carry(): lax.ppermute(pair, 'owner', [(2 * s + c, 2 * (s ^ (k | c)) + c) for s in...  15.2 us
    all_to_all x1, starting transfers between devices, meet(): lax.all_to_all(found.reshape(OWNERS, 8, 128), 'owner', split_axis=0, conc...  14.2 us
    ppermute x4, starting transfers between devices, carry(): lax.ppermute(pair, 'owner', [(2 * s + c, 2 * (s ^ (k | c)) + c) for s in...  10.2 us
    all_to_all x1, waiting for transfers between devices, meet(): lax.all_to_all(found.reshape(OWNERS, 8, 128), 'owner', split_axis=0, conc...  6.9 us
    pallas_call x1, Pallas kernels, meet(): pl.pallas_call(pack_kernel, out_shape=[two_blocks, jax.ShapeDtypeStruct((...  1.88 us
    ppermute x2, starting transfers between devices, meet(): halves = [lax.ppermute(block, 'owner', swap) for block in halves]  1.35 us
  transfers between devices with their start and end apart: 9, of which 4 were waited for; matrix products, arithmetic and copies ran while one was open for 0% of the time, Pallas kernels for 1%

profile of v9, /device:TPU:0, one launch (start us, length us, event | category | flops | bytes accessed | tf_op | source)
XLA Modules:
  0.0 55.9 jit_solution(1682187269514111919)
XLA Ops:
  0.0 1.9 %pack.1 = (bf16[320,768]{1,0:T(8,128)(2,1)S(1)}, s32[8,512]{1,0:T(8,128)S(1)}, bf16[512,768]{1,0:T(8,128)(2,1)S(1)}, bf16[16,512]{1,0:T(8,128)(2,1)S(1)}) custom-call(bf16[512,768]{1,0:T(8,128)(2,1)} %x_ref.1, s32[1,512]{1,0:T(1,128)} %bitcast.58, s32[1,512]{1,0:T(1,128)} %bitcast.59), custom_call_target="tpu_custom_call" | custom-call | tf_op jit(solution)/shard_map/pack/pallas_call | solution.py:248
  1.9 0.5 collective-permute-start.9
  2.4 0.5 keep.1.keep_ref
  2.9 1.0 %collective-permute-done.9.got_ref = bf16[320,768]{1,0:T(8,128)(2,1)S(1)} collective-permute-done((bf16[320,768]{1,0:T(8,128)(2,1)S(1)}, bf16[320,768]{1,0:T(8,128)(2,1)S(1)}, u32[]{:S(2)}, u32[]{:S(2)}) %collective-permute-start.9) | collective-permute-done | bytes 491552 | tf_op jit(solution)/shard_map/ppermute | solution.py:261
  3.9 0.1 pair.1
  4.0 4.9 %collective-permute-start.10 = (bf16[320,768]{1,0:T(8,128)(2,1)S(1)}, bf16[320,768]{1,0:T(8,128)(2,1)S(1)}, u32[]{:S(2)}, u32[]{:S(2)}) collective-permute-start(bf16[320,768]{1,0:T(8,128)(2,1)S(1)} %get-tuple-element.1187.mine_ref), channel_id=1, source_target_pairs={{0,4},{1,7},{2,6},{3,5},{12,8},{13,11},{14,10},{15,9},{16,20},{17,... | collective-permute-start | bytes 1474568 | tf_op jit(solution)/shard_map/ppermute | solution.py:284
  8.8 0.7 %collective-permute-start.13 = (bf16[320,768]{1,0:T(8,128)(2,1)S(1)}, bf16[320,768]{1,0:T(8,128)(2,1)S(1)}, u32[]{:S(2)}, u32[]{:S(2)}) collective-permute-start(bf16[320,768]{1,0:T(8,128)(2,1)S(1)} %get-tuple-element.1190), channel_id=1, source_target_pairs={{4,8},{5,11},{6,10},{7,9},{8,4},{9,7},{10,6},{11,5},{20,24},{21,27... | collective-permute-start | bytes 1474568 | tf_op jit(solution)/shard_map/ppermute | solution.py:284
  9.5 0.7 %collective-permute-start.14 = (bf16[320,768]{1,0:T(8,128)(2,1)S(1)}, bf16[320,768]{1,0:T(8,128)(2,1)S(1)}, u32[]{:S(2)}, u32[]{:S(2)}) collective-permute-start(bf16[320,768]{1,0:T(8,128)(2,1)S(1)} %get-tuple-element.1187.mine_ref), channel_id=1, source_target_pairs={{5,7},{7,5},{9,11},{11,9},{21,23},{23,21},{25,27},{27,25}} | collective-permute-start | bytes 1474568 | tf_op jit(solution)/shard_map/ppermute | solution.py:284
  10.2 4.0 %collective-permute-start.15 = (bf16[320,768]{1,0:T(8,128)(2,1)S(1)}, bf16[320,768]{1,0:T(8,128)(2,1)S(1)}, u32[]{:S(2)}, u32[]{:S(2)}) collective-permute-start(bf16[320,768]{1,0:T(8,128)(2,1)S(1)} %get-tuple-element.1190), channel_id=1, source_target_pairs={{0,8},{1,11},{2,10},{3,9},{12,4},{13,7},{14,6},{15,5},{16,24},{17,... | collective-permute-start | bytes 1474568 | tf_op jit(solution)/shard_map/ppermute | solution.py:284
  14.2 6.1 %collective-permute-done.10.pair_ref.refs_0_ = bf16[320,768]{1,0:T(8,128)(2,1)S(1)} collective-permute-done((bf16[320,768]{1,0:T(8,128)(2,1)S(1)}, bf16[320,768]{1,0:T(8,128)(2,1)S(1)}, u32[]{:S(2)}, u32[]{:S(2)}) %collective-permute-start.10) | collective-permute-done | bytes 491552 | tf_op jit(solution)/shard_map/ppermute | solution.py:284
  20.3 0.7 %collective-permute-start.11 = (bf16[160,768]{1,0:T(8,128)(2,1)S(1)}, bf16[160,768]{1,0:T(8,128)(2,1)S(1)}, u32[]{:S(2)}, u32[]{:S(2)}) collective-permute-start(bf16[160,768]{1,0:T(8,128)(2,1)S(1)} %get-tuple-element.1188), channel_id=1, source_target_pairs={{4,5},{5,4},{6,7},{7,6},{8,9},{9,8},{10,11},{11,10},{20,21},{21,20... | collective-permute-start | bytes 737288 | tf_op jit(solution)/shard_map/ppermute | solution.py:303
  21.0 0.7 %collective-permute-start.12 = (bf16[160,768]{1,0:T(8,128)(2,1)S(1)}, bf16[160,768]{1,0:T(8,128)(2,1)S(1)}, u32[]{:S(2)}, u32[]{:S(2)}) collective-permute-start(bf16[160,768]{1,0:T(8,128)(2,1)S(1)} %get-tuple-element.1189), channel_id=1, source_target_pairs={{4,5},{5,4},{6,7},{7,6},{8,9},{9,8},{10,11},{11,10},{20,21},{21,20... | collective-permute-start | bytes 737288 | tf_op jit(solution)/shard_map/ppermute | solution.py:303
  21.7 0.0 collective-permute-done.11.one_ref
  21.7 0.0 collective-permute-done.12.two_ref
  21.7 0.0 collective-permute-done.13.refs_1_
  21.7 0.0 collective-permute-done.14.refs_2_
  21.8 9.1 %collective-permute-done.15.refs_3_ = bf16[320,768]{1,0:T(8,128)(2,1)S(1)} collective-permute-done((bf16[320,768]{1,0:T(8,128)(2,1)S(1)}, bf16[320,768]{1,0:T(8,128)(2,1)S(1)}, u32[]{:S(2)}, u32[]{:S(2)}) %collective-permute-start.15) | collective-permute-done | bytes 491552 | tf_op jit(solution)/shard_map/ppermute | solution.py:284
  30.9 0.3 join.1
  31.2 0.8 %collective-permute-start.16 = (bf16[960,768]{1,0:T(8,128)(2,1)S(1)}, bf16[960,768]{1,0:T(8,128)(2,1)S(1)}, u32[]{:S(2)}, u32[]{:S(2)}) collective-permute-start(bf16[960,768]{1,0:T(8,128)(2,1)S(1)} %get-tuple-element.1192.late_ref), channel_id=1, source_target_pairs={{4,5},{5,4},{6,7},{7,6},{8,9},{9,8},{10,11},{11,10},{20,21},{21,20... | collective-permute-start | bytes 4423688 | tf_op jit(solution)/shard_map/ppermute | solution.py:329
  31.9 0.0 collective-permute-done.16.other_ref
  32.0 0.0 copy-start
  32.0 0.0 copy-start.2
  32.0 0.0 copy-start.3
  32.0 0.6 %other.1 = f32[128,128]{1,0:T(8,128)} custom-call(bf16[1600,768]{1,0:T(8,128)(2,1)S(1)} %get-tuple-element.1191.mine_ref, bf16[960,768]{1,0:T(8,128)(2,1)S(1)} %collective-permute-done.16.other_ref, f32[8,1280]{1,0:T(8,128)S(1)} %get-tuple-element.1194.best_ref, f32[8,1280]{1,0:T(8,128)S(1)} %get-tuple-element.1195.top_ref, ...), custom_call_target="tpu_custom_call" | custom-call | flops 2516582400 | bytes 1966080 | tf_op jit(solution)/shard_map/other/pallas_call | solution.py:340
  32.6 14.2 %all-to-all-start.4 = ((f32[16,8,128]{2,1,0:T(8,128)}), f32[16,8,128]{2,1,0:T(8,128)S(1)}, u32[]{:S(2)}, u32[]{:S(2)}) async-start(f32[16,8,128]{2,1,0:T(8,128)} %bitcast.12), calls=%async_computation.4 | async-start | bytes 131072 | tf_op jit(solution)/shard_map/all_to_all | solution.py:350
  46.8 6.9 %all-to-all-done.4 = f32[16,8,128]{2,1,0:T(8,128)S(1)} async-done(((f32[16,8,128]{2,1,0:T(8,128)}), f32[16,8,128]{2,1,0:T(8,128)S(1)}, u32[]{:S(2)}, u32[]{:S(2)}) %all-to-all-start.4) | async-done | bytes 65568 | tf_op jit(solution)/shard_map/all_to_all | solution.py:350
  53.7 0.7 %unpack.1 = (f32[1,512]{1,0:T(1,128)S(1)}, s32[1,1]{1,0:T(1,128)}) custom-call(f32[128,128]{1,0:T(8,128)S(1)} %bitcast.55, s32[8,512]{1,0:T(8,128)S(1)} %get-tuple-element.1185.slot_ref), custom_call_target="tpu_custom_call" | custom-call | tf_op jit(solution)/shard_map/unpack/pallas_call | solution.py:353
  55.0 0.0 copy-done
  55.0 0.0 copy-done.2
  55.0 0.0 copy-done.3
  55.0 0.2 conditional.1
  55.3 0.0 copy-start.4
  55.3 0.6 %copy-done.4 = f32[512]{0:T(512)} copy-done((f32[512]{0:T(512)}, f32[512]{0:T(512)S(1)}, u32[]{:S(2)}) %copy-start.4) | copy-done | bytes 2072
  (3 shorter events, 0.1 us)
Async XLA Ops:
  1.9 2.0 %collective-permute-start.9 = (bf16[320,768]{1,0:T(8,128)(2,1)S(1)}, bf16[320,768]{1,0:T(8,128)(2,1)S(1)}, u32[]{:S(2)}, u32[]{:S(2)}) collective-permute-start(bf16[320,768]{1,0:T(8,128)(2,1)S(1)} %get-tuple-element.1186), channel_id=1, source_target_pairs={{0,1},{1,0},{2,3},{3,2},{4,5},{5,4},{6,7},{7,6},{8,9},{9,8},{10,11... | collective-permute-start | bytes 1474568 | tf_op jit(solution)/shard_map/ppermute | solution.py:261
  4.0 16.3 %collective-permute-start.10 = (bf16[320,768]{1,0:T(8,128)(2,1)S(1)}, bf16[320,768]{1,0:T(8,128)(2,1)S(1)}, u32[]{:S(2)}, u32[]{:S(2)}) collective-permute-start(bf16[320,768]{1,0:T(8,128)(2,1)S(1)} %get-tuple-element.1187.mine_ref), channel_id=1, source_target_pairs={{0,4},{1,7},{2,6},{3,5},{12,8},{13,11},{14,10},{15,9},{16,20},{17,... | collective-permute-start | bytes 1474568 | tf_op jit(solution)/shard_map/ppermute | solution.py:284
  8.8 12.9 %collective-permute-start.13 = (bf16[320,768]{1,0:T(8,128)(2,1)S(1)}, bf16[320,768]{1,0:T(8,128)(2,1)S(1)}, u32[]{:S(2)}, u32[]{:S(2)}) collective-permute-start(bf16[320,768]{1,0:T(8,128)(2,1)S(1)} %get-tuple-element.1190), channel_id=1, source_target_pairs={{4,8},{5,11},{6,10},{7,9},{8,4},{9,7},{10,6},{11,5},{20,24},{21,27... | collective-permute-start | bytes 1474568 | tf_op jit(solution)/shard_map/ppermute | solution.py:284
  9.5 12.2 %collective-permute-start.14 = (bf16[320,768]{1,0:T(8,128)(2,1)S(1)}, bf16[320,768]{1,0:T(8,128)(2,1)S(1)}, u32[]{:S(2)}, u32[]{:S(2)}) collective-permute-start(bf16[320,768]{1,0:T(8,128)(2,1)S(1)} %get-tuple-element.1187.mine_ref), channel_id=1, source_target_pairs={{5,7},{7,5},{9,11},{11,9},{21,23},{23,21},{25,27},{27,25}} | collective-permute-start | bytes 1474568 | tf_op jit(solution)/shard_map/ppermute | solution.py:284
  10.2 20.6 %collective-permute-start.15 = (bf16[320,768]{1,0:T(8,128)(2,1)S(1)}, bf16[320,768]{1,0:T(8,128)(2,1)S(1)}, u32[]{:S(2)}, u32[]{:S(2)}) collective-permute-start(bf16[320,768]{1,0:T(8,128)(2,1)S(1)} %get-tuple-element.1190), channel_id=1, source_target_pairs={{0,8},{1,11},{2,10},{3,9},{12,4},{13,7},{14,6},{15,5},{16,24},{17,... | collective-permute-start | bytes 1474568 | tf_op jit(solution)/shard_map/ppermute | solution.py:284
  20.3 1.4 %collective-permute-start.11 = (bf16[160,768]{1,0:T(8,128)(2,1)S(1)}, bf16[160,768]{1,0:T(8,128)(2,1)S(1)}, u32[]{:S(2)}, u32[]{:S(2)}) collective-permute-start(bf16[160,768]{1,0:T(8,128)(2,1)S(1)} %get-tuple-element.1188), channel_id=1, source_target_pairs={{4,5},{5,4},{6,7},{7,6},{8,9},{9,8},{10,11},{11,10},{20,21},{21,20... | collective-permute-start | bytes 737288 | tf_op jit(solution)/shard_map/ppermute | solution.py:303
  21.0 0.7 %collective-permute-start.12 = (bf16[160,768]{1,0:T(8,128)(2,1)S(1)}, bf16[160,768]{1,0:T(8,128)(2,1)S(1)}, u32[]{:S(2)}, u32[]{:S(2)}) collective-permute-start(bf16[160,768]{1,0:T(8,128)(2,1)S(1)} %get-tuple-element.1189), channel_id=1, source_target_pairs={{4,5},{5,4},{6,7},{7,6},{8,9},{9,8},{10,11},{11,10},{20,21},{21,20... | collective-permute-start | bytes 737288 | tf_op jit(solution)/shard_map/ppermute | solution.py:303
  31.2 0.8 %collective-permute-start.16 = (bf16[960,768]{1,0:T(8,128)(2,1)S(1)}, bf16[960,768]{1,0:T(8,128)(2,1)S(1)}, u32[]{:S(2)}, u32[]{:S(2)}) collective-permute-start(bf16[960,768]{1,0:T(8,128)(2,1)S(1)} %get-tuple-element.1192.late_ref), channel_id=1, source_target_pairs={{4,5},{5,4},{6,7},{7,6},{8,9},{9,8},{10,11},{11,10},{20,21},{21,20... | collective-permute-start | bytes 4423688 | tf_op jit(solution)/shard_map/ppermute | solution.py:329
  32.0 23.1 %copy-start = (bf16[512,768]{1,0:T(8,128)(2,1)S(1)}, bf16[512,768]{1,0:T(8,128)(2,1)}, u32[]{:S(2)}) copy-start(bf16[512,768]{1,0:T(8,128)(2,1)} %x_ref.1) | copy-start | bytes 2359300
  32.0 23.1 %copy-start.2 = (s32[512]{0:T(512)S(1)}, s32[512]{0:T(512)}, u32[]{:S(2)}) copy-start(s32[512]{0:T(512)} %param.22) | copy-start | bytes 6148
  32.0 23.1 %copy-start.3 = (s32[512]{0:T(512)S(1)}, s32[512]{0:T(512)}, u32[]{:S(2)}) copy-start(s32[512]{0:T(512)} %param.23) | copy-start | bytes 6148
  32.6 21.1 %all-to-all-start.4 = ((f32[16,8,128]{2,1,0:T(8,128)}), f32[16,8,128]{2,1,0:T(8,128)S(1)}, u32[]{:S(2)}, u32[]{:S(2)}) async-start(f32[16,8,128]{2,1,0:T(8,128)} %bitcast.12), calls=%async_computation.4 | async-start | bytes 131072 | tf_op jit(solution)/shard_map/all_to_all | solution.py:350
  55.3 0.6 %copy-start.4 = (f32[512]{0:T(512)}, f32[512]{0:T(512)S(1)}, u32[]{:S(2)}) copy-start(f32[512]{0:T(512)S(1)} %get-tuple-element.2179) | copy-start | bytes 6148
